TPU v7x, 32 devices: a whole 2x2x4 slice. The times are simulated.
32 devices in a mesh: seq: 8 (over y, x, core), fsdp: 4 (over z).
Axes of the slice: x: 2, y: 2, z: 4, core: 2. Of those that a mesh axis runs over, the one named last changes fastest.
Arguments:
- tokens: bfloat16 [4, 1536, 2048], P('fsdp', 'seq'), may hold values from -41 to 41
- cotangent: bfloat16 [4, 1536, 2048], P('fsdp', 'seq'), may hold values from -6 to 6
- attn_gain: bfloat16 [2048], P(('seq', 'fsdp')), may hold values from 0.099609375 to 1.8984375
- mlp_gain: bfloat16 [2048], P(('seq', 'fsdp')), may hold values from 0.099609375 to 1.8984375
- w_q: bfloat16 [2048, 2048], P(('seq', 'fsdp')), may hold values from -0.1875 to 0.1875
- w_k: bfloat16 [2048, 2048], P(('seq', 'fsdp')), may hold values from -0.1875 to 0.1875
- w_v: bfloat16 [2048, 2048], P(('seq', 'fsdp')), may hold values from -0.125 to 0.125
- w_o: bfloat16 [2048, 2048], P(('seq', 'fsdp')), may hold values from -0.5 to 0.5
- w_gate: bfloat16 [2048, 8192], P(('seq', 'fsdp')), may hold values from -0.125 to 0.125
- w_up: bfloat16 [2048, 8192], P(('seq', 'fsdp')), may hold values from -0.125 to 0.125
- w_down: bfloat16 [8192, 2048], P(('seq', 'fsdp')), may hold values from -0.0625 to 0.0625
Outputs:
- layer_out: bfloat16 [4, 1536, 2048], P('fsdp', 'seq')
- input_grad: bfloat16 [4, 1536, 2048], P('fsdp', 'seq')
- attn_gain_grad: float32 [2048], P(('seq', 'fsdp'))
- mlp_gain_grad: float32 [2048], P(('seq', 'fsdp'))
- w_q_grad: float32 [2048, 2048], P(('seq', 'fsdp'))
- w_k_grad: float32 [2048, 2048], P(('seq', 'fsdp'))
- w_v_grad: float32 [2048, 2048], P(('seq', 'fsdp'))
- w_o_grad: float32 [2048, 2048], P(('seq', 'fsdp'))
- w_gate_grad: float32 [2048, 8192], P(('seq', 'fsdp'))
- w_up_grad: float32 [2048, 8192], P(('seq', 'fsdp'))
- w_down_grad: float32 [8192, 2048], P(('seq', 'fsdp'))
All inputs are finite; a program needn't handle non-finite values.
Results may differ from a plain program's by a relative error of at most 0.017.
Values may be sent and summed in bfloat16 or wider, within the bound.
No kernel may reach another device: no remote copies, remote signals or barrier semaphores. Data moves between devices by JAX's collectives and lax.ppermute only.
A program may use at most 576 MiB of HBM per device.

v0:
```python
import jax
import jax.numpy as jnp
from jax import lax
from jax.sharding import PartitionSpec as P

HEADS = 32
HD = 64


EPS = 1e-05
THETA = 130000.0


def rms_scale(values):
    return lax.rsqrt(jnp.mean(values * values, axis=-1, keepdims=True) + EPS)


def rotary_tables(positions):
    halfway = HD // 2
    frequency = THETA ** (-(jnp.arange(halfway, dtype=jnp.float32) * 2.0) / HD)
    angles = positions.astype(jnp.float32)[:, None] * frequency[None, :]
    cosine = jnp.cos(angles)
    sine = jnp.sin(angles)
    return (
        jnp.concatenate([cosine, cosine], -1)[:, None, :],
        jnp.concatenate([sine, sine], -1)[:, None, :],
    )


def rotate(values):
    halfway = values.shape[-1] // 2
    return jnp.concatenate([-values[..., halfway:], values[..., :halfway]], -1)


def rotary(values, cosine, sine):
    return values * cosine + rotate(values) * sine


def rotary_back(values, cosine, sine):
    return values * cosine - rotate(values * sine)


def masked_scores(query_block, key_heads, start, block, length):
    scores = jnp.einsum(
        "qhd,khd->hqk", query_block, key_heads, preferred_element_type=jnp.float32
    ) * HD ** (-0.5)
    key_places = jnp.arange(length, dtype=jnp.int32)
    allowed = key_places[None, :] <= (start + jnp.arange(block, dtype=jnp.int32))[:, None]
    return jnp.where(allowed[None], scores, -1e30)


def attend_forward(queries, keys_all, values):
    length = queries.shape[0]
    heads = queries.shape[1] // HD
    block = min(512, length)
    count = length // block
    query_blocks = queries.reshape(count, block, heads, HD)
    key_heads = keys_all.reshape(length, heads, HD)
    value_heads = values.reshape(length, heads, HD)

    def one_block(pair):
        query_block, start = pair
        scores = masked_scores(query_block, key_heads, start, block, length)
        highest = jnp.max(scores, axis=-1, keepdims=True)
        weights = jnp.exp(scores - highest)
        totals = jnp.sum(weights, axis=-1, keepdims=True)
        probs = (weights / totals).astype(jnp.bfloat16)
        output = jnp.einsum("hqk,khd->qhd", probs, value_heads, preferred_element_type=jnp.float32)
        return (output.astype(jnp.bfloat16), (highest + jnp.log(totals))[..., 0])

    starts = jnp.arange(count, dtype=jnp.int32) * block
    outputs, log_totals = lax.map(one_block, (query_blocks, starts))
    return (outputs.reshape(length, heads * HD), log_totals)


def attend_backward(queries, keys_all, values, grad_heads, log_totals):
    length = queries.shape[0]
    heads = queries.shape[1] // HD
    block = min(512, length)
    count = length // block
    scale = HD ** (-0.5)
    query_blocks = queries.reshape(count, block, heads, HD)
    grad_blocks = grad_heads.reshape(count, block, heads, HD)
    key_heads = keys_all.reshape(length, heads, HD)
    value_heads = values.reshape(length, heads, HD)

    def one_block(carry, inputs):
        key_sum, value_sum = carry
        query_block, grad_block, log_block, start = inputs
        scores = masked_scores(query_block, key_heads, start, block, length)
        probs = jnp.exp(scores - log_block[..., None])
        grad_probs = jnp.einsum(
            "qhd,khd->hqk", grad_block, value_heads, preferred_element_type=jnp.float32
        )
        inner = jnp.sum(probs * grad_probs, axis=-1, keepdims=True)
        grad_scores = (probs * (grad_probs - inner)).astype(jnp.bfloat16)
        grad_query = (
            jnp.einsum("hqk,khd->qhd", grad_scores, key_heads, preferred_element_type=jnp.float32)
            * scale
        )
        key_sum = (
            key_sum
            + jnp.einsum(
                "hqk,qhd->khd", grad_scores, query_block, preferred_element_type=jnp.float32
            )
            * scale
        )
        value_sum = value_sum + jnp.einsum(
            "hqk,qhd->khd",
            probs.astype(jnp.bfloat16),
            grad_block,
            preferred_element_type=jnp.float32,
        )
        return ((key_sum, value_sum), grad_query.astype(jnp.bfloat16))

    empty = jnp.zeros((length, heads, HD), jnp.float32)
    starts = jnp.arange(count, dtype=jnp.int32) * block
    (key_sum, value_sum), grad_queries = lax.scan(
        one_block, (empty, empty), (query_blocks, grad_blocks, log_totals, starts)
    )
    return (
        grad_queries.reshape(length, heads * HD),
        key_sum.astype(jnp.bfloat16).reshape(length, heads * HD),
        value_sum.astype(jnp.bfloat16).reshape(length, heads * HD),
    )


def per_device(tokens, cotangent, attn_gain, mlp_gain, w_q, w_k, w_v, w_o, w_gate, w_up, w_down):
    rows = tokens.shape[1]
    width = tokens.shape[2]
    inputs = tokens[0].astype(jnp.float32)
    grad_out = cotangent[0]
    places = lax.axis_index("seq") * rows + jnp.arange(rows, dtype=jnp.int32)
    cosine, sine = rotary_tables(places)
    heads_shape = (rows, HEADS, HD)
    scale_one = rms_scale(inputs)
    normal_one = inputs * scale_one
    gain = lax.all_gather(attn_gain, ("seq", "fsdp"), axis=0, tiled=True)
    query_rows = lax.all_gather(w_q, ("seq", "fsdp"), axis=0, tiled=True)
    key_rows = lax.all_gather(w_k, ("seq", "fsdp"), axis=0, tiled=True)
    value_rows = lax.all_gather(w_v, ("seq", "fsdp"), axis=0, tiled=True)
    piece = (normal_one * gain.astype(jnp.float32)).astype(jnp.bfloat16)
    query_sum = jnp.dot(piece, query_rows, preferred_element_type=jnp.float32)
    key_sum = jnp.dot(piece, key_rows, preferred_element_type=jnp.float32)
    value_sum = jnp.dot(piece, value_rows, preferred_element_type=jnp.float32)
    normed_one = piece
    query_rot = (
        rotary(query_sum.reshape(heads_shape), cosine, sine)
        .astype(jnp.bfloat16)
        .reshape(rows, width)
    )
    key_rot = (
        rotary(key_sum.reshape(heads_shape), cosine, sine).astype(jnp.bfloat16).reshape(rows, width)
    )
    value_low = value_sum.astype(jnp.bfloat16)
    query_heads, key_heads, value_heads = (
        lax.all_to_all(query_rot, "seq", split_axis=1, concat_axis=0, tiled=True),
        lax.all_to_all(key_rot, "seq", split_axis=1, concat_axis=0, tiled=True),
        lax.all_to_all(value_low, "seq", split_axis=1, concat_axis=0, tiled=True),
    )
    attended_heads, log_totals = attend_forward(query_heads, key_heads, value_heads)
    attended = lax.all_to_all(attended_heads, "seq", split_axis=0, concat_axis=1, tiled=True)
    projected = jnp.dot(
        attended,
        lax.all_gather(w_o, ("seq", "fsdp"), axis=0, tiled=True),
        preferred_element_type=jnp.float32,
    )
    middle = inputs + projected
    scale_two = rms_scale(middle)
    normal_two = middle * scale_two
    gain = lax.all_gather(mlp_gain, ("seq", "fsdp"), axis=0, tiled=True)
    gate_rows = lax.all_gather(w_gate, ("seq", "fsdp"), axis=0, tiled=True)
    up_rows = lax.all_gather(w_up, ("seq", "fsdp"), axis=0, tiled=True)
    piece = (normal_two * gain.astype(jnp.float32)).astype(jnp.bfloat16)
    gate_sum = jnp.dot(piece, gate_rows, preferred_element_type=jnp.float32)
    up_sum = jnp.dot(piece, up_rows, preferred_element_type=jnp.float32)
    sigmoid_gate = jax.nn.sigmoid(gate_sum)
    silu_gate = jax.nn.silu(gate_sum)
    mixed = (silu_gate * up_sum).astype(jnp.bfloat16)
    down_sum = jnp.dot(
        mixed,
        lax.all_gather(w_down, ("seq", "fsdp"), axis=0, tiled=True),
        preferred_element_type=jnp.float32,
    )
    layer_out = (middle + down_sum).astype(jnp.bfloat16)[None]
    grad_mixed = jnp.einsum(
        "td,fd->tf",
        grad_out,
        lax.all_gather(w_down, ("seq", "fsdp"), axis=0, tiled=True),
        preferred_element_type=jnp.float32,
    )
    grad_gate = (
        grad_mixed * up_sum * sigmoid_gate * (1.0 + gate_sum * (1.0 - sigmoid_gate))
    ).astype(jnp.bfloat16)
    grad_up = (grad_mixed * silu_gate).astype(jnp.bfloat16)
    gain = lax.all_gather(mlp_gain, ("seq", "fsdp"), axis=0, tiled=True)
    gate_rows = lax.all_gather(w_gate, ("seq", "fsdp"), axis=0, tiled=True)
    up_rows = lax.all_gather(w_up, ("seq", "fsdp"), axis=0, tiled=True)
    grad_normed = jnp.einsum(
        "tf,df->td", grad_gate, gate_rows, preferred_element_type=jnp.float32
    ) + jnp.einsum("tf,df->td", grad_up, up_rows, preferred_element_type=jnp.float32)
    gain_piece = jnp.sum(grad_normed * normal_two, axis=0)
    grad_two = grad_normed * gain.astype(jnp.float32)
    gain_two = gain_piece
    grad_down_full = jnp.einsum("tf,td->fd", mixed, grad_out, preferred_element_type=jnp.float32)
    grad_gate_full = jnp.einsum("td,tf->df", piece, grad_gate, preferred_element_type=jnp.float32)
    grad_up_full = jnp.einsum("td,tf->df", piece, grad_up, preferred_element_type=jnp.float32)
    grad_gate_w, grad_up_w, grad_down_w = (
        lax.psum_scatter(grad_gate_full, ("seq", "fsdp"), scatter_dimension=0, tiled=True),
        lax.psum_scatter(grad_up_full, ("seq", "fsdp"), scatter_dimension=0, tiled=True),
        lax.psum_scatter(grad_down_full, ("seq", "fsdp"), scatter_dimension=0, tiled=True),
    )
    grad_middle = grad_out.astype(jnp.float32) + scale_two * (
        grad_two - normal_two * jnp.mean(grad_two * normal_two, axis=-1, keepdims=True)
    )
    grad_proj = grad_middle.astype(jnp.bfloat16)
    grad_out_w = jnp.einsum("ti,to->io", attended, grad_proj, preferred_element_type=jnp.float32)
    grad_attended = jnp.einsum(
        "to,io->ti",
        grad_proj,
        lax.all_gather(w_o, ("seq", "fsdp"), axis=0, tiled=True),
        preferred_element_type=jnp.float32,
    ).astype(jnp.bfloat16)
    grad_heads = lax.all_to_all(grad_attended, "seq", split_axis=1, concat_axis=0, tiled=True)
    grad_query_heads, grad_key_heads, grad_value_heads = attend_backward(
        query_heads, key_heads, value_heads, grad_heads, log_totals
    )
    grad_query_rot, grad_key_rot, grad_values = (
        lax.all_to_all(grad_query_heads, "seq", split_axis=0, concat_axis=1, tiled=True),
        lax.all_to_all(grad_key_heads, "seq", split_axis=0, concat_axis=1, tiled=True),
        lax.all_to_all(grad_value_heads, "seq", split_axis=0, concat_axis=1, tiled=True),
    )
    grad_queries = (
        rotary_back(grad_query_rot.astype(jnp.float32).reshape(heads_shape), cosine, sine)
        .astype(jnp.bfloat16)
        .reshape(rows, width)
    )
    grad_keys = (
        rotary_back(grad_key_rot.astype(jnp.float32).reshape(heads_shape), cosine, sine)
        .astype(jnp.bfloat16)
        .reshape(rows, width)
    )
    grad_query_w = jnp.einsum(
        "ti,to->io", normed_one, grad_queries, preferred_element_type=jnp.float32
    )
    grad_key_w = jnp.einsum("ti,to->io", normed_one, grad_keys, preferred_element_type=jnp.float32)
    grad_value_w = jnp.einsum(
        "ti,to->io", normed_one, grad_values, preferred_element_type=jnp.float32
    )
    gain = lax.all_gather(attn_gain, ("seq", "fsdp"), axis=0, tiled=True)
    query_rows = lax.all_gather(w_q, ("seq", "fsdp"), axis=0, tiled=True)
    key_rows = lax.all_gather(w_k, ("seq", "fsdp"), axis=0, tiled=True)
    value_rows = lax.all_gather(w_v, ("seq", "fsdp"), axis=0, tiled=True)
    grad_normed = (
        jnp.einsum("to,io->ti", grad_queries, query_rows, preferred_element_type=jnp.float32)
        + jnp.einsum("to,io->ti", grad_keys, key_rows, preferred_element_type=jnp.float32)
        + jnp.einsum("to,io->ti", grad_values, value_rows, preferred_element_type=jnp.float32)
    )
    gain_piece = jnp.sum(grad_normed * normal_one, axis=0)
    grad_one = grad_normed * gain.astype(jnp.float32)
    grad_inputs = grad_middle + scale_one * (
        grad_one - normal_one * jnp.mean(grad_one * normal_one, axis=-1, keepdims=True)
    )
    attn_grads = (
        lax.psum_scatter(gain_piece, ("seq", "fsdp"), scatter_dimension=0, tiled=True),
        lax.psum_scatter(gain_two, ("seq", "fsdp"), scatter_dimension=0, tiled=True),
        lax.psum_scatter(grad_query_w, ("seq", "fsdp"), scatter_dimension=0, tiled=True),
        lax.psum_scatter(grad_key_w, ("seq", "fsdp"), scatter_dimension=0, tiled=True),
        lax.psum_scatter(grad_value_w, ("seq", "fsdp"), scatter_dimension=0, tiled=True),
        lax.psum_scatter(grad_out_w, ("seq", "fsdp"), scatter_dimension=0, tiled=True),
    )
    return (
        layer_out,
        grad_inputs.astype(jnp.bfloat16)[None],
        attn_grads[0],
        attn_grads[1],
        attn_grads[2],
        attn_grads[3],
        attn_grads[4],
        attn_grads[5],
        grad_gate_w,
        grad_up_w,
        grad_down_w,
    )


def solution(mesh):
    placed = (
        P("fsdp", "seq", None),
        P("fsdp", "seq", None),
        P(("seq", "fsdp")),
        P(("seq", "fsdp")),
        P(("seq", "fsdp"), None),
        P(("seq", "fsdp"), None),
        P(("seq", "fsdp"), None),
        P(("seq", "fsdp"), None),
        P(("seq", "fsdp"), None),
        P(("seq", "fsdp"), None),
        P(("seq", "fsdp"), None),
    )
    return jax.shard_map(
        per_device,
        mesh=mesh,
        in_specs=placed,
        out_specs=(
            P("fsdp", "seq", None),
            P("fsdp", "seq", None),
            P(("seq", "fsdp")),
            P(("seq", "fsdp")),
            P(("seq", "fsdp"), None),
            P(("seq", "fsdp"), None),
            P(("seq", "fsdp"), None),
            P(("seq", "fsdp"), None),
            P(("seq", "fsdp"), None),
            P(("seq", "fsdp"), None),
            P(("seq", "fsdp"), None),
        ),
        check_vma=False,
    )
```

profile of v0, /device:TPU:0, one launch (start us, length us, event | category | flops | bytes accessed | tf_op | source)
XLA Modules:
  0.0 6706.3 jit_solution(17779259133178520421)
XLA Ops:
  12.4 42.6 all-reduce.5
  55.6 35.9 all-gather.10.cloned.1.call-done
  103.9 66.6 all-gather.8.cloned.1.call-done
  220.8 39.7 all-gather.12.cloned.1.call-done
  290.0 41.8 while.27
  364.8 174.1 %all-gather.16.cloned.1.call-done = bf16[2048,8192]{1,0:T(8,128)(2,1)} async-done(((bf16[64,8192]{1,0:T(8,128)(2,1)}), bf16[2048,8192]{1,0:T(8,128)(2,1)}) %all-gather.16.cloned.1.call-update) | async-done | bytes 33554448 | tf_op jit(solution)/shard_map/all_gather | solution.py:172
  538.9 17.5 fusion.88
  556.4 178.3 %all-gather.18.cloned.1.call-done = bf16[2048,8192]{1,0:T(8,128)(2,1)} async-done(((bf16[64,8192]{1,0:T(8,128)(2,1)}), bf16[2048,8192]{1,0:T(8,128)(2,1)}) %all-gather.18.cloned.1.call-update) | async-done | bytes 33554448 | tf_op jit(solution)/shard_map/all_gather | solution.py:173
  752.1 178.5 %all-gather.20.cloned.1.call-done = bf16[8192,2048]{1,0:T(8,128)(2,1)} async-done(((bf16[256,2048]{1,0:T(8,128)(2,1)}), bf16[8192,2048]{1,0:T(8,128)(2,1)}) %all-gather.20.cloned.1.call-update) | async-done | bytes 33554448 | tf_op jit(solution)/shard_map/all_gather | solution.py:182
  930.6 21.6 multiply_convert_fusion.1
  952.2 18.3 fusion.90
  970.5 20.0 multiply_reduce_fusion.1
  1034.3 91.1 %while.28 = (s32[]{:T(128)}, f32[1536,4,64]{0,2,1:T(8,128)}, f32[1536,4,64]{0,2,1:T(8,128)}, bf16[3,512,4,64]{1,3,2,0:T(8,128)(2,1)}, bf16[3,512,4,64]{1,3,2,0:T...) while((s32[]{:T(128)}, f32[1536,4,64]{0,2,1:T(8,128)}, ...), condition=%wide.region_9.10_spmd.clone, body=%wide.region_7.9_spmd.clone.sunk | while | flops 2044590592 | bytes 200323536 | solution.py:118
  1201.6 18.0 all_to_all.128
  1230.0 25.4 fusion.91
  1255.5 25.4 fusion.92
  1282.8 24.9 fusion.64
  1356.9 39.9 all-reduce.4
  1400.7 330.5 %reduce-scatter.8.cloned.1.call-done = f32[64,2048]{1,0:T(8,128)} async-done(((f32[2048,2048]{1,0:T(8,128)}), f32[64,2048]{1,0:T(8,128)}) %reduce-scatter.8.cloned.1.call-update) | async-done | bytes 524304 | tf_op jit(solution)/shard_map/reduce_scatter | solution.py:267
  1731.1 364.7 %reduce-scatter.10.cloned.1.call-done = f32[64,2048]{1,0:T(8,128)} async-done(((f32[2048,2048]{1,0:T(8,128)}), f32[64,2048]{1,0:T(8,128)}) %reduce-scatter.10.cloned.1.call-update) | async-done | bytes 524304 | tf_op jit(solution)/shard_map/reduce_scatter | solution.py:268
  2095.9 365.1 %reduce-scatter.12.cloned.1.call-done = f32[64,2048]{1,0:T(8,128)} async-done(((f32[2048,2048]{1,0:T(8,128)}), f32[64,2048]{1,0:T(8,128)}) %reduce-scatter.12.cloned.1.call-update) | async-done | bytes 524304 | tf_op jit(solution)/shard_map/reduce_scatter | solution.py:269
  2460.9 1411.4 %reduce-scatter.16.cloned.1.call-done = f32[64,8192]{1,0:T(8,128)} async-done(((f32[2048,8192]{1,0:T(8,128)}), f32[64,8192]{1,0:T(8,128)}) %reduce-scatter.16.cloned.1.call-update) | async-done | bytes 2097168 | tf_op jit(solution)/shard_map/reduce_scatter | solution.py:209
  3872.3 1413.6 %reduce-scatter.18.cloned.1.call-done = f32[64,8192]{1,0:T(8,128)} async-done(((f32[2048,8192]{1,0:T(8,128)}), f32[64,8192]{1,0:T(8,128)}) %reduce-scatter.18.cloned.1.call-update) | async-done | bytes 2097168 | tf_op jit(solution)/shard_map/reduce_scatter | solution.py:210
  5285.9 1413.4 %reduce-scatter.20.cloned.1.call-done = f32[256,2048]{1,0:T(8,128)} async-done(((f32[8192,2048]{1,0:T(8,128)}), f32[256,2048]{1,0:T(8,128)}) %reduce-scatter.20.cloned.1.call-update) | async-done | bytes 2097168 | tf_op jit(solution)/shard_map/reduce_scatter | solution.py:211
  (317 shorter events, 465.5 us)
Async XLA Ops:
  7.2 84.3 %all-gather.10.cloned.1.call-start = ((), (), s32[]{:S(2)}) async-start(), calls=%async_computation.16 | async-start | bytes 8650752 | tf_op jit(solution)/shard_map/all_gather | solution.py:140
  7.9 162.5 %all-gather.8.cloned.1.call-start = ((), (), s32[]{:S(2)}) async-start(), calls=%async_computation.15 | async-start | bytes 8650752 | tf_op jit(solution)/shard_map/all_gather | solution.py:139
  8.7 251.8 %all-gather.12.cloned.1.call-start = ((), (), s32[]{:S(2)}) async-start(), calls=%async_computation.17 | async-start | bytes 8650752 | tf_op jit(solution)/shard_map/all_gather | solution.py:141
  9.4 348.4 %all-gather.14.cloned.1.call-start = ((), (), s32[]{:S(2)}) async-start(), calls=%async_computation.18 | async-start | bytes 8650752 | tf_op jit(solution)/shard_map/all_gather | solution.py:165
  10.0 528.9 %all-gather.16.cloned.1.call-start = ((), (), s32[]{:S(2)}) async-start(), calls=%async_computation.19 | async-start | bytes 34603008 | tf_op jit(solution)/shard_map/all_gather | solution.py:172
  10.6 724.1 %all-gather.18.cloned.1.call-start = ((), (), s32[]{:S(2)}) async-start(), calls=%async_computation.20 | async-start | bytes 34603008 | tf_op jit(solution)/shard_map/all_gather | solution.py:173
  11.2 919.4 %all-gather.20.cloned.1.call-start = ((), (), s32[]{:S(2)}) async-start(), calls=%async_computation.21 | async-start | bytes 34603008 | tf_op jit(solution)/shard_map/all_gather | solution.py:182
  55.1 205.4 %copy-start.36 = (f32[2048]{0:T(1024)}, f32[2048]{0:T(1024)S(1)}, u32[]{:S(2)}) copy-start(f32[2048]{0:T(1024)S(1)} %convert_element_type.184) | copy-start | bytes 24580
  55.6 204.9 %copy-start.39 = (f32[192]{0:T(256)}, f32[192]{0:T(256)S(1)}, u32[]{:S(2)}) copy-start(f32[192]{0:T(256)S(1)} %add_rsqrt_fusion.1) | copy-start | bytes 2308
  196.6 20.7 all-to-all-start
  217.3 49.4 all-to-all-start.1
  266.7 17.8 all-to-all-start.2
  338.9 16.8 all-to-all-start.3
  343.1 1057.6 %reduce-scatter.14.cloned.1.call-start = ((), (), s32[]{:S(2)}) async-start(), calls=%async_computation.25 | async-start | bytes 17301504 | tf_op jit(solution)/shard_map/reduce_scatter | solution.py:270
  364.8 369.9 %copy-start.17 = (bf16[192,2048]{1,0:T(8,128)(2,1)}, bf16[192,2048]{1,0:T(8,128)(2,1)S(1)}, u32[]{:S(2)}) copy-start(bf16[192,2048]{1,0:T(8,128)(2,1)S(1)} %multiply_convert_fusion.4) | copy-start | bytes 2359300
  1010.0 19.2 all-to-all-start.4
  1129.4 19.0 all-to-all-start.6
  1148.5 19.6 all-to-all-start.5
  1152.7 578.5 %reduce-scatter.8.cloned.1.call-start = ((), (), s32[]{:S(2)}) async-start(), calls=%async_computation.22 | async-start | bytes 17301504 | tf_op jit(solution)/shard_map/reduce_scatter | solution.py:267
  1189.9 905.9 %reduce-scatter.10.cloned.1.call-start = ((), (), s32[]{:S(2)}) async-start(), calls=%async_computation.23 | async-start | bytes 17301504 | tf_op jit(solution)/shard_map/reduce_scatter | solution.py:268
  1198.3 1262.6 %reduce-scatter.12.cloned.1.call-start = ((), (), s32[]{:S(2)}) async-start(), calls=%async_computation.24 | async-start | bytes 17301504 | tf_op jit(solution)/shard_map/reduce_scatter | solution.py:269
  1228.9 2643.4 %reduce-scatter.16.cloned.1.call-start = ((), (), s32[]{:S(2)}) async-start(), calls=%async_computation.26 | async-start | bytes 69206016 | tf_op jit(solution)/shard_map/reduce_scatter | solution.py:209
  1255.4 4030.5 %reduce-scatter.18.cloned.1.call-start = ((), (), s32[]{:S(2)}) async-start(), calls=%async_computation.27 | async-start | bytes 69206016 | tf_op jit(solution)/shard_map/reduce_scatter | solution.py:210
  1280.9 5418.4 %reduce-scatter.20.cloned.1.call-start = ((), (), s32[]{:S(2)}) async-start(), calls=%async_computation.28 | async-start | bytes 69206016 | tf_op jit(solution)/shard_map/reduce_scatter | solution.py:211
  (65 other events, 737.1 us)
Sparse Core Ops, SparseCore 0:
  11.0 80.4 all-gather.9
  94.4 75.9 all-gather.7
  173.4 87.0 all-gather.11
  263.3 79.2 all-gather.13
  345.4 193.4 all-gather.15
  541.7 192.9 all-gather.17
  737.6 192.9 all-gather.19
  1002.4 358.8 reduce-scatter.13
  1364.1 367.0 reduce-scatter.7
  1733.8 361.9 reduce-scatter.9
  2098.7 362.1 reduce-scatter.11
  2463.7 1408.5 reduce-scatter.15
  3875.2 1410.6 reduce-scatter.17
  5288.6 1410.6 reduce-scatter.19
where the time goes:
time: 6720 us; the launch traced here: 6710 us
  waiting for transfers between devices  6050 us (90%)
  matrix products  355 us (5%)
  local copies, waits for them, and re-layouts  104 us (2%)
  blocking collectives  100 us (1%)
    reduce_scatter x1, waiting for transfers between devices, per_device(): lax.psum_scatter(grad_up_full, ('seq', 'fsdp'), scatter_dimension=0, tile...  1410 us
    reduce_scatter x1, waiting for transfers between devices, per_device(): lax.psum_scatter(grad_down_full, ('seq', 'fsdp'), scatter_dimension=0, ti...  1410 us
    reduce_scatter x1, waiting for transfers between devices, per_device(): lax.psum_scatter(grad_gate_full, ('seq', 'fsdp'), scatter_dimension=0, ti...  1410 us
    reduce_scatter x1, waiting for transfers between devices, per_device(): lax.psum_scatter(grad_value_w, ('seq', 'fsdp'), scatter_dimension=0, tile...  365 us
    reduce_scatter x1, waiting for transfers between devices, per_device(): lax.psum_scatter(grad_key_w, ('seq', 'fsdp'), scatter_dimension=0, tiled=...  365 us
    reduce_scatter x1, waiting for transfers between devices, per_device(): lax.psum_scatter(grad_query_w, ('seq', 'fsdp'), scatter_dimension=0, tile...  330 us
    all_gather x1, waiting for transfers between devices, per_device(): lax.all_gather(w_down, ('seq', 'fsdp'), axis=0, tiled=True)  179 us
    all_gather x1, waiting for transfers between devices, per_device(): up_rows = lax.all_gather(w_up, ('seq', 'fsdp'), axis=0, tiled=True)  178 us
  transfers between devices with their start and end apart: 21, of which 18 were waited for; matrix products, arithmetic and copies ran while one was open for 6% of the time, Pallas kernels for 0%

commit v1 on v0

v1 whole, which is shorter than its diff:
```python
import functools

import jax
import jax.numpy as jnp
from jax import lax
from jax.sharding import PartitionSpec as P

HEADS = 32
HD = 64


EPS = 1e-05
THETA = 130000.0

F32 = jnp.float32
LOW = jnp.bfloat16


def rms_scale(values):
    return lax.rsqrt(jnp.mean(values * values, axis=-1, keepdims=True) + EPS)


def rotary_tables(positions):
    halfway = HD // 2
    frequency = THETA ** (-(jnp.arange(halfway, dtype=F32) * 2.0) / HD)
    angles = positions.astype(F32)[:, None] * frequency[None, :]
    cosine = jnp.cos(angles)
    sine = jnp.sin(angles)
    return (
        jnp.concatenate([cosine, cosine], -1)[:, None, :],
        jnp.concatenate([sine, sine], -1)[:, None, :],
    )


def rotate(values):
    halfway = values.shape[-1] // 2
    return jnp.concatenate([-values[..., halfway:], values[..., :halfway]], -1)


def rotary(values, cosine, sine):
    return values * cosine + rotate(values) * sine


def rotary_back(values, cosine, sine):
    return values * cosine - rotate(values * sine)


def masked_scores(query_block, key_heads, query_places, key_places):
    scores = jnp.einsum(
        "qhd,khd->hqk", query_block, key_heads, preferred_element_type=F32
    ) * HD ** (-0.5)
    allowed = key_places[None, :] <= query_places[:, None]
    return jnp.where(allowed[None], scores, -1e30)


def attend_forward(queries, keys_all, values, places):
    length = queries.shape[0]
    heads = queries.shape[1] // HD
    block = min(512, length)
    count = length // block
    query_blocks = queries.reshape(count, block, heads, HD)
    key_heads = keys_all.reshape(length, heads, HD)
    value_heads = values.reshape(length, heads, HD)

    def one_block(pair):
        query_block, query_places = pair
        scores = masked_scores(query_block, key_heads, query_places, places)
        highest = jnp.max(scores, axis=-1, keepdims=True)
        weights = jnp.exp(scores - highest)
        totals = jnp.sum(weights, axis=-1, keepdims=True)
        probs = (weights / totals).astype(LOW)
        output = jnp.einsum("hqk,khd->qhd", probs, value_heads, preferred_element_type=F32)
        return (output.astype(LOW), (highest + jnp.log(totals))[..., 0])

    outputs, log_totals = lax.map(one_block, (query_blocks, places.reshape(count, block)))
    return (outputs.reshape(length, heads * HD), log_totals)


def attend_backward(queries, keys_all, values, grad_heads, log_totals, places):
    length = queries.shape[0]
    heads = queries.shape[1] // HD
    block = min(512, length)
    count = length // block
    scale = HD ** (-0.5)
    query_blocks = queries.reshape(count, block, heads, HD)
    grad_blocks = grad_heads.reshape(count, block, heads, HD)
    key_heads = keys_all.reshape(length, heads, HD)
    value_heads = values.reshape(length, heads, HD)

    def one_block(carry, inputs):
        key_sum, value_sum = carry
        query_block, grad_block, log_block, query_places = inputs
        scores = masked_scores(query_block, key_heads, query_places, places)
        probs = jnp.exp(scores - log_block[..., None])
        grad_probs = jnp.einsum(
            "qhd,khd->hqk", grad_block, value_heads, preferred_element_type=F32
        )
        inner = jnp.sum(probs * grad_probs, axis=-1, keepdims=True)
        grad_scores = (probs * (grad_probs - inner)).astype(LOW)
        grad_query = (
            jnp.einsum("hqk,khd->qhd", grad_scores, key_heads, preferred_element_type=F32) * scale
        )
        key_sum = (
            key_sum
            + jnp.einsum("hqk,qhd->khd", grad_scores, query_block, preferred_element_type=F32)
            * scale
        )
        value_sum = value_sum + jnp.einsum(
            "hqk,qhd->khd", probs.astype(LOW), grad_block, preferred_element_type=F32
        )
        return ((key_sum, value_sum), grad_query.astype(LOW))

    empty = jnp.zeros((length, heads, HD), F32)
    (key_sum, value_sum), grad_queries = lax.scan(
        one_block, (empty, empty), (query_blocks, grad_blocks, log_totals, places.reshape(count, block))
    )
    return (
        grad_queries.reshape(length, heads * HD),
        key_sum.astype(LOW).reshape(length, heads * HD),
        value_sum.astype(LOW).reshape(length, heads * HD),
    )


def flip(values, axis, count, mask):
    return lax.ppermute(values, axis, [(i, i ^ mask) for i in range(count)])


def bits_of(count):
    return list(range(count.bit_length() - 1))


def token_bits(count, half):
    bits = bits_of(count)
    return bits[:1] + (bits[1:] if half == 0 else bits[:0:-1])


def token_places(count, rows):
    me = lax.axis_index("seq")
    places = []
    for half in (0, 1):
        ranks = [0]
        for bit in reversed(token_bits(count, half)):
            ranks = ranks + [rank ^ (1 << bit) for rank in ranks]
        for rank in ranks:
            places.append((me ^ rank) * rows + half * (rows // 2) + jnp.arange(rows // 2, dtype=jnp.int32))
    return jnp.concatenate(places)


def gather_tokens(values, count):
    rows = values.shape[0] // 2
    halves = []
    for half in (0, 1):
        blocks = [values[half * rows : (half + 1) * rows]]
        for bit in reversed(token_bits(count, half)):
            blocks = blocks + [flip(block, "seq", count, 1 << bit) for block in blocks]
        halves.append(jnp.concatenate(blocks, 0))
    return halves


def reduce_tokens(part, size, count):
    outs = []
    for half in (0, 1):
        bits = token_bits(count, half)
        got = flip(part(half, size // 2, size).astype(LOW), "seq", count, 1 << bits[0])
        kept = part(half, 0, size // 2) + got.astype(F32)
        for bit in bits[1:]:
            middle = kept.shape[0] // 2
            got = flip(kept[middle:].astype(LOW), "seq", count, 1 << bit)
            kept = kept[:middle] + got.astype(F32)
        outs.append(kept)
    return jnp.concatenate(outs, 0)


def gather_rows(piece, count):
    me = lax.axis_index("fsdp")
    pieces = [(0, piece)]
    for bit in reversed(bits_of(count)):
        pieces = pieces + [(j ^ (1 << bit), flip(p, "fsdp", count, 1 << bit)) for j, p in pieces]
    outer, rows, width = piece.shape
    whole = jnp.zeros((outer, count, rows, width), piece.dtype)
    for j, p in pieces:
        whole = lax.dynamic_update_slice(whole, p[:, None], (0, me ^ j, 0, 0))
    return whole


def reduce_rows(whole, count):
    me = lax.axis_index("fsdp")
    outer, _, rows, width = whole.shape
    left = count
    for bit in bits_of(count):
        mine = (me >> bit) & 1
        pairs = whole.reshape(outer, left // 2, 2, rows, width)
        sent = lax.dynamic_slice_in_dim(pairs, 1 - mine, 1, 2).astype(LOW)
        kept = lax.dynamic_slice_in_dim(pairs, mine, 1, 2)
        got = flip(sent, "fsdp", count, 1 << bit)
        whole = kept.astype(F32) + got.astype(F32)
        left //= 2
    return whole.reshape(outer, rows, width)


def gather_small(values, counts):
    for axis in ("fsdp", "seq"):
        count = counts[axis]
        me = lax.axis_index(axis)
        for bit in bits_of(count):
            other = flip(values, axis, count, 1 << bit)
            mine = (me >> bit) & 1
            values = jnp.where(
                mine == 0,
                jnp.concatenate([values, other], -1),
                jnp.concatenate([other, values], -1),
            )
    return values


def scatter_small(values, counts):
    for axis in ("seq", "fsdp"):
        count = counts[axis]
        me = lax.axis_index(axis)
        for bit in reversed(bits_of(count)):
            mine = (me >> bit) & 1
            middle = values.shape[-1] // 2
            low, high = values[..., :middle], values[..., middle:]
            sent = jnp.where(mine == 0, high, low)
            values = jnp.where(mine == 0, low, high) + flip(sent, axis, count, 1 << bit)
    return values


def per_device(
    counts, tokens, cotangent, attn_gain, mlp_gain, w_q, w_k, w_v, w_o, w_gate, w_up, w_down
):
    seq, fsdp = counts["seq"], counts["fsdp"]
    rows = tokens.shape[1]
    width = tokens.shape[2]
    size = rows // 2 * seq
    inputs = tokens[0].astype(F32)
    own_grad = cotangent[0]
    heads = HEADS // seq
    group = heads * HD
    hidden = w_gate.shape[1] // seq
    wrows = w_q.shape[0]

    def columns(weight):
        return lax.all_to_all(
            weight.reshape(wrows, seq, weight.shape[1] // seq), "seq", split_axis=1, concat_axis=0, tiled=False
        )

    def to_columns(weight):
        return columns(weight).reshape(seq, wrows, -1)

    gains = gather_small(jnp.stack([attn_gain, mlp_gain]), counts).astype(F32)
    gain_one, gain_two = gains[0], gains[1]

    out_weight = gather_rows(w_o[None], fsdp).reshape(group, width)
    qkv_piece = to_columns(
        jnp.concatenate([w.reshape(wrows, seq, group) for w in (w_q, w_k, w_v)], -1).reshape(wrows, -1)
    )
    qkv_weight = gather_rows(qkv_piece, fsdp).reshape(width, 3 * group)
    gate_weight = gather_rows(to_columns(w_gate), fsdp).reshape(width, hidden)
    up_weight = gather_rows(to_columns(w_up), fsdp).reshape(width, hidden)
    down_weight = gather_rows(w_down[None], fsdp).reshape(hidden, width)

    places = token_places(seq, rows)
    cosine, sine = rotary_tables(places)
    scale_one = rms_scale(inputs)
    normal_one = inputs * scale_one
    normed_one = gather_tokens((normal_one * gain_one).astype(LOW), seq)
    grad_out = gather_tokens(own_grad, seq)

    length = 2 * size
    qkv = jnp.concatenate(
        [jnp.dot(h, qkv_weight, preferred_element_type=F32) for h in normed_one], 0
    )
    heads_shape = (length, heads, HD)
    queries = rotary(qkv[:, :group].reshape(heads_shape), cosine, sine).astype(LOW).reshape(length, group)
    keys_all = (
        rotary(qkv[:, group : 2 * group].reshape(heads_shape), cosine, sine).astype(LOW).reshape(length, group)
    )
    values = qkv[:, 2 * group :].astype(LOW)
    attended, log_totals = attend_forward(queries, keys_all, values, places)
    projected = reduce_tokens(
        lambda half, low, high: jnp.dot(
            attended[half * size + low : half * size + high], out_weight, preferred_element_type=F32
        ),
        size,
        seq,
    )
    middle = inputs + projected
    scale_two = rms_scale(middle)
    normal_two = middle * scale_two
    normed_two = gather_tokens((normal_two * gain_two).astype(LOW), seq)
    mixed, grad_gate, grad_up = [], [], []
    for half in (0, 1):
        gate = jnp.dot(normed_two[half], gate_weight, preferred_element_type=F32)
        up = jnp.dot(normed_two[half], up_weight, preferred_element_type=F32)
        sigmoid = jax.nn.sigmoid(gate)
        silu = gate * sigmoid
        mixed.append((silu * up).astype(LOW))
        grad_mixed = jnp.einsum("td,fd->tf", grad_out[half], down_weight, preferred_element_type=F32)
        grad_gate.append(
            (grad_mixed * up * sigmoid * (1.0 + gate * (1.0 - sigmoid))).astype(LOW)
        )
        grad_up.append((grad_mixed * silu).astype(LOW))
    down_sum = reduce_tokens(
        lambda half, low, high: jnp.dot(mixed[half][low:high], down_weight, preferred_element_type=F32),
        size,
        seq,
    )
    layer_out = (middle + down_sum).astype(LOW)[None]
    grad_normed = reduce_tokens(
        lambda half, low, high: jnp.einsum(
            "tf,df->td", grad_gate[half][low:high], gate_weight, preferred_element_type=F32
        )
        + jnp.einsum("tf,df->td", grad_up[half][low:high], up_weight, preferred_element_type=F32),
        size,
        seq,
    )
    mixed, grad_gate, grad_up, normed_one, normed_two, grad_out = (
        jnp.concatenate(pair, 0) for pair in (mixed, grad_gate, grad_up, normed_one, normed_two, grad_out)
    )

    def outer(left, right):
        return jnp.einsum("ti,to->io", left, right, preferred_element_type=F32).astype(LOW)

    def row_grad(left, right):
        whole = outer(left, right)
        return reduce_rows(whole.reshape(1, fsdp, -1, width), fsdp)[0]

    def column_grad(left, right):
        whole = outer(left, right)
        piece = reduce_rows(whole.reshape(seq, fsdp, wrows, -1), fsdp)
        swapped = lax.all_to_all(piece.astype(LOW), "seq", split_axis=0, concat_axis=1, tiled=False)
        return swapped.astype(F32)

    grad_down_w = row_grad(mixed, grad_out)
    grad_gate_w = column_grad(normed_two, grad_gate).reshape(wrows, -1)
    grad_up_w = column_grad(normed_two, grad_up).reshape(wrows, -1)
    gain_two_piece = jnp.sum(grad_normed * normal_two, axis=0)
    grad_two = grad_normed * gain_two
    grad_middle = own_grad.astype(F32) + scale_two * (
        grad_two - normal_two * jnp.mean(grad_two * normal_two, axis=-1, keepdims=True)
    )
    grad_proj = jnp.concatenate(gather_tokens(grad_middle.astype(LOW), seq), 0)
    grad_heads = jnp.einsum("to,io->ti", grad_proj, out_weight, preferred_element_type=F32).astype(LOW)
    grad_out_w = row_grad(attended, grad_proj)
    grad_query_rot, grad_key_rot, grad_values = attend_backward(
        queries, keys_all, values, grad_heads, log_totals, places
    )
    grad_queries = rotary_back(grad_query_rot.astype(F32).reshape(heads_shape), cosine, sine)
    grad_keys = rotary_back(grad_key_rot.astype(F32).reshape(heads_shape), cosine, sine)
    grad_qkv = jnp.concatenate(
        [
            grad_queries.astype(LOW).reshape(length, group),
            grad_keys.astype(LOW).reshape(length, group),
            grad_values,
        ],
        -1,
    )
    grad_qkv_w = column_grad(normed_one, grad_qkv)
    grad_normed = reduce_tokens(
        lambda half, low, high: jnp.einsum(
            "to,io->ti",
            grad_qkv[half * size + low : half * size + high],
            qkv_weight,
            preferred_element_type=F32,
        ),
        size,
        seq,
    )
    gain_one_piece = jnp.sum(grad_normed * normal_one, axis=0)
    grad_one = grad_normed * gain_one
    grad_inputs = grad_middle + scale_one * (
        grad_one - normal_one * jnp.mean(grad_one * normal_one, axis=-1, keepdims=True)
    )
    return (
        layer_out,
        grad_inputs.astype(LOW)[None],
        scatter_small(gain_one_piece, counts),
        scatter_small(gain_two_piece, counts),
        grad_qkv_w[:, :, :group].reshape(wrows, width),
        grad_qkv_w[:, :, group : 2 * group].reshape(wrows, width),
        grad_qkv_w[:, :, 2 * group :].reshape(wrows, width),
        grad_out_w,
        grad_gate_w,
        grad_up_w,
        grad_down_w,
    )


def solution(mesh):
    tokens = P("fsdp", "seq", None)
    vector = P(("seq", "fsdp"))
    matrix = P(("seq", "fsdp"), None)
    return jax.shard_map(
        functools.partial(per_device, dict(mesh.shape)),
        mesh=mesh,
        in_specs=(tokens, tokens, vector, vector) + (matrix,) * 7,
        out_specs=(tokens, tokens, vector, vector) + (matrix,) * 7,
        check_vma=False,
    )
```

time: 6720 us -> 1070 us (0.16)
  waiting for transfers between devices: 6050 us -> 459 us
  matrix products: 355 us -> 241 us
  blocking collectives: 100 us -> 0 us
  starting transfers between devices: 28.4 us -> 109 us
    reduce_scatter x7 -> x0, waiting for transfers between devices: 5300 us -> none  [the longest x1 1410 us: per_device(): lax.psum_scatter(grad_up_full, ('seq', 'fsdp'), scatter_dimension=0, tile...]
    all_gather x7 -> x0, waiting for transfers between devices: 673 us -> none  [the longest x1 179 us: per_device(): lax.all_gather(w_down, ('seq', 'fsdp'), axis=0, tiled=True)]
    ppermute x0 -> x120, waiting for transfers between devices: none -> 449 us  [flip(): return lax.ppermute(values, axis, [(i, i ^ mask) for i in range(count)])]
    dot_general x27 -> x40, matrix products: 298 us -> 176 us  [the longest x5 42.9 us: outer(): jnp.einsum('ti,to->io', left, right, preferred_element_type=F32).astype(LOW)]
    ppermute x0 -> x120, starting transfers between devices: none -> 83.9 us  [flip(): return lax.ppermute(values, axis, [(i, i ^ mask) for i in range(count)])]
    unnamed x2 -> x0, blocking collectives: 82.5 us -> none
  transfers between devices with their start and end apart: 21 -> 126, of which waited for: 18 -> 48; matrix products, arithmetic and copies ran while one was open for 6% -> 44% of each run, Pallas kernels for 0% -> 0%
where the time goes in v1:
time: 1070 us; the launch traced here: 1060 us
  waiting for transfers between devices  459 us (43%)
  matrix products  241 us (23%)
  local copies, waits for them, and re-layouts  156 us (15%)
  starting transfers between devices  109 us (10%)
  other arithmetic  91.4 us (9%)
    ppermute x120, waiting for transfers between devices, flip(): return lax.ppermute(values, axis, [(i, i ^ mask) for i in range(count)])  449 us
    ppermute x120, starting transfers between devices, flip(): return lax.ppermute(values, axis, [(i, i ^ mask) for i in range(count)])  83.9 us
    unnamed x299, local copies, waits for them, and re-layouts  74.7 us
    dot_general x5, matrix products, outer(): jnp.einsum('ti,to->io', left, right, preferred_element_type=F32).astype(LOW)  42.9 us
    dot_general x6, matrix products, masked_scores(): jnp.einsum('qhd,khd->hqk', query_block, key_heads, preferred_element_type...  24 us
    dynamic_update_slice x19, local copies, waits for them, and re-layouts, gather_rows(): whole = lax.dynamic_update_slice(whole, p[:, None], (0, me ^ j, 0, 0))  23.9 us
  transfers between devices with their start and end apart: 126, of which 48 were waited for; matrix products, arithmetic and copies ran while one was open for 44% of the time, Pallas kernels for 0%

profile of v1, /device:TPU:0, one launch (start us, length us, event | category | flops | bytes accessed | tf_op | source)
XLA Modules:
  0.0 1061.2 jit_solution(9025603226171367678)
XLA Ops:
  30.0 32.2 %collective-permute-done = bf16[2,64]{1,0:T(2,128)(2,1)} collective-permute-done((bf16[2,64]{1,0:T(2,128)(2,1)}, bf16[2,64]{1,0:T(2,128)(2,1)}, u32[]{:S(2)}, u32[]{:S(2)}) %collective-permute-start) | collective-permute-done | bytes 288 | tf_op jit(solution)/shard_map/ppermute | solution.py:125
  118.4 8.2 collective-permute-done.62
  133.7 9.2 collective-permute-done.7
  200.9 14.2 %collective-permute-done.12 = bf16[8,64,768]{2,1,0:T(8,128)(2,1)S(1)} collective-permute-done((bf16[8,64,768]{2,1,0:T(8,128)(2,1)}, bf16[8,64,768]{2,1,0:T(8,128)(2,1)S(1)}, u32[]{:S(2)}, u32[]{:S(2)}) %collective-permute-start.12) | collective-permute-done | bytes 786464 | tf_op jit(solution)/shard_map/ppermute | solution.py:125
  234.0 26.2 %collective-permute-done.38 = bf16[8,64,1024]{2,1,0:T(8,128)(2,1)S(1)} collective-permute-done((bf16[8,64,1024]{2,1,0:T(8,128)(2,1)}, bf16[8,64,1024]{2,1,0:T(8,128)(2,1)S(1)}, u32[]{:S(2)}, u32[]{:S(2)}) %collective-permute-start.38) | collective-permute-done | bytes 1048608 | tf_op jit(solution)/shard_map/ppermute | solution.py:125
  267.2 39.3 %collective-permute-done.14 = bf16[8,64,768]{2,1,0:T(8,128)(2,1)S(1)} collective-permute-done((bf16[8,64,768]{2,1,0:T(8,128)(2,1)S(1)}, bf16[8,64,768]{2,1,0:T(8,128)(2,1)S(1)}, u32[]{:S(2)}, u32[]{:S(2)}) %collective-permute-start.14) | collective-permute-done | bytes 786464 | tf_op jit(solution)/shard_map/ppermute | solution.py:125
  330.7 35.7 %while.27 = (s32[]{:T(128)}, bf16[3,512,4,64]{1,3,2,0:T(8,128)(2,1)S(1)}, f32[3,4,512]{2,1,0:T(4,128)}, s32[1536]{0:T(1024)S(1)}, s32[3,512]{1,0:T(4,128)S(1)}, ...) while((s32[]{:T(128)}, ...), condition=%wide.region_4.5_spmd, body=%wide.region_1.4_spmd.sunk | while | flops 843970560 | bytes 43070056 | solution.py:75
  390.2 9.9 collective-permute-done.26
  403.0 7.5 collective-permute-done.27
  425.3 9.9 collective-permute-done.33
  471.5 8.8 collective-permute-done.52
  490.1 8.6 multiply_convert_fusion.2
  498.7 7.6 convolution_convert_fusion
  509.2 9.5 convolution_convert_fusion.1
  518.6 10.0 convolution_convert_fusion.2
  557.5 9.3 collective-permute-done.68
  568.2 15.0 %collective-permute-done.48 = bf16[192,2048]{1,0:T(8,128)(2,1)} collective-permute-done((bf16[192,2048]{1,0:T(8,128)(2,1)S(1)}, bf16[192,2048]{1,0:T(8,128)(2,1)}, u32[]{:S(2)}, u32[]{:S(2)}) %collective-permute-start.48) | collective-permute-done | bytes 786464 | tf_op jit(solution)/shard_map/ppermute | solution.py:125
  624.8 62.5 %collective-permute-done.114 = bf16[8,2,1,64,1024]{4,3,0,2,1:T(8,128)(2,1)S(1)} collective-permute-done((bf16[8,2,1,64,1024]{4,3,0,2,1:T(8,128)(2,1)S(1)}, bf16[8,2,1,64,1024]{4,3,0,2,1:T(8,128)(2,1)S(1)}, u32[]{:S(2)}, u32[]{:S(2)}) %collective-permute-start.114) | collective-permute-done | bytes 2097184 | tf_op jit(solution)/shard_map/ppermute | solution.py:125
  706.4 39.8 %collective-permute-done.108 = f32[128]{0:T(128)S(1)} collective-permute-done((f32[128]{0:T(128)S(1)}, f32[128]{0:T(128)S(1)}, u32[]{:S(2)}, u32[]{:S(2)}) %collective-permute-start.108) | collective-permute-done | bytes 544 | tf_op jit(solution)/shard_map/ppermute | solution.py:125
  770.1 19.4 %collective-permute-done.82 = bf16[96,2048]{1,0:T(8,128)(2,1)S(1)} collective-permute-done((bf16[96,2048]{1,0:T(8,128)(2,1)S(1)}, bf16[96,2048]{1,0:T(8,128)(2,1)S(1)}, u32[]{:S(2)}, u32[]{:S(2)}) %collective-permute-start.82) | collective-permute-done | bytes 393248 | tf_op jit(solution)/shard_map/ppermute | solution.py:125
  822.7 98.3 %while.28 = (s32[]{:T(128)}, f32[1536,4,64]{0,2,1:T(8,128)}, f32[1536,4,64]{0,2,1:T(8,128)}, bf16[3,512,4,64]{1,3,2,0:T(8,128)(2,1)}, bf16[3,512,4,64]{1,3,2,0:T...) while((s32[]{:T(128)}, f32[1536,4,64]{0,2,1:T(8,128)}, ...), condition=%wide.region_9.10_spmd.clone, body=%wide.region_7.9_spmd.clone.sunk | while | flops 2044590080 | bytes 216061760 | solution.py:114
  929.2 10.1 convolution_convert_fusion.3
  974.6 8.9 collective-permute-done.110
  1011.8 27.2 %collective-permute-done.111 = bf16[8,1,1,64,768]{4,3,0,2,1:T(8,128)(2,1)S(1)} collective-permute-done((bf16[8,1,1,64,768]{4,3,0,2,1:T(8,128)(2,1)S(1)}, bf16[8,1,1,64,768]{4,3,0,2,1:T(8,128)(2,1)S(1)}, u32[]{:S(2)}, u32[]{:S(2)}) %collective-permute-start.111) | collective-permute-done | bytes 786464 | tf_op jit(solution)/shard_map/ppermute | solution.py:125
  (825 shorter events, 663.5 us)
Async XLA Ops:
  0.6 86.8 %collective-permute-start.22 = (bf16[1,64,2048]{2,1,0:T(8,128)(2,1)}, bf16[1,64,2048]{2,1,0:T(8,128)(2,1)}, u32[]{:S(2)}, u32[]{:S(2)}) collective-permute-start(bf16[1,64,2048]{2,1,0:T(8,128)(2,1)} %bitcast.449), channel_id=1, source_target_pairs={{0,2},{1,3},{2,0},{3,1},{4,6},{5,7},{6,4},{7,5},{8,10},{9,11},{10,... | collective-permute-start | bytes 786440 | tf_op jit(solution)/shard_map/ppermute | solution.py:125
  4.7 85.2 %collective-permute-start.23 = (bf16[1,64,2048]{2,1,0:T(8,128)(2,1)}, bf16[1,64,2048]{2,1,0:T(8,128)(2,1)}, u32[]{:S(2)}, u32[]{:S(2)}) collective-permute-start(bf16[1,64,2048]{2,1,0:T(8,128)(2,1)} %bitcast.450), channel_id=1, source_target_pairs={{0,1},{1,0},{2,3},{3,2},{4,5},{5,4},{6,7},{7,6},{8,9},{9,8},{10,11... | collective-permute-start | bytes 786440 | tf_op jit(solution)/shard_map/ppermute | solution.py:125
  6.3 165.2 %collective-permute-start.44 = (bf16[1,256,2048]{2,1,0:T(8,128)(2,1)}, bf16[1,256,2048]{2,1,0:T(8,128)(2,1)}, u32[]{:S(2)}, u32[]{:S(2)}) collective-permute-start(bf16[1,256,2048]{2,1,0:T(8,128)(2,1)} %bitcast.437), channel_id=1, source_target_pairs={{0,2},{1,3},{2,0},{3,1},{4,6},{5,7},{6,4},{7,5},{8,10},{9,11},{10,... | collective-permute-start | bytes 3145736 | tf_op jit(solution)/shard_map/ppermute | solution.py:125
  6.7 167.7 %collective-permute-start.45 = (bf16[1,256,2048]{2,1,0:T(8,128)(2,1)}, bf16[1,256,2048]{2,1,0:T(8,128)(2,1)}, u32[]{:S(2)}, u32[]{:S(2)}) collective-permute-start(bf16[1,256,2048]{2,1,0:T(8,128)(2,1)} %bitcast.438), channel_id=1, source_target_pairs={{0,1},{1,0},{2,3},{3,2},{4,5},{5,4},{6,7},{7,6},{8,9},{9,8},{10,11... | collective-permute-start | bytes 3145736 | tf_op jit(solution)/shard_map/ppermute | solution.py:125
  8.0 54.2 %collective-permute-start = (bf16[2,64]{1,0:T(2,128)(2,1)}, bf16[2,64]{1,0:T(2,128)(2,1)}, u32[]{:S(2)}, u32[]{:S(2)}) collective-permute-start(bf16[2,64]{1,0:T(2,128)(2,1)} %pad_maximum_fusion.9), channel_id=1, source_target_pairs={{0,1},{1,0},{2,3},{3,2},{4,5},{5,4},{6,7},{7,6},{8,9},{9,8},{10,11... | collective-permute-start | bytes 776 | tf_op jit(solution)/shard_map/ppermute | solution.py:125
  14.1 98.5 %all-to-all-start = ((bf16[1,64,8,768]{3,1,0,2:T(8,128)(2,1)}), bf16[1,64,8,768]{3,1,0,2:T(8,128)(2,1)}, u32[]{:S(2)}, u32[]{:S(2)}) async-start(bf16[1,64,8,768]{3,1,0,2:T(8,128)(2,1)} %copy.116), calls=%async_computation | async-start | bytes 1572864 | tf_op jit(solution)/shard_map/all_to_all | solution.py:244
  191.4 68.7 %collective-permute-start.38 = (bf16[8,64,1024]{2,1,0:T(8,128)(2,1)}, bf16[8,64,1024]{2,1,0:T(8,128)(2,1)S(1)}, u32[]{:S(2)}, u32[]{:S(2)}) collective-permute-start(bf16[8,64,1024]{2,1,0:T(8,128)(2,1)} %bitcast.40), channel_id=1, source_target_pairs={{0,2},{1,3},{2,0},{3,1},{4,6},{5,7},{6,4},{7,5},{8,10},{9,11},{10,... | collective-permute-start | bytes 3145736 | tf_op jit(solution)/shard_map/ppermute | solution.py:125
  195.0 175.4 %collective-permute-start.39 = (bf16[8,64,1024]{2,1,0:T(8,128)(2,1)}, bf16[8,64,1024]{2,1,0:T(8,128)(2,1)}, u32[]{:S(2)}, u32[]{:S(2)}) collective-permute-start(bf16[8,64,1024]{2,1,0:T(8,128)(2,1)} %bitcast.40), channel_id=1, source_target_pairs={{0,1},{1,0},{2,3},{3,2},{4,5},{5,4},{6,7},{7,6},{8,9},{9,8},{10,11... | collective-permute-start | bytes 3145736 | tf_op jit(solution)/shard_map/ppermute | solution.py:125
  196.7 176.1 %collective-permute-start.41 = (bf16[8,64,1024]{2,1,0:T(8,128)(2,1)}, bf16[8,64,1024]{2,1,0:T(8,128)(2,1)}, u32[]{:S(2)}, u32[]{:S(2)}) collective-permute-start(bf16[8,64,1024]{2,1,0:T(8,128)(2,1)} %bitcast.53), channel_id=1, source_target_pairs={{0,2},{1,3},{2,0},{3,1},{4,6},{5,7},{6,4},{7,5},{8,10},{9,11},{10,... | collective-permute-start | bytes 3145736 | tf_op jit(solution)/shard_map/ppermute | solution.py:125
  263.5 110.7 %collective-permute-start.42 = (bf16[8,64,1024]{2,1,0:T(8,128)(2,1)}, bf16[8,64,1024]{2,1,0:T(8,128)(2,1)}, u32[]{:S(2)}, u32[]{:S(2)}) collective-permute-start(bf16[8,64,1024]{2,1,0:T(8,128)(2,1)} %bitcast.53), channel_id=1, source_target_pairs={{0,1},{1,0},{2,3},{3,2},{4,5},{5,4},{6,7},{7,6},{8,9},{9,8},{10,11... | collective-permute-start | bytes 3145736 | tf_op jit(solution)/shard_map/ppermute | solution.py:125
  266.3 111.3 %collective-permute-start.46 = (bf16[1,256,2048]{2,1,0:T(8,128)(2,1)}, bf16[1,256,2048]{2,1,0:T(8,128)(2,1)}, u32[]{:S(2)}, u32[]{:S(2)}) collective-permute-start(bf16[1,256,2048]{2,1,0:T(8,128)(2,1)} %collective-permute-done.44), channel_id=1, source_target_pairs={{0,1},{1,0},{2,3},{3,2},{4,5},{5,4},{6,7},{7,6},{8,9},{9,8},{10,11... | collective-permute-start | bytes 3145736 | tf_op jit(solution)/shard_map/ppermute | solution.py:125
  463.2 82.1 %collective-permute-start.67 = (bf16[384,2048]{1,0:T(8,128)(2,1)}, bf16[384,2048]{1,0:T(8,128)(2,1)S(1)}, u32[]{:S(2)}, u32[]{:S(2)}) collective-permute-start(bf16[384,2048]{1,0:T(8,128)(2,1)} %add_convert_fusion.1), channel_id=1, source_target_pairs={{0,4},{4,0},{8,12},{12,8},{16,20},{20,16},{24,28},{28,24},{1,5},{5... | collective-permute-start | bytes 4718600 | tf_op jit(solution)/shard_map/ppermute | solution.py:125
  468.9 78.5 %collective-permute-start.47 = (bf16[384,2048]{1,0:T(8,128)(2,1)}, bf16[384,2048]{1,0:T(8,128)(2,1)}, u32[]{:S(2)}, u32[]{:S(2)}) collective-permute-start(bf16[384,2048]{1,0:T(8,128)(2,1)} %convolution_convert_fusion.7), channel_id=1, source_target_pairs={{0,4},{4,0},{8,12},{12,8},{16,20},{20,16},{24,28},{28,24},{1,5},{5... | collective-permute-start | bytes 4718600 | tf_op jit(solution)/shard_map/ppermute | solution.py:125
  506.6 101.9 %collective-permute-start.118 = (bf16[1,2,1,256,2048]{4,3,2,1,0:T(8,128)(2,1)S(1)}, bf16[1,2,1,256,2048]{4,3,2,1,0:T(8,128)(2,1)}, u32[]{:S(2)}, u32[]{:S(2)}) collective-permute-start(bf16[1,2,1,256,2048]{4,3,2,1,0:T(8,128)(2,1)S(1)} %constant_dynamic-slice_fusion.2), channel_id=1, source_target_pairs={{0,1},{1,0},{2,3},{3,2},{4,5},{5,4},{6,7},{7,6},{8,9},{9,8},{10,11... | collective-permute-start | bytes 6291464 | tf_op jit(solution)/shard_map/ppermute | solution.py:125
  534.2 51.8 %collective-permute-start.77 = (bf16[384,2048]{1,0:T(8,128)(2,1)}, bf16[384,2048]{1,0:T(8,128)(2,1)}, u32[]{:S(2)}, u32[]{:S(2)}) collective-permute-start(bf16[384,2048]{1,0:T(8,128)(2,1)} %add_convert_fusion), channel_id=1, source_target_pairs={{0,4},{4,0},{8,12},{12,8},{16,20},{20,16},{24,28},{28,24},{1,5},{5... | collective-permute-start | bytes 4718600 | tf_op jit(solution)/shard_map/ppermute | solution.py:125
  555.4 57.2 %collective-permute-start.116 = (bf16[8,2,1,64,1024]{4,3,0,2,1:T(8,128)(2,1)}, bf16[8,2,1,64,1024]{4,3,0,2,1:T(8,128)(2,1)}, u32[]{:S(2)}, u32[]{:S(2)}) collective-permute-start(bf16[8,2,1,64,1024]{4,3,0,2,1:T(8,128)(2,1)} %copy.157), channel_id=1, source_target_pairs={{0,1},{1,0},{2,3},{3,2},{4,5},{5,4},{6,7},{7,6},{8,9},{9,8},{10,11... | collective-permute-start | bytes 6291464 | tf_op jit(solution)/shard_map/ppermute | solution.py:125
  583.3 104.0 %collective-permute-start.114 = (bf16[8,2,1,64,1024]{4,3,0,2,1:T(8,128)(2,1)S(1)}, bf16[8,2,1,64,1024]{4,3,0,2,1:T(8,128)(2,1)S(1)}, u32[]{:S(2)}, u32[]{:S(2)}) collective-permute-start(bf16[8,2,1,64,1024]{4,3,0,2,1:T(8,128)(2,1)S(1)} %copy.155), channel_id=1, source_target_pairs={{0,1},{1,0},{2,3},{3,2},{4,5},{5,4},{6,7},{7,6},{8,9},{9,8},{10,11... | collective-permute-start | bytes 6291464 | tf_op jit(solution)/shard_map/ppermute | solution.py:125
  606.6 86.1 %collective-permute-start.58 = (bf16[192,2048]{1,0:T(8,128)(2,1)S(1)}, bf16[192,2048]{1,0:T(8,128)(2,1)S(1)}, u32[]{:S(2)}, u32[]{:S(2)}) collective-permute-start(bf16[192,2048]{1,0:T(8,128)(2,1)S(1)} %slice.647), channel_id=1, source_target_pairs={{0,16},{4,20},{8,24},{12,28},{16,0},{20,4},{24,8},{28,12},{1,17},{... | collective-permute-start | bytes 2359304 | tf_op jit(solution)/shard_map/ppermute | solution.py:125
  611.0 147.3 %collective-permute-start.119 = (bf16[1,1,1,256,2048]{4,3,2,1,0:T(8,128)(2,1)S(1)}, bf16[1,1,1,256,2048]{4,3,2,1,0:T(8,128)(2,1)}, u32[]{:S(2)}, u32[]{:S(2)}) collective-permute-start(bf16[1,1,1,256,2048]{4,3,2,1,0:T(8,128)(2,1)S(1)} %dynamic-slice_convert_fusion), channel_id=1, source_target_pairs={{0,2},{1,3},{2,0},{3,1},{4,6},{5,7},{6,4},{7,5},{8,10},{9,11},{10,... | collective-permute-start | bytes 3145736 | tf_op jit(solution)/shard_map/ppermute | solution.py:125
  615.2 137.4 %collective-permute-start.117 = (bf16[8,1,1,64,1024]{4,3,0,2,1:T(8,128)(2,1)S(1)}, bf16[8,1,1,64,1024]{4,3,0,2,1:T(8,128)(2,1)S(1)}, u32[]{:S(2)}, u32[]{:S(2)}) collective-permute-start(bf16[8,1,1,64,1024]{4,3,0,2,1:T(8,128)(2,1)S(1)} %dynamic-slice_convert_fusion.1), channel_id=1, source_target_pairs={{0,2},{1,3},{2,0},{3,1},{4,6},{5,7},{6,4},{7,5},{8,10},{9,11},{10,... | collective-permute-start | bytes 3145736 | tf_op jit(solution)/shard_map/ppermute | solution.py:125
  623.7 65.7 %collective-permute-start.79 = (bf16[96,2048]{1,0:T(8,128)(2,1)S(1)}, bf16[96,2048]{1,0:T(8,128)(2,1)S(1)}, u32[]{:S(2)}, u32[]{:S(2)}) collective-permute-start(bf16[96,2048]{1,0:T(8,128)(2,1)S(1)} %slice.653), channel_id=1, source_target_pairs={{0,8},{4,12},{8,0},{12,4},{16,24},{20,28},{24,16},{28,20},{1,9},{5... | collective-permute-start | bytes 1179656 | tf_op jit(solution)/shard_map/ppermute | solution.py:125
  689.4 74.4 %collective-permute-start.115 = (bf16[8,1,1,64,1024]{4,3,0,2,1:T(8,128)(2,1)}, bf16[8,1,1,64,1024]{4,3,0,2,1:T(8,128)(2,1)S(1)}, u32[]{:S(2)}, u32[]{:S(2)}) collective-permute-start(bf16[8,1,1,64,1024]{4,3,0,2,1:T(8,128)(2,1)} %dynamic-slice_convert_fusion.2), channel_id=1, source_target_pairs={{0,2},{1,3},{2,0},{3,1},{4,6},{5,7},{6,4},{7,5},{8,10},{9,11},{10,... | collective-permute-start | bytes 3145736 | tf_op jit(solution)/shard_map/ppermute | solution.py:125
  693.0 54.5 %collective-permute-start.59 = (bf16[96,2048]{1,0:T(8,128)(2,1)S(1)}, bf16[96,2048]{1,0:T(8,128)(2,1)S(1)}, u32[]{:S(2)}, u32[]{:S(2)}) collective-permute-start(bf16[96,2048]{1,0:T(8,128)(2,1)S(1)} %slice.655), channel_id=1, source_target_pairs={{0,8},{4,12},{8,0},{12,4},{16,24},{20,28},{24,16},{28,20},{1,9},{5... | collective-permute-start | bytes 1179656 | tf_op jit(solution)/shard_map/ppermute | solution.py:125
  754.0 190.4 %all-to-all-start.5 = ((bf16[8,64,1,1024]{3,1,2,0:T(8,128)(2,1)}), bf16[8,64,1,1024]{3,1,2,0:T(8,128)(2,1)}, u32[]{:S(2)}, u32[]{:S(2)}) async-start(bf16[8,64,1,1024]{3,1,2,0:T(8,128)(2,1)} %fusion.80), calls=%async_computation.5 | async-start | bytes 2097152 | tf_op jit(solution)/shard_map/all_to_all | solution.py:332
  (221 other events, 3266.1 us)

commit v2 on v1

v2 whole, which is shorter than its diff:
```python
import functools

import jax
import jax.numpy as jnp
from jax import lax
from jax.experimental import pallas as pl
from jax.experimental.pallas import tpu as pltpu
from jax.sharding import PartitionSpec as P

HEADS = 32
HD = 64
PAIR = 2 * HD
LANES = 128
TILE = 256
NT = (((1,), (1,)), ((), ()))

EPS = 1e-05
THETA = 130000.0

F32 = jnp.float32
LOW = jnp.bfloat16


def rms_scale(values):
    return lax.rsqrt(jnp.mean(values * values, axis=-1, keepdims=True) + EPS)


def rotary_tables(length):
    halfway = HD // 2
    frequency = THETA ** (-(jnp.arange(halfway, dtype=F32) * 2.0) / HD)
    angles = jnp.arange(length, dtype=jnp.int32).astype(F32)[:, None] * frequency[None, :]
    cosine = jnp.cos(angles)
    sine = jnp.sin(angles)
    return (
        jnp.concatenate([cosine, cosine, cosine, cosine], -1),
        jnp.concatenate([-sine, sine, -sine, sine], -1),
    )


def head_lanes(head):
    lane = lax.broadcasted_iota(jnp.int32, (1, PAIR), 1)
    return (lane >= head * HD) & (lane < (head + 1) * HD)


def half_turn(values):
    lane = lax.broadcasted_iota(jnp.int32, values.shape, 1)
    return jnp.where(
        lane % HD < HD // 2,
        pltpu.roll(values, PAIR - HD // 2, 1),
        pltpu.roll(values, HD // 2, 1),
    )


def causal(shape):
    return lax.broadcasted_iota(jnp.int32, shape, 0) <= lax.broadcasted_iota(jnp.int32, shape, 1)


def attend_kernel(
    block, order, q, k, v, cos, sin, q_out, k_out, v_out, o_out, log_out,
    v_turn, o_turn, o_flat, scores,
):
    length = q_out.shape[0]
    count = length // block
    for b in range(count):
        here = slice(b * block, (b + 1) * block)
        there = pl.ds(pl.multiple_of(order[b] * block, block), block)
        c, s = cos[there, :], sin[there, :]
        u = q[here, :]
        q_out[there, :] = (u * c + half_turn(u) * s).astype(LOW)
        u = k[here, :]
        k_out[there, :] = (u * c + half_turn(u) * s).astype(LOW)
        v_out[there, :] = v[here, :].astype(LOW)
    v_turn[...] = v_out[...].astype(F32).T.astype(LOW)
    for i in range(length // TILE):
        queries = q_out[i * TILE : (i + 1) * TILE, :] * HD ** (-0.5)
        for head in range(2):
            mine = jnp.where(head_lanes(head), queries, 0).astype(LOW)
            rows = slice(head * HD, (head + 1) * HD)
            highest = None
            for j in range(i + 1):
                part = lax.dot_general(
                    k_out[j * TILE : (j + 1) * TILE, :], mine, NT, preferred_element_type=F32
                )
                if i == j:
                    part = jnp.where(causal(part.shape), part, -1e30)
                scores[head, j * TILE : (j + 1) * TILE, :] = part
                top = jnp.max(part, axis=0, keepdims=True)
                highest = top if highest is None else jnp.maximum(highest, top)
            total = jnp.zeros((1, TILE), F32)
            acc = jnp.zeros((HD, TILE), F32)
            for j in range(i + 1):
                weights = jnp.exp(scores[head, j * TILE : (j + 1) * TILE, :] - highest)
                total += jnp.sum(weights, axis=0, keepdims=True)
                acc += jnp.dot(
                    v_turn[rows, j * TILE : (j + 1) * TILE], weights.astype(LOW), preferred_element_type=F32
                )
            o_turn[rows, i * TILE : (i + 1) * TILE] = acc / total
            log_out[0, head : head + 1, i * TILE : (i + 1) * TILE] = highest + jnp.log(total)
    o_flat[...] = o_turn[...].T
    for b in range(count):
        there = pl.ds(pl.multiple_of(order[b] * block, block), block)
        o_out[b * block : (b + 1) * block, :] = o_flat[there, :].astype(LOW)


def attend_forward(qkv, order, cos, sin, block):
    length, group = qkv.shape[0], qkv.shape[1] // 3
    pairs = group // PAIR

    def column(which):
        return pl.BlockSpec((length, PAIR), lambda p, order: (0, which * pairs + p))

    whole = pl.BlockSpec((length, PAIR), lambda p, order: (0, p))
    table = pl.BlockSpec((length, PAIR), lambda p, order: (0, 0))
    low = jax.ShapeDtypeStruct((length, group), LOW)
    return pl.pallas_call(
        functools.partial(attend_kernel, block),
        grid_spec=pltpu.PrefetchScalarGridSpec(
            num_scalar_prefetch=1,
            grid=(pairs,),
            in_specs=[column(0), column(1), column(2), table, table],
            out_specs=[whole] * 4 + [pl.BlockSpec((1, 2, length), lambda p, order: (p, 0, 0))],
            scratch_shapes=[
                pltpu.VMEM((PAIR, length), LOW),
                pltpu.VMEM((PAIR, length), F32),
                pltpu.VMEM((length, PAIR), F32),
                pltpu.VMEM((2, length, TILE), F32),
            ],
        ),
        out_shape=[low] * 4 + [jax.ShapeDtypeStruct((pairs, 2, length), F32)],
        compiler_params=pltpu.CompilerParams(vmem_limit_bytes=50 << 20),
        name="attend_forward",
    )(order, qkv, qkv, qkv, cos, sin)


def attend_back_kernel(
    block, order, q, k, v, o, grad, log, cos, sin, dq_out, dk_out, dv_out,
    do, k_turn, delta, dk, dv, dq_turn, flat,
):
    length = q.shape[0]
    count = length // block
    for b in range(count):
        here = slice(b * block, (b + 1) * block)
        there = pl.ds(pl.multiple_of(order[b] * block, block), block)
        do[there, :] = grad[here, :]
        flat[there, :] = grad[here, :].astype(F32) * o[here, :].astype(F32)
    turned = flat[...].T
    for head in range(2):
        delta[head : head + 1, :] = jnp.sum(turned[head * HD : (head + 1) * HD], axis=0, keepdims=True)
    k_turn[...] = k[...].astype(F32).T.astype(LOW)
    dk[...] = jnp.zeros_like(dk)
    dv[...] = jnp.zeros_like(dv)
    for i in range(length // TILE):
        span = slice(i * TILE, (i + 1) * TILE)
        queries = q[span, :] * HD ** (-0.5)
        for head in range(2):
            lanes = head_lanes(head)
            rows = slice(head * HD, (head + 1) * HD)
            mine = jnp.where(lanes, queries, 0).astype(LOW)
            mine_do = jnp.where(lanes, do[span, :], 0).astype(LOW)
            log_here = log[0, head : head + 1, span]
            delta_here = delta[head : head + 1, span]
            acc = jnp.zeros((HD, TILE), F32)
            for j in range(i + 1):
                keys = slice(j * TILE, (j + 1) * TILE)
                part = lax.dot_general(k[keys, :], mine, NT, preferred_element_type=F32)
                probs = jnp.exp(part - log_here)
                if i == j:
                    probs = jnp.where(causal(part.shape), probs, 0.0)
                d_probs = lax.dot_general(v[keys, :], mine_do, NT, preferred_element_type=F32)
                d_scores = (probs * (d_probs - delta_here)).astype(LOW)
                dv[keys, :] += jnp.dot(probs.astype(LOW), mine_do, preferred_element_type=F32)
                dk[keys, :] += jnp.dot(d_scores, mine, preferred_element_type=F32)
                acc += jnp.dot(k_turn[rows, keys], d_scores, preferred_element_type=F32)
            dq_turn[rows, span] = acc * HD ** (-0.5)
    flat[...] = dq_turn[...].T
    for b in range(count):
        here = slice(b * block, (b + 1) * block)
        there = pl.ds(pl.multiple_of(order[b] * block, block), block)
        c, s = cos[there, :], sin[there, :]
        u = flat[there, :].astype(LOW).astype(F32)
        dq_out[here, :] = (u * c - half_turn(u) * s).astype(LOW)
        u = dk[there, :].astype(LOW).astype(F32)
        dk_out[here, :] = (u * c - half_turn(u) * s).astype(LOW)
        dv_out[here, :] = dv[there, :].astype(LOW)


def attend_backward(q, k, v, o, grad, log, order, cos, sin, block):
    length, group = q.shape
    pairs = group // PAIR
    whole = pl.BlockSpec((length, PAIR), lambda p, order: (0, p))
    table = pl.BlockSpec((length, PAIR), lambda p, order: (0, 0))
    low = jax.ShapeDtypeStruct((length, group), LOW)
    return pl.pallas_call(
        functools.partial(attend_back_kernel, block),
        grid_spec=pltpu.PrefetchScalarGridSpec(
            num_scalar_prefetch=1,
            grid=(pairs,),
            in_specs=[whole] * 5 + [pl.BlockSpec((1, 2, length), lambda p, order: (p, 0, 0)), table, table],
            out_specs=[whole] * 3,
            scratch_shapes=[
                pltpu.VMEM((length, PAIR), LOW),
                pltpu.VMEM((PAIR, length), LOW),
                pltpu.VMEM((2, length), F32),
                pltpu.VMEM((length, PAIR), F32),
                pltpu.VMEM((length, PAIR), F32),
                pltpu.VMEM((PAIR, length), F32),
                pltpu.VMEM((length, PAIR), F32),
            ],
        ),
        out_shape=[low] * 3,
        compiler_params=pltpu.CompilerParams(vmem_limit_bytes=50 << 20),
        name="attend_backward",
    )(order, q, k, v, o, grad, log, cos, sin)


def pieces_of(width, seq, fsdp):
    piece = width // (seq * fsdp)
    for i in range(seq):
        for j in range(fsdp):
            here, there = i * fsdp + j, j * seq + i
            yield slice(here * piece, (here + 1) * piece), slice(there * piece, (there + 1) * piece)


def norm_kernel(seq, fsdp, which, gains, tokens, *refs):
    if which:
        terms, (middle, normed, flat) = refs[:-3], refs[-3:]
        block = terms[0].shape[0]
        each = len(terms) // 2
        for half in range(2):
            rows = slice(half * block, (half + 1) * block)
            total = tokens[rows, :].astype(F32)
            for term in terms[half * each : (half + 1) * each]:
                total = total + term[...].astype(F32)
            middle[rows, :] = total
        values = middle[...]
    else:
        normed, flat = refs
        values = tokens[...].astype(F32)
    normal = values * rms_scale(values)
    for here, there in pieces_of(normal.shape[1], seq, fsdp):
        flat[:, there] = normal[:, here]
    normed[...] = (flat[...] * gains[which : which + 1, :].astype(F32)).astype(LOW)


def norm_back_kernel(seq, fsdp, which, gains, source, straight, *refs):
    count = len([r for r in refs if r.shape[0] * 2 == source.shape[0]])
    terms, outs, (flat, sums) = refs[:count], refs[count:-2], refs[-2:]
    block = terms[0].shape[0]
    each = count // 2
    for half in range(2):
        total = None
        for term in terms[half * each : (half + 1) * each]:
            total = term[...].astype(F32) if total is None else total + term[...].astype(F32)
        sums[half * block : (half + 1) * block, :] = total * gains[which : which + 1, :].astype(F32)
    for here, there in pieces_of(source.shape[1], seq, fsdp):
        flat[:, here] = sums[:, there]
    values = source[...].astype(F32)
    scale = rms_scale(values)
    normal = values * scale
    grad = flat[...]
    total = straight[...].astype(F32) + scale * (
        grad - normal * jnp.mean(grad * normal, axis=-1, keepdims=True)
    )
    for out in outs:
        out[...] = total.astype(out.dtype)


def norm_call(kernel, name, counts, which, gains, args, sums, outs, steps=1):
    size, width = args[0].shape
    rows = size // steps
    whole = pl.BlockSpec((rows, width), lambda i: (i, 0))
    half = pl.BlockSpec((rows // 2, width), lambda i: (0, 0))
    flat = pltpu.VMEM((rows, width), F32)
    return pl.pallas_call(
        functools.partial(kernel, counts["seq"], counts["fsdp"], which),
        grid=(steps,),
        in_specs=[pl.BlockSpec(gains.shape, lambda i: (0, 0))] + [whole] * len(args) + [half] * len(sums),
        out_specs=[whole] * len(outs),
        out_shape=[jax.ShapeDtypeStruct((size, width), dtype) for dtype in outs],
        scratch_shapes=[flat] if kernel is norm_kernel else [flat, flat],
        compiler_params=pltpu.CompilerParams(vmem_limit_bytes=40 << 20),
        name=name,
    )(gains, *args, *sums)


def flip(values, axis, count, mask):
    return lax.ppermute(values, axis, [(i, i ^ mask) for i in range(count)])


def bits_of(count):
    return list(range(count.bit_length() - 1))


def token_bits(count, half):
    bits = bits_of(count)
    return bits[:1] + (bits[1:] if half == 0 else bits[:0:-1])


def by_core(parts):
    middle = len(parts[0]) // 2
    return parts[0][:middle] + parts[1][:middle] + parts[0][middle:] + parts[1][middle:]


def token_order(count):
    me = lax.axis_index("seq")
    parts = []
    for half in (0, 1):
        ranks = [0]
        for bit in reversed(token_bits(count, half)):
            ranks = ranks + [rank ^ (1 << bit) for rank in ranks]
        parts.append([(me ^ rank) * 2 + half for rank in ranks])
    return jnp.stack(by_core(parts)).astype(jnp.int32)


def after(values, *others):
    return lax.optimization_barrier((values,) + others)[0]


def gather_tokens(values, count):
    rows = values.shape[0] // 2
    parts = []
    for half in (0, 1):
        part = [values[half * rows : (half + 1) * rows]]
        for bit in reversed(token_bits(count, half)):
            part = part + [flip(block, "seq", count, 1 << bit) for block in part]
        parts.append(part)
    return jnp.concatenate(by_core(parts), 0)


def reduce_tokens(values, weight, dims, count, pins=(), parts=1):
    size = values.shape[0] // 2

    def part(rows):
        return lax.dot_general(rows, weight, (dims, ((), ())), preferred_element_type=F32)

    def pinned(step, got, kept):
        return pins[step](got, kept) if step < len(pins) and pins[step] else got

    rows = size // parts
    got = [
        flip(part(values[size + i * rows : size + (i + 1) * rows]).astype(LOW), "seq", count, 1)
        for i in range(parts)
    ]
    kept = [part(values[i * rows : (i + 1) * rows]) for i in range(parts)]
    kept = [k + g.astype(F32) for k, g in zip(kept, pinned(0, got, kept))]
    if parts == 1:
        kept = [kept[0][: size // 2], kept[0][size // 2 :]]
    for step in range(1, count.bit_length() - 1):
        got = []
        for half in (0, 1):
            middle = kept[half].shape[0] // 2
            sent = kept[half][middle:].astype(LOW)
            kept[half] = kept[half][:middle]
            got.append(flip(sent, "seq", count, 1 << token_bits(count, half)[step]))
        got = pinned(step, got, kept)
        if step < count.bit_length() - 2:
            kept = [k + g.astype(F32) for k, g in zip(kept, got)]
    return [kept[0], got[0], kept[1], got[1]]


def per_device(
    counts, tokens, cotangent, attn_gain, mlp_gain, w_q, w_k, w_v, w_o, w_gate, w_up, w_down
):
    seq, fsdp = counts["seq"], counts["fsdp"]
    rows = tokens.shape[1]
    width = tokens.shape[2]
    block = rows // 2
    length = rows * seq
    own_tokens = tokens[0]
    own_grad = cotangent[0]
    group = HEADS // seq * HD
    hidden = w_gate.shape[1] // seq
    wrows = w_q.shape[0]
    def swap(*weights):
        piece = jnp.concatenate([w.reshape(wrows, seq, -1) for w in weights], -1)
        return lax.all_to_all(piece, "seq", split_axis=1, concat_axis=0, tiled=True).reshape(seq * wrows, -1)

    def swap_back(piece):
        return lax.all_to_all(
            piece.reshape(seq, wrows, -1), "seq", split_axis=0, concat_axis=1, tiled=False
        )

    def gathered(piece):
        return lax.all_gather(piece, "fsdp", axis=0, tiled=True)

    def summed(whole):
        return lax.psum_scatter(whole, "fsdp", scatter_dimension=0, tiled=True)

    def outer(left, right):
        return jnp.einsum("ti,to->io", left, right, preferred_element_type=F32).astype(LOW)

    near = jnp.zeros((wrows, LANES), LOW).at[:, 0].set(attn_gain).at[:, 1].set(mlp_gain)
    near = jnp.broadcast_to(near[:, None], (wrows, seq, LANES)).reshape(wrows, seq * LANES)
    qkv_piece = swap(w_q, w_k, w_v, near)
    pair_piece = swap(after(w_gate, qkv_piece), w_up)
    first = gathered(jnp.concatenate([qkv_piece, w_o.reshape(seq * wrows, group)], -1))
    qkv_weight = first[:, : 3 * group]
    gains = first[:, 3 * group : 3 * group + 2].T
    out_weight = first[:, 3 * group + LANES :].reshape(group, width)
    pair_weight = gathered(after(pair_piece, first))
    down_weight = gathered(after(w_down, pair_weight))

    (normed_one,) = norm_call(
        norm_kernel, "norm_one", counts, 0, gains, [after(gather_tokens(own_tokens, seq), pair_piece)], [], [LOW], seq
    )
    order = token_order(seq)
    cosine, sine = rotary_tables(length)
    qkv = jnp.dot(normed_one, qkv_weight, preferred_element_type=F32)
    queries, keys, values, attended, logs = attend_forward(qkv, order, cosine, sine, block)
    sums = reduce_tokens(attended, out_weight, ((1,), (0,)), seq, parts=2)
    middle, own_two = norm_call(
        norm_kernel, "norm_two", counts, 1, gains, [own_tokens], sums, [F32, LOW]
    )
    normed_two = gather_tokens(own_two, seq)
    grad_out = gather_tokens(after(own_grad, normed_two, pair_weight), seq)
    gates = jnp.dot(normed_two, pair_weight, preferred_element_type=F32)
    gate, up = gates[:, :hidden], gates[:, hidden:]
    sigmoid = jax.nn.sigmoid(gate)
    mixed = (gate * sigmoid * up).astype(LOW)
    down_whole = outer(mixed, grad_out)
    down_part = summed(down_whole)
    grad_mixed = jnp.einsum(
        "td,fd->tf", after(grad_out, down_whole), down_weight, preferred_element_type=F32
    )
    grad_gate = (grad_mixed * up * sigmoid * (1.0 + gate * (1.0 - sigmoid))).astype(LOW)
    grad_up = (grad_mixed * gate * sigmoid).astype(LOW)
    grad_pair = jnp.concatenate([grad_gate, grad_up], -1)
    pair_whole = []

    def beside_pair(got, kept):
        pair_whole.append(outer(normed_two, after(grad_pair, *kept)))
        return got

    def after_pair(got, kept):
        return [after(g, pair_whole[0]) for g in got]

    sums = reduce_tokens(grad_pair, pair_weight, ((1,), (1,)), seq, [beside_pair, after_pair])
    pair_part = summed(after(pair_whole[0], down_part))
    grad_middle, own_proj = norm_call(
        norm_back_kernel, "norm_two_back", counts, 1, gains, [middle, own_grad], sums, [F32, LOW]
    )
    grad_proj = gather_tokens(own_proj, seq)

    out_whole = outer(attended, grad_proj)
    marks = []

    def hold(got, kept):
        marks.extend(kept)
        return [after(g, grad_proj) for g in got]

    def ahead(got, kept):
        marks.extend(got)
        return got

    down = reduce_tokens(after(mixed, own_proj), down_weight, ((1,), (0,)), seq, [hold, ahead])
    down_sum = jnp.concatenate([down[0] + down[1].astype(F32), down[2] + down[3].astype(F32)], 0)
    layer_out = (middle + down_sum).astype(LOW)[None]
    grad_heads = jnp.einsum(
        "to,io->ti", after(grad_proj, marks[0]), out_weight, preferred_element_type=F32
    ).astype(LOW)
    grad_qkv = jnp.concatenate(
        attend_backward(queries, keys, values, attended, grad_heads, logs, order, cosine, sine, block), -1
    )
    qkv_whole = outer(normed_one, after(grad_qkv, *marks[1:]))
    sums = reduce_tokens(after(grad_qkv, qkv_whole), qkv_weight, ((1,), (1,)), seq)
    (grad_inputs,) = norm_call(
        norm_back_kernel, "norm_one_back", counts, 0, gains, [own_tokens, grad_middle], sums, [LOW]
    )
    last_whole = jnp.concatenate([qkv_whole, out_whole.reshape(width, group)], -1)
    last_part = summed(after(last_whole, pair_part))
    qkv_part, out_part = last_part[:, : 3 * group], last_part[:, 3 * group :].reshape(wrows, width)

    def finish(piece, weight):
        piece = piece.reshape(wrows, -1).astype(F32)
        return piece, jnp.sum(piece * weight.astype(F32), axis=-1)

    pair_near = swap_back(pair_part)
    grad_gate_w, gate_gain = finish(pair_near[:, :, :hidden], w_gate)
    grad_up_w, up_gain = finish(pair_near[:, :, hidden:], w_up)
    qkv_near = swap_back(qkv_part)
    grad_q_w, q_gain = finish(qkv_near[:, :, :group], w_q)
    grad_k_w, k_gain = finish(qkv_near[:, :, group : 2 * group], w_k)
    grad_v_w, v_gain = finish(qkv_near[:, :, 2 * group :], w_v)
    return (
        layer_out,
        grad_inputs[None],
        (q_gain + k_gain + v_gain) / attn_gain.astype(F32),
        (gate_gain + up_gain) / mlp_gain.astype(F32),
        grad_q_w,
        grad_k_w,
        grad_v_w,
        out_part.astype(F32),
        grad_gate_w,
        grad_up_w,
        down_part.astype(F32),
    )


def solution(mesh):
    tokens = P("fsdp", "seq", None)
    vector = P(("seq", "fsdp"))
    matrix = P(("seq", "fsdp"), None)
    return jax.shard_map(
        functools.partial(per_device, dict(mesh.shape)),
        mesh=mesh,
        in_specs=(tokens, tokens, vector, vector) + (matrix,) * 7,
        out_specs=(tokens, tokens, vector, vector) + (matrix,) * 7,
        check_vma=False,
    )
```

time: 1070 us -> 703 us (0.66)
  waiting for transfers between devices: 459 us -> 295 us
  matrix products: 241 us -> 125 us
  local copies, waits for them, and re-layouts: 156 us -> 85.6 us
  Pallas kernels: 0 us -> 51.5 us
  other arithmetic: 91.4 us -> 45.1 us
  starting transfers between devices: 109 us -> 76.4 us
  between operations: 3.5 us -> 16 us
    ppermute x120 -> x77, waiting for transfers between devices: 449 us -> 183 us  [flip(): return lax.ppermute(values, axis, [(i, i ^ mask) for i in range(count)])]
    dot_general x50 -> x14, matrix products: 198 us -> 90.9 us  [the longest x10 43.8 us: part(): lax.dot_general(rows, weight, (dims, ((), ())), preferred_element_type=F32)]
    all_gather x0 -> x3, waiting for transfers between devices: none -> 61.3 us  [gathered(): return lax.all_gather(piece, 'fsdp', axis=0, tiled=True)]
    pallas_call x0 -> x6, Pallas kernels: none -> 51.5 us  [the longest x1 23.6 us: attend_backward(): pl.pallas_call(functools.partial(attend_back_kernel, block), grid_spec=pl...]
    reduce_scatter x0 -> x3, waiting for transfers between devices: none -> 29 us  [summed(): return lax.psum_scatter(whole, 'fsdp', scatter_dimension=0, tiled=True)]
    ppermute x120 -> x77, starting transfers between devices: 83.9 us -> 58.8 us  [flip(): return lax.ppermute(values, axis, [(i, i ^ mask) for i in range(count)])]
    dynamic_update_slice x19 -> x0, local copies, waits for them, and re-layouts: 23.9 us -> none  [gather_rows(): whole = lax.dynamic_update_slice(whole, p[:, None], (0, me ^ j, 0, 0))]
    convert_element_type x19 -> x4, other arithmetic: 27.2 us -> 4.56 us  [the longest x1 1.99 us: per_device(): mixed = (gate * sigmoid * up).astype(LOW)]
  transfers between devices with their start and end apart: 126 -> 87, of which waited for: 48 -> 39; matrix products, arithmetic and copies ran while one was open for 44% -> 32% of each run, Pallas kernels for 0% -> 7%
where the time goes in v2:
time: 703 us; the launch traced here: 694 us
  waiting for transfers between devices  295 us (42%)
  matrix products  125 us (18%)
  local copies, waits for them, and re-layouts  85.6 us (12%)
  starting transfers between devices  76.4 us (11%)
  Pallas kernels  51.5 us (7%)
  other arithmetic  45.1 us (6%)
  between operations  16 us (2%)
    ppermute x77, waiting for transfers between devices, flip(): return lax.ppermute(values, axis, [(i, i ^ mask) for i in range(count)])  183 us
    all_gather x3, waiting for transfers between devices, gathered(): return lax.all_gather(piece, 'fsdp', axis=0, tiled=True)  61.3 us
    ppermute x77, starting transfers between devices, flip(): return lax.ppermute(values, axis, [(i, i ^ mask) for i in range(count)])  58.8 us
    unnamed x172, local copies, waits for them, and re-layouts  57 us
    dot_general x10, matrix products, part(): lax.dot_general(rows, weight, (dims, ((), ())), preferred_element_type=F32)  43.8 us
    dot_general x4, matrix products, outer(): jnp.einsum('ti,to->io', left, right, preferred_element_type=F32).astype(LOW)  33.9 us
    reduce_scatter x3, waiting for transfers between devices, summed(): return lax.psum_scatter(whole, 'fsdp', scatter_dimension=0, tiled=True)  29 us
    pallas_call x1, Pallas kernels, attend_backward(): pl.pallas_call(functools.partial(attend_back_kernel, block), grid_spec=pl...  23.6 us
  transfers between devices with their start and end apart: 87, of which 39 were waited for; matrix products, arithmetic and copies ran while one was open for 32% of the time, Pallas kernels for 7%

profile of v2, /device:TPU:0, one launch (start us, length us, event | category | flops | bytes accessed | tf_op | source)
XLA Modules:
  0.0 694.4 jit_solution(14021237372441443946)
XLA Ops:
  21.0 13.7 %all-to-all-done = bf16[64,8,896]{2,0,1:T(8,128)(2,1)S(1)} async-done(((bf16[64,8,896]{2,0,1:T(8,128)(2,1)}), bf16[64,8,896]{2,0,1:T(8,128)(2,1)S(1)}, u32[]{:S(2)}, u32[]{:S(2)}) %all-to-all-start) | async-done | bytes 917536 | tf_op jit(solution)/shard_map/all_to_all | solution.py:376
  50.8 8.7 %collective-permute-done = bf16[96,2048]{1,0:T(8,128)(2,1)} collective-permute-done((bf16[96,2048]{1,0:T(8,128)(2,1)}, bf16[96,2048]{1,0:T(8,128)(2,1)}, u32[]{:S(2)}, u32[]{:S(2)}) %collective-permute-start) | collective-permute-done | bytes 393248 | tf_op jit(solution)/shard_map/ppermute | solution.py:287
  78.8 22.9 %collective-permute-done.5 = bf16[96,2048]{1,0:T(8,128)(2,1)S(1)} collective-permute-done((bf16[96,2048]{1,0:T(8,128)(2,1)}, bf16[96,2048]{1,0:T(8,128)(2,1)S(1)}, u32[]{:S(2)}, u32[]{:S(2)}) %collective-permute-start.5) | collective-permute-done | bytes 393248 | tf_op jit(solution)/shard_map/ppermute | solution.py:287
  102.6 24.7 %all-gather.4.cloned.1.call-done = bf16[2048,1152]{0,1:T(8,128)(2,1)} async-done(((bf16[512,1152]{0,1:T(8,128)(2,1)}), bf16[2048,1152]{0,1:T(8,128)(2,1)}) %all-gather.4.cloned.1.call-update) | async-done | bytes 4718608 | tf_op jit(solution)/shard_map/all_gather | solution.py:384
  153.1 10.9 %fusion.8.q.k.v = f32[1536,768]{1,0:T(8,128)} fusion(bf16[1536,2048]{1,0:T(8,128)(2,1)S(1)} %norm_one.1, bf16[2048,1152]{0,1:T(8,128)(2,1)} %all-gather.4.cloned.1.call-done), kind=kOutput, calls=%fused_computation.31 | convolution fusion | flops 4831838208 | bytes 14155776 | tf_op jit(solution)/shard_map/dot_general | solution.py:408
  164.0 17.1 %attend_forward.1 = (bf16[1536,256]{1,0:T(8,128)(2,1)S(1)}, bf16[1536,256]{1,0:T(8,128)(2,1)S(1)}, bf16[1536,256]{1,0:T(8,128)(2,1)S(1)}, bf16[1536,256]{1,0:T(8,128)(2,1)S(1)}, f32[2,2,1536]{2,1,0:T(2,128)S(1)}) custom-call(s32[16]{0:T(128)S(1)} %stack.67.order, f32[1536,768]{1,0:T(8,128)} %fusion.8.q.k.v, f32[1536,768]{1,0:T(8,128)} %fusion.8.q.k.v, ...), custom_call_target="tpu_custom_call" | custom-call | tf_op jit(solution)/shard_map/attend_forward/pallas_call | solution.py:115
  189.9 16.1 %collective-permute-done.15 = bf16[192,2048]{1,0:T(8,128)(2,1)S(1)} collective-permute-done((bf16[192,2048]{1,0:T(8,128)(2,1)S(1)}, bf16[192,2048]{1,0:T(8,128)(2,1)S(1)}, u32[]{:S(2)}, u32[]{:S(2)}) %collective-permute-start.15) | collective-permute-done | bytes 786464 | tf_op jit(solution)/shard_map/ppermute | solution.py:287
  263.6 13.3 %all-gather.6.cloned.1.call-done = bf16[2048,2048]{1,0:T(8,128)(2,1)} async-done(((bf16[512,2048]{1,0:T(8,128)(2,1)}), bf16[2048,2048]{1,0:T(8,128)(2,1)}) %all-gather.6.cloned.1.call-update) | async-done | bytes 8388624 | tf_op jit(solution)/shard_map/all_gather | solution.py:384
  282.2 17.5 %fusion.43 = f32[1536,2048]{1,0:T(8,128)S(1)} fusion(bf16[1536,2048]{1,0:T(8,128)(2,1)} %constant_dynamic-update-slice_fusion.16, bf16[2048,2048]{1,0:T(8,128)(2,1)} %all-gather.6.cloned.1.call-done), kind=kOutput, calls=%fused_computation.178 | convolution fusion | flops 12884901888 | bytes 27262976 | tf_op jit(solution)/shard_map/dot_general | solution.py:416
  329.4 8.4 %convolution_convert_fusion.1 = bf16[1024,2048]{1,0:T(8,128)(2,1)} fusion(bf16[1536,1024]{1,0:T(8,128)(2,1)S(1)} %multiply_convert_fusion.2, bf16[1536,2048]{1,0:T(8,128)(2,1)S(1)} %constant_dynamic-update-slice_fusion.32), kind=kOutput, calls=%fused_computation.14 | convolution fusion | flops 6444548096 | bytes 13631488 | tf_op jit(solution)/shard_map/ti,to->io/dot_general | solution.py:390
  337.8 23.4 %all-gather.8.cloned.1.call-done = bf16[1024,2048]{1,0:T(8,128)(2,1)} async-done(((bf16[256,2048]{1,0:T(8,128)(2,1)}), bf16[1024,2048]{1,0:T(8,128)(2,1)}) %all-gather.8.cloned.1.call-update) | async-done | bytes 4194320 | tf_op jit(solution)/shard_map/all_gather | solution.py:384
  361.2 15.8 %multiply_convert_fusion = (bf16[1536,1024]{1,0:T(8,128)(2,1)S(1)}, bf16[1536,1024]{1,0:T(8,128)(2,1)S(1)}) fusion(f32[1536,2048]{1,0:T(8,128)} %copy-done.20, bf16[1536,2048]{1,0:T(8,128)(2,1)} %copy-done.43, bf16[1024,2048]{1,0:T(8,128)(2,1)} %all-gather.8.cloned.1.call-done), kind=kOutput, calls=%fused_computation.9 | convolution fusion | flops 6462898176 | bytes 29360128 | tf_op jit(solution)/shard_map/td,fd->tf/dot_general | solution.py:422
  377.1 11.4 %convolution_convert_fusion.2 = bf16[768,2048]{1,0:T(8,128)(2,1)} fusion(bf16[2048,2048]{1,0:T(8,128)(2,1)} %all-gather.6.cloned.1.call-done, bf16[1536,1024]{1,0:T(8,128)(2,1)S(1)} %get-tuple-element.96, bf16[1536,1024]{1,0:T(8,128)(2,1)S(1)} %get-tuple-element.95), kind=kOutput, calls=%fused_computation.15 | convolution fusion | flops 6450315264 | bytes 17825792 | tf_op jit(solution)/shard_map/dot_general | solution.py:334
  394.5 13.3 %fusion.35 = (bf16[768,2048]{1,0:T(8,128)(2,1)}, f32[768,2048]{1,0:T(8,128)}) fusion(bf16[768,2048]{1,0:T(8,128)(2,1)} %collective-permute-done.48, bf16[2048,2048]{1,0:T(8,128)(2,1)} %all-gather.6.cloned.1.call-done, bf16[1536,1024]{1,0:T(8,128)(2,1)} %copy-done.29, bf16[1536,1024]{1,0:T(8,128)(2,1)S(1)} %get-tuple-element.95), kind=kOutput, calls=%fused_computation.170 | convolution fusion | flops 6453460992 | bytes 27262976 | tf_op jit(solution)/shard_map/dot_general | solution.py:334
  407.8 18.0 %convolution_convert_fusion = bf16[2048,2048]{1,0:T(8,128)(2,1)} fusion(bf16[1536,2048]{1,0:T(8,128)(2,1)} %constant_dynamic-update-slice_fusion.16, bf16[1536,2048]{1,0:T(8,128)(2,1)S(1)} %pad_maximum_fusion), kind=kOutput, calls=%fused_computation.5 | convolution fusion | flops 12889096192 | bytes 20971520 | tf_op jit(solution)/shard_map/ti,to->io/dot_general | solution.py:390
  425.8 12.9 %reduce-scatter.4.cloned.1.call-done = bf16[256,2048]{1,0:T(8,128)(2,1)} async-done(((bf16[1024,2048]{1,0:T(8,128)(2,1)}), bf16[256,2048]{1,0:T(8,128)(2,1)}) %reduce-scatter.4.cloned.1.call-update) | async-done | bytes 1048592 | tf_op jit(solution)/shard_map/reduce_scatter | solution.py:387
  443.3 16.4 %collective-permute-done.51 = bf16[192,2048]{1,0:T(8,128)(2,1)S(1)} collective-permute-done((bf16[192,2048]{1,0:T(8,128)(2,1)S(1)}, bf16[192,2048]{1,0:T(8,128)(2,1)S(1)}, u32[]{:S(2)}, u32[]{:S(2)}) %collective-permute-start.51) | collective-permute-done | bytes 786464 | tf_op jit(solution)/shard_map/ppermute | solution.py:287
  486.4 8.5 %collective-permute-done.54 = bf16[96,2048]{1,0:T(8,128)(2,1)S(1)} collective-permute-done((bf16[96,2048]{1,0:T(8,128)(2,1)S(1)}, bf16[96,2048]{1,0:T(8,128)(2,1)S(1)}, u32[]{:S(2)}, u32[]{:S(2)}) %collective-permute-start.54) | collective-permute-done | bytes 393248 | tf_op jit(solution)/shard_map/ppermute | solution.py:287
  497.2 8.5 %collective-permute-done.56 = bf16[96,2048]{1,0:T(8,128)(2,1)S(1)} collective-permute-done((bf16[96,2048]{1,0:T(8,128)(2,1)S(1)}, bf16[96,2048]{1,0:T(8,128)(2,1)S(1)}, u32[]{:S(2)}, u32[]{:S(2)}) %collective-permute-start.56) | collective-permute-done | bytes 393248 | tf_op jit(solution)/shard_map/ppermute | solution.py:287
  507.3 8.4 %collective-permute-done.59 = bf16[96,2048]{1,0:T(8,128)(2,1)S(1)} collective-permute-done((bf16[96,2048]{1,0:T(8,128)(2,1)S(1)}, bf16[96,2048]{1,0:T(8,128)(2,1)S(1)}, u32[]{:S(2)}, u32[]{:S(2)}) %collective-permute-start.59) | collective-permute-done | bytes 393248 | tf_op jit(solution)/shard_map/ppermute | solution.py:287
  541.7 23.6 %attend_backward.1 = (bf16[1536,256]{1,0:T(8,128)(2,1)S(1)}, bf16[1536,256]{1,0:T(8,128)(2,1)S(1)}, bf16[1536,256]{1,0:T(8,128)(2,1)S(1)}) custom-call(s32[16]{0:T(128)S(1)} %copy-done.17, bf16[1536,256]{1,0:T(8,128)(2,1)S(1)} %copy-done.12, bf16[1536,256]{1,0:T(8,128)(2,1)S(1)} %copy-done.14, bf16[1536,256]{1,0:T(8,128)(2,1)} %copy-done.15, ...), custom_call_target="tpu_custom_call" | custom-call | tf_op jit(solution)/shard_map/attend_backward/pallas_call | solution.py:193
  573.5 12.5 %reduce-scatter.6.cloned.1.call-done = bf16[512,2048]{1,0:T(8,128)(2,1)} async-done(((bf16[2048,2048]{1,0:T(8,128)(2,1)}), bf16[512,2048]{1,0:T(8,128)(2,1)}) %reduce-scatter.6.cloned.1.call-update) | async-done | bytes 2097168 | tf_op jit(solution)/shard_map/reduce_scatter | solution.py:387
  614.2 13.8 %collective-permute-done.75 = bf16[192,2048]{1,0:T(8,128)(2,1)} collective-permute-done((bf16[192,2048]{1,0:T(8,128)(2,1)}, bf16[192,2048]{1,0:T(8,128)(2,1)}, u32[]{:S(2)}, u32[]{:S(2)}) %collective-permute-start.75) | collective-permute-done | bytes 786464 | tf_op jit(solution)/shard_map/ppermute | solution.py:287
  640.2 17.5 %collective-permute-done.74.refs_1_ = bf16[96,2048]{1,0:T(8,128)(2,1)S(1)} collective-permute-done((bf16[96,2048]{1,0:T(8,128)(2,1)S(1)}, bf16[96,2048]{1,0:T(8,128)(2,1)S(1)}, u32[]{:S(2)}, u32[]{:S(2)}) %collective-permute-start.74) | collective-permute-done | bytes 393248 | tf_op jit(solution)/shard_map/ppermute | solution.py:287
  (443 shorter events, 321.1 us)
Async XLA Ops:
  20.7 106.6 %all-gather.4.cloned.1.call-start = ((), (), s32[]{:S(2)}) async-start(), calls=%async_computation.7 | async-start | bytes 5898240 | tf_op jit(solution)/shard_map/all_gather | solution.py:384
  39.2 94.3 %collective-permute-start.10 = (bf16[96,2048]{1,0:T(8,128)(2,1)}, bf16[96,2048]{1,0:T(8,128)(2,1)}, u32[]{:S(2)}, u32[]{:S(2)}) collective-permute-start(bf16[96,2048]{1,0:T(8,128)(2,1)} %get-tuple-element.123), channel_id=1, source_target_pairs={{0,4},{4,0},{8,12},{12,8},{16,20},{20,16},{24,28},{28,24},{1,5},{5... | collective-permute-start | bytes 1179656 | tf_op jit(solution)/shard_map/ppermute | solution.py:287
  39.2 32.6 %collective-permute-start.4 = (bf16[96,2048]{1,0:T(8,128)(2,1)}, bf16[96,2048]{1,0:T(8,128)(2,1)S(1)}, u32[]{:S(2)}, u32[]{:S(2)}) collective-permute-start(bf16[96,2048]{1,0:T(8,128)(2,1)} %get-tuple-element.123), channel_id=1, source_target_pairs={{0,16},{4,20},{8,24},{12,28},{16,0},{20,4},{24,8},{28,12},{1,17},{... | collective-permute-start | bytes 1179656 | tf_op jit(solution)/shard_map/ppermute | solution.py:287
  39.8 29.7 %collective-permute-start.3 = (bf16[96,2048]{1,0:T(8,128)(2,1)}, bf16[96,2048]{1,0:T(8,128)(2,1)}, u32[]{:S(2)}, u32[]{:S(2)}) collective-permute-start(bf16[96,2048]{1,0:T(8,128)(2,1)} %get-tuple-element.123), channel_id=1, source_target_pairs={{0,8},{4,12},{8,0},{12,4},{16,24},{20,28},{24,16},{28,20},{1,9},{5... | collective-permute-start | bytes 1179656 | tf_op jit(solution)/shard_map/ppermute | solution.py:287
  40.4 29.4 %collective-permute-start.1 = (bf16[96,2048]{1,0:T(8,128)(2,1)}, bf16[96,2048]{1,0:T(8,128)(2,1)}, u32[]{:S(2)}, u32[]{:S(2)}) collective-permute-start(bf16[96,2048]{1,0:T(8,128)(2,1)} %get-tuple-element.124), channel_id=1, source_target_pairs={{0,8},{4,12},{8,0},{12,4},{16,24},{20,28},{24,16},{28,20},{1,9},{5... | collective-permute-start | bytes 1179656 | tf_op jit(solution)/shard_map/ppermute | solution.py:287
  63.3 39.2 %all-to-all-start.1 = ((bf16[64,8,2048]{2,0,1:T(8,128)(2,1)}), bf16[64,8,2048]{2,0,1:T(8,128)(2,1)}, u32[]{:S(2)}, u32[]{:S(2)}) async-start(bf16[64,8,2048]{2,0,1:T(8,128)(2,1)} %copy.97), calls=%async_computation.1 | async-start | bytes 4194304 | tf_op jit(solution)/shard_map/all_to_all | solution.py:376
  67.7 209.2 %all-gather.6.cloned.1.call-start = ((), (), s32[]{:S(2)}) async-start(), calls=%async_computation.8 | async-start | bytes 10485760 | tf_op jit(solution)/shard_map/all_gather | solution.py:384
  69.5 58.3 %collective-permute-start.6 = (bf16[96,2048]{1,0:T(8,128)(2,1)}, bf16[96,2048]{1,0:T(8,128)(2,1)}, u32[]{:S(2)}, u32[]{:S(2)}) collective-permute-start(bf16[96,2048]{1,0:T(8,128)(2,1)} %get-tuple-element.124), channel_id=1, source_target_pairs={{0,4},{4,0},{8,12},{12,8},{16,20},{20,16},{24,28},{28,24},{1,5},{5... | collective-permute-start | bytes 1179656 | tf_op jit(solution)/shard_map/ppermute | solution.py:287
  69.9 65.5 %collective-permute-start.11 = (bf16[96,2048]{1,0:T(8,128)(2,1)}, bf16[96,2048]{1,0:T(8,128)(2,1)}, u32[]{:S(2)}, u32[]{:S(2)}) collective-permute-start(bf16[96,2048]{1,0:T(8,128)(2,1)} %collective-permute-done.3), channel_id=1, source_target_pairs={{0,4},{4,0},{8,12},{12,8},{16,20},{20,16},{24,28},{28,24},{1,5},{5... | collective-permute-start | bytes 1179656 | tf_op jit(solution)/shard_map/ppermute | solution.py:287
  71.8 29.9 %collective-permute-start.5 = (bf16[96,2048]{1,0:T(8,128)(2,1)}, bf16[96,2048]{1,0:T(8,128)(2,1)S(1)}, u32[]{:S(2)}, u32[]{:S(2)}) collective-permute-start(bf16[96,2048]{1,0:T(8,128)(2,1)} %collective-permute-done.3), channel_id=1, source_target_pairs={{0,16},{4,20},{8,24},{12,28},{16,0},{20,4},{24,8},{28,12},{1,17},{... | collective-permute-start | bytes 1179656 | tf_op jit(solution)/shard_map/ppermute | solution.py:287
  73.7 63.5 %collective-permute-start.12 = (bf16[96,2048]{1,0:T(8,128)(2,1)S(1)}, bf16[96,2048]{1,0:T(8,128)(2,1)}, u32[]{:S(2)}, u32[]{:S(2)}) collective-permute-start(bf16[96,2048]{1,0:T(8,128)(2,1)S(1)} %collective-permute-done.4), channel_id=1, source_target_pairs={{0,4},{4,0},{8,12},{12,8},{16,20},{20,16},{24,28},{28,24},{1,5},{5... | collective-permute-start | bytes 1179656 | tf_op jit(solution)/shard_map/ppermute | solution.py:287
  101.7 28.0 %collective-permute-start.7 = (bf16[96,2048]{1,0:T(8,128)(2,1)}, bf16[96,2048]{1,0:T(8,128)(2,1)}, u32[]{:S(2)}, u32[]{:S(2)}) collective-permute-start(bf16[96,2048]{1,0:T(8,128)(2,1)} %collective-permute-done), channel_id=1, source_target_pairs={{0,4},{4,0},{8,12},{12,8},{16,20},{20,16},{24,28},{28,24},{1,5},{5... | collective-permute-start | bytes 1179656 | tf_op jit(solution)/shard_map/ppermute | solution.py:287
  127.3 234.0 %all-gather.8.cloned.1.call-start = ((), (), s32[]{:S(2)}) async-start(), calls=%async_computation.9 | async-start | bytes 5242880 | tf_op jit(solution)/shard_map/all_gather | solution.py:384
  224.8 35.7 %collective-permute-start.30 = (bf16[96,2048]{1,0:T(8,128)(2,1)S(1)}, bf16[96,2048]{1,0:T(8,128)(2,1)S(1)}, u32[]{:S(2)}, u32[]{:S(2)}) collective-permute-start(bf16[96,2048]{1,0:T(8,128)(2,1)S(1)} %get-tuple-element.120), channel_id=1, source_target_pairs={{0,4},{4,0},{8,12},{12,8},{16,20},{20,16},{24,28},{28,24},{1,5},{5... | collective-permute-start | bytes 1179656 | tf_op jit(solution)/shard_map/ppermute | solution.py:287
  278.0 47.5 %collective-permute-start.44 = (bf16[96,2048]{1,0:T(8,128)(2,1)}, bf16[96,2048]{1,0:T(8,128)(2,1)}, u32[]{:S(2)}, u32[]{:S(2)}) collective-permute-start(bf16[96,2048]{1,0:T(8,128)(2,1)} %get-tuple-element.117), channel_id=1, source_target_pairs={{0,4},{4,0},{8,12},{12,8},{16,20},{20,16},{24,28},{28,24},{1,5},{5... | collective-permute-start | bytes 1179656 | tf_op jit(solution)/shard_map/ppermute | solution.py:287
  278.1 32.4 %collective-permute-start.38 = (bf16[96,2048]{1,0:T(8,128)(2,1)}, bf16[96,2048]{1,0:T(8,128)(2,1)}, u32[]{:S(2)}, u32[]{:S(2)}) collective-permute-start(bf16[96,2048]{1,0:T(8,128)(2,1)} %get-tuple-element.117), channel_id=1, source_target_pairs={{0,16},{4,20},{8,24},{12,28},{16,0},{20,4},{24,8},{28,12},{1,17},{... | collective-permute-start | bytes 1179656 | tf_op jit(solution)/shard_map/ppermute | solution.py:287
  279.5 29.3 %collective-permute-start.37 = (bf16[96,2048]{1,0:T(8,128)(2,1)}, bf16[96,2048]{1,0:T(8,128)(2,1)}, u32[]{:S(2)}, u32[]{:S(2)}) collective-permute-start(bf16[96,2048]{1,0:T(8,128)(2,1)} %get-tuple-element.117), channel_id=1, source_target_pairs={{0,8},{4,12},{8,0},{12,4},{16,24},{20,28},{24,16},{28,20},{1,9},{5... | collective-permute-start | bytes 1179656 | tf_op jit(solution)/shard_map/ppermute | solution.py:287
  282.1 156.6 %reduce-scatter.4.cloned.1.call-start = ((), (), s32[]{:S(2)}) async-start(), calls=%async_computation.10 | async-start | bytes 5242880 | tf_op jit(solution)/shard_map/reduce_scatter | solution.py:387
  337.8 248.3 %reduce-scatter.6.cloned.1.call-start = ((), (), s32[]{:S(2)}) async-start(), calls=%async_computation.11 | async-start | bytes 10485760 | tf_op jit(solution)/shard_map/reduce_scatter | solution.py:387
  438.7 227.1 %reduce-scatter.8.cloned.1.call-start = ((), (), s32[]{:S(2)}) async-start(), calls=%async_computation.12 | async-start | bytes 5242880 | tf_op jit(solution)/shard_map/reduce_scatter | solution.py:387
  474.9 44.4 %collective-permute-start.64 = (bf16[96,2048]{1,0:T(8,128)(2,1)S(1)}, bf16[96,2048]{1,0:T(8,128)(2,1)S(1)}, u32[]{:S(2)}, u32[]{:S(2)}) collective-permute-start(bf16[96,2048]{1,0:T(8,128)(2,1)S(1)} %get-tuple-element.114), channel_id=1, source_target_pairs={{0,4},{4,0},{8,12},{12,8},{16,20},{20,16},{24,28},{28,24},{1,5},{5... | collective-permute-start | bytes 1179656 | tf_op jit(solution)/shard_map/ppermute | solution.py:287
  531.0 34.5 %collective-permute-start.68 = (bf16[192,2048]{1,0:T(8,128)(2,1)}, bf16[192,2048]{1,0:T(8,128)(2,1)}, u32[]{:S(2)}, u32[]{:S(2)}) collective-permute-start(bf16[192,2048]{1,0:T(8,128)(2,1)} %get-tuple-element.105), channel_id=1, source_target_pairs={{0,8},{4,12},{8,0},{12,4},{16,24},{20,28},{24,16},{28,20},{1,9},{5... | collective-permute-start | bytes 2359304 | tf_op jit(solution)/shard_map/ppermute | solution.py:287
  532.5 33.0 %collective-permute-start.70 = (bf16[192,2048]{1,0:T(8,128)(2,1)}, bf16[192,2048]{1,0:T(8,128)(2,1)}, u32[]{:S(2)}, u32[]{:S(2)}) collective-permute-start(bf16[192,2048]{1,0:T(8,128)(2,1)} %get-tuple-element.106), channel_id=1, source_target_pairs={{0,16},{4,20},{8,24},{12,28},{16,0},{20,4},{24,8},{28,12},{1,17},{... | collective-permute-start | bytes 2359304 | tf_op jit(solution)/shard_map/ppermute | solution.py:287
  607.8 51.9 %all-to-all-start.3 = ((bf16[8,64,1,2048]{3,1,2,0:T(8,128)(2,1)}), bf16[8,64,1,2048]{3,1,2,0:T(8,128)(2,1)S(1)}, u32[]{:S(2)}, u32[]{:S(2)}) async-start(bf16[8,64,1,2048]{3,1,2,0:T(8,128)(2,1)} %bitcast.131), calls=%async_computation.6 | async-start | bytes 4194304 | tf_op jit(solution)/shard_map/all_to_all | solution.py:379
  (118 other events, 1930.5 us)
Sparse Core Ops, SparseCore 0:
  38.4 88.8 all-gather.3
  128.8 148.0 all-gather.5
  282.3 78.9 all-gather.7
  363.4 75.2 reduce-scatter.3
  441.0 144.9 reduce-scatter.5
  588.3 77.4 reduce-scatter.7

commit v3 on v2

--- a/solution.py
+++ b/solution.py
@@ -11,6 +11,7 @@
 HD = 64
 PAIR = 2 * HD
 LANES = 128
+GAIN_ROWS = 16
 TILE = 256
 NT = (((1,), (1,)), ((), ()))
 
@@ -393,12 +394,20 @@
     near = jnp.broadcast_to(near[:, None], (wrows, seq, LANES)).reshape(wrows, seq * LANES)
     qkv_piece = swap(w_q, w_k, w_v, near)
     pair_piece = swap(after(w_gate, qkv_piece), w_up)
-    first = gathered(jnp.concatenate([qkv_piece, w_o.reshape(seq * wrows, group)], -1))
-    qkv_weight = first[:, : 3 * group]
-    gains = first[:, 3 * group : 3 * group + 2].T
-    out_weight = first[:, 3 * group + LANES :].reshape(group, width)
-    pair_weight = gathered(after(pair_piece, first))
-    down_weight = gathered(after(w_down, pair_weight))
+    down_first = gathered(w_down[:, : width // 2])
+    tall = seq * wrows
+    wide = 4 * group
+    piece = jnp.concatenate([qkv_piece[:, : 3 * group], w_o.reshape(tall, group)], -1)
+    own_gains = qkv_piece[:, 3 * group : 3 * group + 2].T
+    extra = GAIN_ROWS * -(-2 * tall // (GAIN_ROWS * wide))
+    own_gains = jnp.pad(own_gains.reshape(-1), (0, extra * wide - 2 * tall)).reshape(extra, wide)
+    first = gathered(after(jnp.concatenate([piece, own_gains], 0), down_first)).reshape(fsdp, tall + extra, wide)
+    qkv_weight = first[:, :tall, : 3 * group].reshape(width, 3 * group)
+    out_weight = first[:, :tall, 3 * group :].reshape(group, width)
+    gains = first[:, tall:].reshape(fsdp, -1)[:, : 2 * tall].reshape(fsdp, 2, tall).swapaxes(0, 1).reshape(2, width)
+    grad_out = gather_tokens(after(own_grad, pair_piece), seq)
+    pair_weight = gathered(after(pair_piece, first, grad_out))
+    down_last = gathered(after(w_down[:, width // 2 :], pair_weight))
 
     (normed_one,) = norm_call(
         norm_kernel, "norm_one", counts, 0, gains, [after(gather_tokens(own_tokens, seq), pair_piece)], [], [LOW], seq
@@ -412,16 +421,17 @@
         norm_kernel, "norm_two", counts, 1, gains, [own_tokens], sums, [F32, LOW]
     )
     normed_two = gather_tokens(own_two, seq)
-    grad_out = gather_tokens(after(own_grad, normed_two, pair_weight), seq)
     gates = jnp.dot(normed_two, pair_weight, preferred_element_type=F32)
     gate, up = gates[:, :hidden], gates[:, hidden:]
     sigmoid = jax.nn.sigmoid(gate)
     mixed = (gate * sigmoid * up).astype(LOW)
     down_whole = outer(mixed, grad_out)
-    down_part = summed(down_whole)
+    down_part = summed(after(down_whole, down_last))
+    cot = after(grad_out, down_whole)
     grad_mixed = jnp.einsum(
-        "td,fd->tf", after(grad_out, down_whole), down_weight, preferred_element_type=F32
-    )
+        "td,fd->tf", cot[:, : width // 2], down_first, preferred_element_type=F32
+    ) + jnp.einsum("td,fd->tf", cot[:, width // 2 :], down_last, preferred_element_type=F32)
+    down_weight = jnp.concatenate([down_first, down_last], -1)
     grad_gate = (grad_mixed * up * sigmoid * (1.0 + gate * (1.0 - sigmoid))).astype(LOW)
     grad_up = (grad_mixed * gate * sigmoid).astype(LOW)
     grad_pair = jnp.concatenate([grad_gate, grad_up], -1)

time: 703 us -> 680 us (0.967)
  waiting for transfers between devices: 295 us -> 258 us
  other arithmetic: 45.1 us -> 53.4 us
    all_gather x3 -> x4, waiting for transfers between devices: 61.3 us -> 32.8 us  [gathered(): return lax.all_gather(piece, 'fsdp', axis=0, tiled=True)]
    all_to_all x2, waiting for transfers between devices: 13.7 us -> 3.45 us  [swap(): lax.all_to_all(piece, 'seq', split_axis=1, concat_axis=0, tiled=True)]
    reduce_scatter x3, waiting for transfers between devices: 29 us -> 37.1 us  [summed(): return lax.psum_scatter(whole, 'fsdp', scatter_dimension=0, tiled=True)]
    dot_general x1 -> x2, matrix products: 15.8 us -> 20.4 us  [the longest x1 11.8 us: per_device(): jnp.einsum('td,fd->tf', cot[:, width // 2:], down_last, preferred_element...]
    unnamed x172 -> x177, local copies, waits for them, and re-layouts: 57 us -> 53 us
  transfers between devices with their start and end apart: 87 -> 88, of which waited for: 39 -> 38; matrix products, arithmetic and copies ran while one was open for 32% -> 39% of each run, Pallas kernels for 7% -> 8%
where the time goes in v3:
time: 680 us; the launch traced here: 672 us
  waiting for transfers between devices  258 us (38%)
  matrix products  132 us (19%)
  local copies, waits for them, and re-layouts  89.7 us (13%)
  starting transfers between devices  72.1 us (11%)
  other arithmetic  53.4 us (8%)
  Pallas kernels  51.4 us (8%)
  between operations  15.9 us (2%)
    ppermute x77, waiting for transfers between devices, flip(): return lax.ppermute(values, axis, [(i, i ^ mask) for i in range(count)])  177 us
    ppermute x77, starting transfers between devices, flip(): return lax.ppermute(values, axis, [(i, i ^ mask) for i in range(count)])  54.4 us
    unnamed x177, local copies, waits for them, and re-layouts  53 us
    dot_general x10, matrix products, part(): lax.dot_general(rows, weight, (dims, ((), ())), preferred_element_type=F32)  45.8 us
    reduce_scatter x3, waiting for transfers between devices, summed(): return lax.psum_scatter(whole, 'fsdp', scatter_dimension=0, tiled=True)  37.1 us
    dot_general x4, matrix products, outer(): jnp.einsum('ti,to->io', left, right, preferred_element_type=F32).astype(LOW)  36.8 us
    all_gather x4, waiting for transfers between devices, gathered(): return lax.all_gather(piece, 'fsdp', axis=0, tiled=True)  32.8 us
    pallas_call x1, Pallas kernels, attend_backward(): pl.pallas_call(functools.partial(attend_back_kernel, block), grid_spec=pl...  23.6 us
  transfers between devices with their start and end apart: 88, of which 38 were waited for; matrix products, arithmetic and copies ran while one was open for 39% of the time, Pallas kernels for 8%

profile of v3, /device:TPU:0, one launch (start us, length us, event | category | flops | bytes accessed | tf_op | source)
XLA Modules:
  0.0 672.1 jit_solution(16496018366797283110)
XLA Ops:
  49.8 9.1 %all-gather.5.cloned.1.call-done = bf16[1024,1024]{1,0:T(8,128)(2,1)} async-done(((bf16[256,1024]{1,0:T(8,128)(2,1)}), bf16[1024,1024]{1,0:T(8,128)(2,1)}) %all-gather.5.cloned.1.call-update) | async-done | bytes 2097168 | tf_op jit(solution)/shard_map/all_gather | solution.py:385
  70.4 13.7 %collective-permute-done.2 = bf16[96,2048]{1,0:T(8,128)(2,1)S(1)} collective-permute-done((bf16[96,2048]{1,0:T(8,128)(2,1)}, bf16[96,2048]{1,0:T(8,128)(2,1)S(1)}, u32[]{:S(2)}, u32[]{:S(2)}) %collective-permute-start.2) | collective-permute-done | bytes 393248 | tf_op jit(solution)/shard_map/ppermute | solution.py:288
  103.1 7.1 %collective-permute-done.37 = bf16[96,2048]{1,0:T(8,128)(2,1)S(1)} collective-permute-done((bf16[96,2048]{1,0:T(8,128)(2,1)S(1)}, bf16[96,2048]{1,0:T(8,128)(2,1)S(1)}, u32[]{:S(2)}, u32[]{:S(2)}) %collective-permute-start.37) | collective-permute-done | bytes 393248 | tf_op jit(solution)/shard_map/ppermute | solution.py:288
  174.4 17.0 %attend_forward.1 = (bf16[1536,256]{1,0:T(8,128)(2,1)S(1)}, bf16[1536,256]{1,0:T(8,128)(2,1)S(1)}, bf16[1536,256]{1,0:T(8,128)(2,1)S(1)}, bf16[1536,256]{1,0:T(8,128)(2,1)S(1)}, f32[2,2,1536]{2,1,0:T(2,128)S(1)}) custom-call(s32[16]{0:T(128)S(1)} %stack.67.order, f32[1536,768]{1,0:T(8,128)} %fusion.43.q.k.v, f32[1536,768]{1,0:T(8,128)} %fusion.43.q.k.v, ...), custom_call_target="tpu_custom_call" | custom-call | tf_op jit(solution)/shard_map/attend_forward/pallas_call | solution.py:116
  200.1 15.8 %collective-permute-done.18 = bf16[192,2048]{1,0:T(8,128)(2,1)S(1)} collective-permute-done((bf16[192,2048]{1,0:T(8,128)(2,1)S(1)}, bf16[192,2048]{1,0:T(8,128)(2,1)S(1)}, u32[]{:S(2)}, u32[]{:S(2)}) %collective-permute-start.18) | collective-permute-done | bytes 786464 | tf_op jit(solution)/shard_map/ppermute | solution.py:288
  235.0 8.0 %collective-permute-done.20 = bf16[96,2048]{1,0:T(8,128)(2,1)S(1)} collective-permute-done((bf16[96,2048]{1,0:T(8,128)(2,1)S(1)}, bf16[96,2048]{1,0:T(8,128)(2,1)S(1)}, u32[]{:S(2)}, u32[]{:S(2)}) %collective-permute-start.20) | collective-permute-done | bytes 393248 | tf_op jit(solution)/shard_map/ppermute | solution.py:288
  275.3 17.1 %all-gather.9.cloned.1.call-done = bf16[2048,2048]{1,0:T(8,128)(2,1)} async-done(((bf16[512,2048]{1,0:T(8,128)(2,1)}), bf16[2048,2048]{1,0:T(8,128)(2,1)}) %all-gather.9.cloned.1.call-update) | async-done | bytes 8388624 | tf_op jit(solution)/shard_map/all_gather | solution.py:385
  292.5 19.2 %fusion.44 = f32[1536,2048]{1,0:T(8,128)} fusion(bf16[1536,2048]{1,0:T(8,128)(2,1)} %constant_dynamic-update-slice_fusion.16, bf16[2048,2048]{1,0:T(8,128)(2,1)} %all-gather.9.cloned.1.call-done), kind=kOutput, calls=%fused_computation.183 | convolution fusion | flops 12884901888 | bytes 27262976 | tf_op jit(solution)/shard_map/dot_general | solution.py:424
  319.1 11.3 %convolution_convert_fusion.1 = bf16[1024,2048]{1,0:T(8,128)(2,1)} fusion(bf16[1536,1024]{1,0:T(8,128)(2,1)S(1)} %multiply_convert_fusion.2, bf16[1536,2048]{1,0:T(8,128)(2,1)} %constant_dynamic-update-slice_fusion.32), kind=kOutput, calls=%fused_computation.15 | convolution fusion | flops 6444548096 | bytes 13631488 | tf_op jit(solution)/shard_map/ti,to->io/dot_general | solution.py:391
  330.3 8.6 %fusion.6 = f32[1536,1024]{1,0:T(8,128)} fusion(bf16[1024,1024]{1,0:T(8,128)(2,1)} %all-gather.5.cloned.1.call-done, bf16[1536,2048]{1,0:T(8,128)(2,1)} %constant_dynamic-update-slice_fusion.32), kind=kOutput, calls=%fused_computation.24 | convolution fusion | flops 3221225472 | bytes 11534336 | tf_op jit(solution)/shard_map/td,fd->tf/dot_general | solution.py:431
  339.0 11.8 %multiply_convert_fusion = (bf16[1536,1024]{1,0:T(8,128)(2,1)S(1)}, bf16[1536,1024]{1,0:T(8,128)(2,1)S(1)}) fusion(f32[1536,2048]{1,0:T(8,128)} %fusion.44, f32[1536,1024]{1,0:T(8,128)} %fusion.6, bf16[1024,1024]{1,0:T(8,128)(2,1)} %all-gather.11.cloned.1.call-done, bf16[1536,2048]{1,0:T(8,128)(2,1)} %constant_dynamic-update-slice_fusion.32), kind=kOutput, calls=%fused_computation.9 | convolution fusion | flops 3243245568 | bytes 30408704 | tf_op jit(solution)/shard_map/td,fd->tf/dot_general | solution.py:433
  350.9 11.5 %convolution_convert_fusion.2 = bf16[768,2048]{1,0:T(8,128)(2,1)} fusion(bf16[2048,2048]{1,0:T(8,128)(2,1)} %all-gather.9.cloned.1.call-done, bf16[1536,1024]{1,0:T(8,128)(2,1)S(1)} %get-tuple-element.100, bf16[1536,1024]{1,0:T(8,128)(2,1)S(1)} %get-tuple-element.99), kind=kOutput, calls=%fused_computation.16 | convolution fusion | flops 6450315264 | bytes 17825792 | tf_op jit(solution)/shard_map/dot_general | solution.py:335
  368.3 13.3 %fusion.34 = (bf16[768,2048]{1,0:T(8,128)(2,1)}, f32[768,2048]{1,0:T(8,128)}) fusion(bf16[768,2048]{1,0:T(8,128)(2,1)} %collective-permute-done.48, bf16[2048,2048]{1,0:T(8,128)(2,1)} %all-gather.9.cloned.1.call-done, bf16[1536,1024]{1,0:T(8,128)(2,1)} %copy-done.32, bf16[1536,1024]{1,0:T(8,128)(2,1)S(1)} %get-tuple-element.99), kind=kOutput, calls=%fused_computation.173 | convolution fusion | flops 6453460992 | bytes 27262976 | tf_op jit(solution)/shard_map/dot_general | solution.py:335
  381.6 18.0 %convolution_convert_fusion = bf16[2048,2048]{1,0:T(8,128)(2,1)} fusion(bf16[1536,2048]{1,0:T(8,128)(2,1)} %constant_dynamic-update-slice_fusion.16, bf16[1536,2048]{1,0:T(8,128)(2,1)S(1)} %pad_maximum_fusion), kind=kOutput, calls=%fused_computation.5 | convolution fusion | flops 12889096192 | bytes 20971520 | tf_op jit(solution)/shard_map/ti,to->io/dot_general | solution.py:391
  399.6 16.6 %reduce-scatter.4.cloned.1.call-done = bf16[256,2048]{1,0:T(8,128)(2,1)} async-done(((bf16[1024,2048]{1,0:T(8,128)(2,1)}), bf16[256,2048]{1,0:T(8,128)(2,1)}) %reduce-scatter.4.cloned.1.call-update) | async-done | bytes 1048592 | tf_op jit(solution)/shard_map/reduce_scatter | solution.py:388
  421.1 16.4 %collective-permute-done.49 = bf16[192,2048]{1,0:T(8,128)(2,1)S(1)} collective-permute-done((bf16[192,2048]{1,0:T(8,128)(2,1)S(1)}, bf16[192,2048]{1,0:T(8,128)(2,1)S(1)}, u32[]{:S(2)}, u32[]{:S(2)}) %collective-permute-start.49) | collective-permute-done | bytes 786464 | tf_op jit(solution)/shard_map/ppermute | solution.py:288
  472.0 7.6 %collective-permute-done.56 = bf16[96,2048]{1,0:T(8,128)(2,1)S(1)} collective-permute-done((bf16[96,2048]{1,0:T(8,128)(2,1)S(1)}, bf16[96,2048]{1,0:T(8,128)(2,1)S(1)}, u32[]{:S(2)}, u32[]{:S(2)}) %collective-permute-start.56) | collective-permute-done | bytes 393248 | tf_op jit(solution)/shard_map/ppermute | solution.py:288
  481.3 8.7 %collective-permute-done.59 = bf16[96,2048]{1,0:T(8,128)(2,1)S(1)} collective-permute-done((bf16[96,2048]{1,0:T(8,128)(2,1)S(1)}, bf16[96,2048]{1,0:T(8,128)(2,1)S(1)}, u32[]{:S(2)}, u32[]{:S(2)}) %collective-permute-start.59) | collective-permute-done | bytes 393248 | tf_op jit(solution)/shard_map/ppermute | solution.py:288
  514.1 23.6 %attend_backward.1 = (bf16[1536,256]{1,0:T(8,128)(2,1)S(1)}, bf16[1536,256]{1,0:T(8,128)(2,1)S(1)}, bf16[1536,256]{1,0:T(8,128)(2,1)S(1)}) custom-call(s32[16]{0:T(128)S(1)} %copy-done.18, bf16[1536,256]{1,0:T(8,128)(2,1)S(1)} %copy-done.13, bf16[1536,256]{1,0:T(8,128)(2,1)S(1)} %copy-done.15, bf16[1536,256]{1,0:T(8,128)(2,1)} %copy-done.16, ...), custom_call_target="tpu_custom_call" | custom-call | tf_op jit(solution)/shard_map/attend_backward/pallas_call | solution.py:194
  545.9 17.7 %reduce-scatter.6.cloned.1.call-done = bf16[512,2048]{1,0:T(8,128)(2,1)} async-done(((bf16[2048,2048]{1,0:T(8,128)(2,1)}), bf16[512,2048]{1,0:T(8,128)(2,1)}) %reduce-scatter.6.cloned.1.call-update) | async-done | bytes 2097168 | tf_op jit(solution)/shard_map/reduce_scatter | solution.py:388
  592.9 13.2 %collective-permute-done.73 = bf16[192,2048]{1,0:T(8,128)(2,1)} collective-permute-done((bf16[192,2048]{1,0:T(8,128)(2,1)}, bf16[192,2048]{1,0:T(8,128)(2,1)}, u32[]{:S(2)}, u32[]{:S(2)}) %collective-permute-start.73) | collective-permute-done | bytes 786464 | tf_op jit(solution)/shard_map/ppermute | solution.py:288
  610.3 7.1 %collective-permute-start.76 = (bf16[96,2048]{1,0:T(8,128)(2,1)S(1)}, bf16[96,2048]{1,0:T(8,128)(2,1)S(1)}, u32[]{:S(2)}, u32[]{:S(2)}) collective-permute-start(bf16[96,2048]{1,0:T(8,128)(2,1)S(1)} %slice.487), channel_id=1, source_target_pairs={{0,8},{4,12},{8,0},{12,4},{16,24},{20,28},{24,16},{28,20},{1,9},{5... | collective-permute-start | bytes 1179656 | tf_op jit(solution)/shard_map/ppermute | solution.py:288
  618.7 17.4 %collective-permute-done.74.refs_1_ = bf16[96,2048]{1,0:T(8,128)(2,1)S(1)} collective-permute-done((bf16[96,2048]{1,0:T(8,128)(2,1)S(1)}, bf16[96,2048]{1,0:T(8,128)(2,1)S(1)}, u32[]{:S(2)}, u32[]{:S(2)}) %collective-permute-start.74) | collective-permute-done | bytes 393248 | tf_op jit(solution)/shard_map/ppermute | solution.py:288
  654.5 7.8 %all-to-all-done.2 = bf16[8,64,1,768]{3,1,2,0:T(8,128)(2,1)S(1)} async-done(((bf16[8,64,1,768]{3,1,2,0:T(8,128)(2,1)}), bf16[8,64,1,768]{3,1,2,0:T(8,128)(2,1)S(1)}, u32[]{:S(2)}, u32[]{:S(2)}) %all-to-all-start.2) | async-done | bytes 786464 | tf_op jit(solution)/shard_map/all_to_all | solution.py:380
  (455 shorter events, 338.7 us)
Async XLA Ops:
  7.2 51.6 %all-gather.5.cloned.1.call-start = ((), (), s32[]{:S(2)}) async-start(), calls=%async_computation.7 | async-start | bytes 2621440 | tf_op jit(solution)/shard_map/all_gather | solution.py:385
  24.0 41.1 %collective-permute-start = (bf16[96,2048]{1,0:T(8,128)(2,1)}, bf16[96,2048]{1,0:T(8,128)(2,1)}, u32[]{:S(2)}, u32[]{:S(2)}) collective-permute-start(bf16[96,2048]{1,0:T(8,128)(2,1)} %get-tuple-element.130), channel_id=1, source_target_pairs={{0,16},{4,20},{8,24},{12,28},{16,0},{20,4},{24,8},{28,12},{1,17},{... | collective-permute-start | bytes 1179656 | tf_op jit(solution)/shard_map/ppermute | solution.py:288
  26.1 42.5 %collective-permute-start.1 = (bf16[96,2048]{1,0:T(8,128)(2,1)}, bf16[96,2048]{1,0:T(8,128)(2,1)}, u32[]{:S(2)}, u32[]{:S(2)}) collective-permute-start(bf16[96,2048]{1,0:T(8,128)(2,1)} %get-tuple-element.130), channel_id=1, source_target_pairs={{0,8},{4,12},{8,0},{12,4},{16,24},{20,28},{24,16},{28,20},{1,9},{5... | collective-permute-start | bytes 1179656 | tf_op jit(solution)/shard_map/ppermute | solution.py:288
  27.5 60.4 %collective-permute-start.3 = (bf16[96,2048]{1,0:T(8,128)(2,1)}, bf16[96,2048]{1,0:T(8,128)(2,1)}, u32[]{:S(2)}, u32[]{:S(2)}) collective-permute-start(bf16[96,2048]{1,0:T(8,128)(2,1)} %get-tuple-element.129), channel_id=1, source_target_pairs={{0,8},{4,12},{8,0},{12,4},{16,24},{20,28},{24,16},{28,20},{1,9},{5... | collective-permute-start | bytes 1179656 | tf_op jit(solution)/shard_map/ppermute | solution.py:288
  28.1 62.3 %collective-permute-start.4 = (bf16[96,2048]{1,0:T(8,128)(2,1)}, bf16[96,2048]{1,0:T(8,128)(2,1)}, u32[]{:S(2)}, u32[]{:S(2)}) collective-permute-start(bf16[96,2048]{1,0:T(8,128)(2,1)} %get-tuple-element.129), channel_id=1, source_target_pairs={{0,16},{4,20},{8,24},{12,28},{16,0},{20,4},{24,8},{28,12},{1,17},{... | collective-permute-start | bytes 1179656 | tf_op jit(solution)/shard_map/ppermute | solution.py:288
  28.1 116.0 %collective-permute-start.6 = (bf16[96,2048]{1,0:T(8,128)(2,1)}, bf16[96,2048]{1,0:T(8,128)(2,1)}, u32[]{:S(2)}, u32[]{:S(2)}) collective-permute-start(bf16[96,2048]{1,0:T(8,128)(2,1)} %get-tuple-element.130), channel_id=1, source_target_pairs={{0,4},{4,0},{8,12},{12,8},{16,20},{20,16},{24,28},{28,24},{1,5},{5... | collective-permute-start | bytes 1179656 | tf_op jit(solution)/shard_map/ppermute | solution.py:288
  43.1 42.5 %all-to-all-start.1 = ((bf16[64,8,2048]{2,0,1:T(8,128)(2,1)}), bf16[64,8,2048]{2,0,1:T(8,128)(2,1)}, u32[]{:S(2)}, u32[]{:S(2)}) async-start(bf16[64,8,2048]{2,0,1:T(8,128)(2,1)} %copy.86), calls=%async_computation.1 | async-start | bytes 4194304 | tf_op jit(solution)/shard_map/all_to_all | solution.py:377
  47.4 95.2 %all-gather.7.cloned.1.call-start = ((), (), s32[]{:S(2)}) async-start(), calls=%async_computation.8 | async-start | bytes 5406720 | tf_op jit(solution)/shard_map/all_gather | solution.py:385
  58.9 233.5 %all-gather.9.cloned.1.call-start = ((), (), s32[]{:S(2)}) async-start(), calls=%async_computation.9 | async-start | bytes 10485760 | tf_op jit(solution)/shard_map/all_gather | solution.py:385
  68.5 80.7 %collective-permute-start.10 = (bf16[96,2048]{1,0:T(8,128)(2,1)}, bf16[96,2048]{1,0:T(8,128)(2,1)S(1)}, u32[]{:S(2)}, u32[]{:S(2)}) collective-permute-start(bf16[96,2048]{1,0:T(8,128)(2,1)} %get-tuple-element.129), channel_id=1, source_target_pairs={{0,4},{4,0},{8,12},{12,8},{16,20},{20,16},{24,28},{28,24},{1,5},{5... | collective-permute-start | bytes 1179656 | tf_op jit(solution)/shard_map/ppermute | solution.py:288
  101.8 41.4 %collective-permute-start.5 = (bf16[96,2048]{1,0:T(8,128)(2,1)}, bf16[96,2048]{1,0:T(8,128)(2,1)S(1)}, u32[]{:S(2)}, u32[]{:S(2)}) collective-permute-start(bf16[96,2048]{1,0:T(8,128)(2,1)} %collective-permute-done.3), channel_id=1, source_target_pairs={{0,16},{4,20},{8,24},{12,28},{16,0},{20,4},{24,8},{28,12},{1,17},{... | collective-permute-start | bytes 1179656 | tf_op jit(solution)/shard_map/ppermute | solution.py:288
  142.7 196.3 %all-gather.11.cloned.1.call-start = ((), (), s32[]{:S(2)}) async-start(), calls=%async_computation.10 | async-start | bytes 2621440 | tf_op jit(solution)/shard_map/all_gather | solution.py:385
  234.5 27.0 %collective-permute-start.24 = (bf16[96,2048]{1,0:T(8,128)(2,1)S(1)}, bf16[96,2048]{1,0:T(8,128)(2,1)S(1)}, u32[]{:S(2)}, u32[]{:S(2)}) collective-permute-start(bf16[96,2048]{1,0:T(8,128)(2,1)S(1)} %get-tuple-element.123), channel_id=1, source_target_pairs={{0,16},{4,20},{8,24},{12,28},{16,0},{20,4},{24,8},{28,12},{1,17},{... | collective-permute-start | bytes 1179656 | tf_op jit(solution)/shard_map/ppermute | solution.py:288
  235.0 33.0 %collective-permute-start.26 = (bf16[96,2048]{1,0:T(8,128)(2,1)S(1)}, bf16[96,2048]{1,0:T(8,128)(2,1)S(1)}, u32[]{:S(2)}, u32[]{:S(2)}) collective-permute-start(bf16[96,2048]{1,0:T(8,128)(2,1)S(1)} %get-tuple-element.125), channel_id=1, source_target_pairs={{0,4},{4,0},{8,12},{12,8},{16,20},{20,16},{24,28},{28,24},{1,5},{5... | collective-permute-start | bytes 1179656 | tf_op jit(solution)/shard_map/ppermute | solution.py:288
  245.4 26.8 %collective-permute-start.30 = (bf16[96,2048]{1,0:T(8,128)(2,1)S(1)}, bf16[96,2048]{1,0:T(8,128)(2,1)S(1)}, u32[]{:S(2)}, u32[]{:S(2)}) collective-permute-start(bf16[96,2048]{1,0:T(8,128)(2,1)S(1)} %get-tuple-element.123), channel_id=1, source_target_pairs={{0,4},{4,0},{8,12},{12,8},{16,20},{20,16},{24,28},{28,24},{1,5},{5... | collective-permute-start | bytes 1179656 | tf_op jit(solution)/shard_map/ppermute | solution.py:288
  292.4 123.8 %reduce-scatter.4.cloned.1.call-start = ((), (), s32[]{:S(2)}) async-start(), calls=%async_computation.11 | async-start | bytes 5242880 | tf_op jit(solution)/shard_map/reduce_scatter | solution.py:388
  339.0 224.6 %reduce-scatter.6.cloned.1.call-start = ((), (), s32[]{:S(2)}) async-start(), calls=%async_computation.12 | async-start | bytes 10485760 | tf_op jit(solution)/shard_map/reduce_scatter | solution.py:388
  416.3 227.2 %reduce-scatter.8.cloned.1.call-start = ((), (), s32[]{:S(2)}) async-start(), calls=%async_computation.13 | async-start | bytes 5242880 | tf_op jit(solution)/shard_map/reduce_scatter | solution.py:388
  457.9 32.2 %collective-permute-start.60 = (bf16[96,2048]{1,0:T(8,128)(2,1)S(1)}, bf16[96,2048]{1,0:T(8,128)(2,1)S(1)}, u32[]{:S(2)}, u32[]{:S(2)}) collective-permute-start(bf16[96,2048]{1,0:T(8,128)(2,1)S(1)} %get-tuple-element.122), channel_id=1, source_target_pairs={{0,4},{4,0},{8,12},{12,8},{16,20},{20,16},{24,28},{28,24},{1,5},{5... | collective-permute-start | bytes 1179656 | tf_op jit(solution)/shard_map/ppermute | solution.py:288
  505.0 32.9 %collective-permute-start.68 = (bf16[192,2048]{1,0:T(8,128)(2,1)}, bf16[192,2048]{1,0:T(8,128)(2,1)}, u32[]{:S(2)}, u32[]{:S(2)}) collective-permute-start(bf16[192,2048]{1,0:T(8,128)(2,1)} %get-tuple-element.109), channel_id=1, source_target_pairs={{0,8},{4,12},{8,0},{12,4},{16,24},{20,28},{24,16},{28,20},{1,9},{5... | collective-permute-start | bytes 2359304 | tf_op jit(solution)/shard_map/ppermute | solution.py:288
  505.6 32.4 %collective-permute-start.70 = (bf16[192,2048]{1,0:T(8,128)(2,1)}, bf16[192,2048]{1,0:T(8,128)(2,1)}, u32[]{:S(2)}, u32[]{:S(2)}) collective-permute-start(bf16[192,2048]{1,0:T(8,128)(2,1)} %get-tuple-element.110), channel_id=1, source_target_pairs={{0,16},{4,20},{8,24},{12,28},{16,0},{20,4},{24,8},{28,12},{1,17},{... | collective-permute-start | bytes 2359304 | tf_op jit(solution)/shard_map/ppermute | solution.py:288
  586.5 51.6 %all-to-all-start.3 = ((bf16[8,64,1,2048]{3,1,2,0:T(8,128)(2,1)}), bf16[8,64,1,2048]{3,1,2,0:T(8,128)(2,1)S(1)}, u32[]{:S(2)}, u32[]{:S(2)}) async-start(bf16[8,64,1,2048]{3,1,2,0:T(8,128)(2,1)} %bitcast.153), calls=%async_computation.6 | async-start | bytes 4194304 | tf_op jit(solution)/shard_map/all_to_all | solution.py:380
  609.7 26.5 %collective-permute-start.74 = (bf16[96,2048]{1,0:T(8,128)(2,1)S(1)}, bf16[96,2048]{1,0:T(8,128)(2,1)S(1)}, u32[]{:S(2)}, u32[]{:S(2)}) collective-permute-start(bf16[96,2048]{1,0:T(8,128)(2,1)S(1)} %slice.488), channel_id=1, source_target_pairs={{0,16},{4,20},{8,24},{12,28},{16,0},{20,4},{24,8},{28,12},{1,17},{... | collective-permute-start | bytes 1179656 | tf_op jit(solution)/shard_map/ppermute | solution.py:288
  610.3 25.8 %collective-permute-start.76 = (bf16[96,2048]{1,0:T(8,128)(2,1)S(1)}, bf16[96,2048]{1,0:T(8,128)(2,1)S(1)}, u32[]{:S(2)}, u32[]{:S(2)}) collective-permute-start(bf16[96,2048]{1,0:T(8,128)(2,1)S(1)} %slice.487), channel_id=1, source_target_pairs={{0,8},{4,12},{8,0},{12,4},{16,24},{20,28},{24,16},{28,20},{1,9},{5... | collective-permute-start | bytes 1179656 | tf_op jit(solution)/shard_map/ppermute | solution.py:288
  (118 other events, 1726.1 us)
Sparse Core Ops, SparseCore 0:
  10.2 48.6 all-gather.4
  61.0 81.6 all-gather.6
  144.2 148.1 all-gather.8
  294.4 44.1 all-gather.10
  340.8 75.4 reduce-scatter.3
  418.6 144.9 reduce-scatter.5
  566.0 77.4 reduce-scatter.7

commit v4 on v3

--- a/solution.py
+++ b/solution.py
@@ -472,13 +472,18 @@
         attend_backward(queries, keys, values, attended, grad_heads, logs, order, cosine, sine, block), -1
     )
     qkv_whole = outer(normed_one, after(grad_qkv, *marks[1:]))
-    sums = reduce_tokens(after(grad_qkv, qkv_whole), qkv_weight, ((1,), (1,)), seq)
+    ready = []
+
+    def early(got, kept):
+        ready.extend(kept)
+        return got
+
+    sums = reduce_tokens(after(grad_qkv, qkv_whole), qkv_weight, ((1,), (1,)), seq, [early])
     (grad_inputs,) = norm_call(
         norm_back_kernel, "norm_one_back", counts, 0, gains, [own_tokens, grad_middle], sums, [LOW]
     )
-    last_whole = jnp.concatenate([qkv_whole, out_whole.reshape(width, group)], -1)
-    last_part = summed(after(last_whole, pair_part))
-    qkv_part, out_part = last_part[:, : 3 * group], last_part[:, 3 * group :].reshape(wrows, width)
+    qkv_part = summed(after(qkv_whole, pair_part, *ready))
+    out_part = summed(after(out_whole, qkv_part))
 
     def finish(piece, weight):
         piece = piece.reshape(wrows, -1).astype(F32)

time: 680 us -> 675 us (level)
  waiting for transfers between devices: 258 us -> 245 us
  local copies, waits for them, and re-layouts: 89.7 us -> 101 us
    ppermute x77, waiting for transfers between devices: 177 us -> 161 us  [flip(): return lax.ppermute(values, axis, [(i, i ^ mask) for i in range(count)])]
    unnamed x177 -> x173, local copies, waits for them, and re-layouts: 53 us -> 67 us
    reduce_scatter x3 -> x4, waiting for transfers between devices: 37.1 us -> 40.6 us  [summed(): return lax.psum_scatter(whole, 'fsdp', scatter_dimension=0, tiled=True)]
  transfers between devices with their start and end apart: 88 -> 89, of which waited for: 38 -> 38; matrix products, arithmetic and copies ran while one was open for 39% -> 41% of each run, Pallas kernels for 8% -> 8%
where the time goes in v4:
time: 675 us; the launch traced here: 667 us
  waiting for transfers between devices  245 us (36%)
  matrix products  137 us (20%)
  local copies, waits for them, and re-layouts  101 us (15%)
  starting transfers between devices  66.7 us (10%)
  Pallas kernels  51.1 us (8%)
  other arithmetic  50.8 us (8%)
  between operations  15.6 us (2%)
    ppermute x77, waiting for transfers between devices, flip(): return lax.ppermute(values, axis, [(i, i ^ mask) for i in range(count)])  161 us
    unnamed x173, local copies, waits for them, and re-layouts  67 us
    ppermute x77, starting transfers between devices, flip(): return lax.ppermute(values, axis, [(i, i ^ mask) for i in range(count)])  48.8 us
    dot_general x10, matrix products, part(): lax.dot_general(rows, weight, (dims, ((), ())), preferred_element_type=F32)  44.5 us
    dot_general x4, matrix products, outer(): jnp.einsum('ti,to->io', left, right, preferred_element_type=F32).astype(LOW)  41.6 us
    reduce_scatter x4, waiting for transfers between devices, summed(): return lax.psum_scatter(whole, 'fsdp', scatter_dimension=0, tiled=True)  40.6 us
    all_gather x4, waiting for transfers between devices, gathered(): return lax.all_gather(piece, 'fsdp', axis=0, tiled=True)  34.1 us
    pallas_call x1, Pallas kernels, attend_backward(): pl.pallas_call(functools.partial(attend_back_kernel, block), grid_spec=pl...  23 us
  transfers between devices with their start and end apart: 89, of which 38 were waited for; matrix products, arithmetic and copies ran while one was open for 41% of the time, Pallas kernels for 8%

profile of v4, /device:TPU:0, one launch (start us, length us, event | category | flops | bytes accessed | tf_op | source)
XLA Modules:
  0.0 667.2 jit_solution(9409121751399408184)
XLA Ops:
  49.8 9.1 %all-gather.5.cloned.1.call-done = bf16[1024,1024]{1,0:T(8,128)(2,1)} async-done(((bf16[256,1024]{1,0:T(8,128)(2,1)}), bf16[1024,1024]{1,0:T(8,128)(2,1)}) %all-gather.5.cloned.1.call-update) | async-done | bytes 2097168 | tf_op jit(solution)/shard_map/all_gather | solution.py:385
  70.4 13.6 %collective-permute-done.2 = bf16[96,2048]{1,0:T(8,128)(2,1)S(1)} collective-permute-done((bf16[96,2048]{1,0:T(8,128)(2,1)}, bf16[96,2048]{1,0:T(8,128)(2,1)S(1)}, u32[]{:S(2)}, u32[]{:S(2)}) %collective-permute-start.2) | collective-permute-done | bytes 393248 | tf_op jit(solution)/shard_map/ppermute | solution.py:288
  103.1 7.1 %collective-permute-done.37 = bf16[96,2048]{1,0:T(8,128)(2,1)S(1)} collective-permute-done((bf16[96,2048]{1,0:T(8,128)(2,1)S(1)}, bf16[96,2048]{1,0:T(8,128)(2,1)S(1)}, u32[]{:S(2)}, u32[]{:S(2)}) %collective-permute-start.37) | collective-permute-done | bytes 393248 | tf_op jit(solution)/shard_map/ppermute | solution.py:288
  173.4 17.2 %attend_forward.1 = (bf16[1536,256]{1,0:T(8,128)(2,1)S(1)}, bf16[1536,256]{1,0:T(8,128)(2,1)S(1)}, bf16[1536,256]{1,0:T(8,128)(2,1)S(1)}, bf16[1536,256]{1,0:T(8,128)(2,1)S(1)}, f32[2,2,1536]{2,1,0:T(2,128)S(1)}) custom-call(s32[16]{0:T(128)S(1)} %stack.67.order, f32[1536,768]{1,0:T(8,128)} %fusion.41.q.k.v, f32[1536,768]{1,0:T(8,128)} %fusion.41.q.k.v, ...), custom_call_target="tpu_custom_call" | custom-call | tf_op jit(solution)/shard_map/attend_forward/pallas_call | solution.py:116
  199.3 15.8 %collective-permute-done.18 = bf16[192,2048]{1,0:T(8,128)(2,1)S(1)} collective-permute-done((bf16[192,2048]{1,0:T(8,128)(2,1)S(1)}, bf16[192,2048]{1,0:T(8,128)(2,1)S(1)}, u32[]{:S(2)}, u32[]{:S(2)}) %collective-permute-start.18) | collective-permute-done | bytes 786464 | tf_op jit(solution)/shard_map/ppermute | solution.py:288
  233.9 8.0 %collective-permute-done.20 = bf16[96,2048]{1,0:T(8,128)(2,1)S(1)} collective-permute-done((bf16[96,2048]{1,0:T(8,128)(2,1)S(1)}, bf16[96,2048]{1,0:T(8,128)(2,1)S(1)}, u32[]{:S(2)}, u32[]{:S(2)}) %collective-permute-start.20) | collective-permute-done | bytes 393248 | tf_op jit(solution)/shard_map/ppermute | solution.py:288
  245.1 6.9 %collective-permute-done.23 = bf16[96,2048]{1,0:T(8,128)(2,1)S(1)} collective-permute-done((bf16[96,2048]{1,0:T(8,128)(2,1)S(1)}, bf16[96,2048]{1,0:T(8,128)(2,1)S(1)}, u32[]{:S(2)}, u32[]{:S(2)}) %collective-permute-start.23) | collective-permute-done | bytes 393248 | tf_op jit(solution)/shard_map/ppermute | solution.py:288
  274.4 18.1 %all-gather.9.cloned.1.call-done = bf16[2048,2048]{1,0:T(8,128)(2,1)} async-done(((bf16[512,2048]{1,0:T(8,128)(2,1)}), bf16[2048,2048]{1,0:T(8,128)(2,1)}) %all-gather.9.cloned.1.call-update) | async-done | bytes 8388624 | tf_op jit(solution)/shard_map/all_gather | solution.py:385
  292.5 17.7 %fusion.42 = f32[1536,2048]{1,0:T(8,128)S(1)} fusion(bf16[1536,2048]{1,0:T(8,128)(2,1)} %constant_dynamic-update-slice_fusion.16, bf16[2048,2048]{1,0:T(8,128)(2,1)} %all-gather.9.cloned.1.call-done), kind=kOutput, calls=%fused_computation.181 | convolution fusion | flops 12884901888 | bytes 27262976 | tf_op jit(solution)/shard_map/dot_general | solution.py:424
  318.5 11.2 %convolution_convert_fusion.1 = bf16[1024,2048]{1,0:T(8,128)(2,1)} fusion(bf16[1536,1024]{1,0:T(8,128)(2,1)S(1)} %multiply_convert_fusion.2, bf16[1536,2048]{1,0:T(8,128)(2,1)} %constant_dynamic-update-slice_fusion.32), kind=kOutput, calls=%fused_computation.14 | convolution fusion | flops 6444548096 | bytes 13631488 | tf_op jit(solution)/shard_map/ti,to->io/dot_general | solution.py:391
  329.7 8.6 %fusion.6 = f32[1536,1024]{1,0:T(8,128)} fusion(bf16[1024,1024]{1,0:T(8,128)(2,1)} %all-gather.5.cloned.1.call-done, bf16[1536,2048]{1,0:T(8,128)(2,1)} %constant_dynamic-update-slice_fusion.32), kind=kOutput, calls=%fused_computation.23 | convolution fusion | flops 3221225472 | bytes 11534336 | tf_op jit(solution)/shard_map/td,fd->tf/dot_general | solution.py:431
  338.7 11.7 %multiply_convert_fusion = (bf16[1536,1024]{1,0:T(8,128)(2,1)S(1)}, bf16[1536,1024]{1,0:T(8,128)(2,1)S(1)}) fusion(f32[1536,2048]{1,0:T(8,128)} %copy-done.19, f32[1536,1024]{1,0:T(8,128)} %fusion.6, bf16[1024,1024]{1,0:T(8,128)(2,1)} %all-gather.11.cloned.1.call-done, bf16[1536,2048]{1,0:T(8,128)(2,1)} %constant_dynamic-update-slice_fusion.32), kind=kOutput, calls=%fused_computation.9 | convolution fusion | flops 3243245568 | bytes 30408704 | tf_op jit(solution)/shard_map/td,fd->tf/dot_general | solution.py:433
  350.4 11.5 %convolution_convert_fusion.2 = bf16[768,2048]{1,0:T(8,128)(2,1)} fusion(bf16[2048,2048]{1,0:T(8,128)(2,1)} %all-gather.9.cloned.1.call-done, bf16[1536,1024]{1,0:T(8,128)(2,1)S(1)} %get-tuple-element.104, bf16[1536,1024]{1,0:T(8,128)(2,1)S(1)} %get-tuple-element.103), kind=kOutput, calls=%fused_computation.15 | convolution fusion | flops 6450315264 | bytes 17825792 | tf_op jit(solution)/shard_map/dot_general | solution.py:335
  367.9 13.3 %fusion.33 = (bf16[768,2048]{1,0:T(8,128)(2,1)}, f32[768,2048]{1,0:T(8,128)}) fusion(bf16[768,2048]{1,0:T(8,128)(2,1)} %collective-permute-done.48, bf16[2048,2048]{1,0:T(8,128)(2,1)} %all-gather.9.cloned.1.call-done, bf16[1536,1024]{1,0:T(8,128)(2,1)} %copy-done.32, bf16[1536,1024]{1,0:T(8,128)(2,1)S(1)} %get-tuple-element.103), kind=kOutput, calls=%fused_computation.172 | convolution fusion | flops 6453460992 | bytes 27262976 | tf_op jit(solution)/shard_map/dot_general | solution.py:335
  381.3 17.9 %convolution_convert_fusion = bf16[2048,2048]{1,0:T(8,128)(2,1)} fusion(bf16[1536,2048]{1,0:T(8,128)(2,1)} %constant_dynamic-update-slice_fusion.16, bf16[1536,2048]{1,0:T(8,128)(2,1)S(1)} %pad_maximum_fusion), kind=kOutput, calls=%fused_computation.5 | convolution fusion | flops 12889096192 | bytes 20971520 | tf_op jit(solution)/shard_map/ti,to->io/dot_general | solution.py:391
  399.2 17.1 %reduce-scatter.5.cloned.1.call-done = bf16[256,2048]{1,0:T(8,128)(2,1)} async-done(((bf16[1024,2048]{1,0:T(8,128)(2,1)}), bf16[256,2048]{1,0:T(8,128)(2,1)}) %reduce-scatter.5.cloned.1.call-update) | async-done | bytes 1048592 | tf_op jit(solution)/shard_map/reduce_scatter | solution.py:388
  421.1 16.4 %collective-permute-done.49 = bf16[192,2048]{1,0:T(8,128)(2,1)S(1)} collective-permute-done((bf16[192,2048]{1,0:T(8,128)(2,1)S(1)}, bf16[192,2048]{1,0:T(8,128)(2,1)S(1)}, u32[]{:S(2)}, u32[]{:S(2)}) %collective-permute-start.49) | collective-permute-done | bytes 786464 | tf_op jit(solution)/shard_map/ppermute | solution.py:288
  444.0 7.1 %collective-permute-done.50.refs_1_ = bf16[96,2048]{1,0:T(8,128)(2,1)S(1)} collective-permute-done((bf16[96,2048]{1,0:T(8,128)(2,1)S(1)}, bf16[96,2048]{1,0:T(8,128)(2,1)S(1)}, u32[]{:S(2)}, u32[]{:S(2)}) %collective-permute-start.50) | collective-permute-done | bytes 393248 | tf_op jit(solution)/shard_map/ppermute | solution.py:288
  508.7 23.0 %attend_backward.1 = (bf16[1536,256]{1,0:T(8,128)(2,1)S(1)}, bf16[1536,256]{1,0:T(8,128)(2,1)S(1)}, bf16[1536,256]{1,0:T(8,128)(2,1)S(1)}) custom-call(s32[16]{0:T(128)S(1)} %copy-done.16, bf16[1536,256]{1,0:T(8,128)(2,1)S(1)} %copy-done.11, bf16[1536,256]{1,0:T(8,128)(2,1)S(1)} %copy-done.13, bf16[1536,256]{1,0:T(8,128)(2,1)} %copy-done.14, ...), custom_call_target="tpu_custom_call" | custom-call | tf_op jit(solution)/shard_map/attend_backward/pallas_call | solution.py:194
  533.4 6.9 %convolution_convert_fusion.5 = bf16[2048,768]{1,0:T(8,128)(2,1)} fusion(bf16[1536,2048]{1,0:T(8,128)(2,1)S(1)} %bitcast.127, bf16[1536,768]{1,0:T(8,128)(2,1)S(1)} %constant_dynamic-update-slice_fusion.66), kind=kOutput, calls=%fused_computation.18 | convolution fusion | flops 4833411072 | bytes 11796480 | tf_op jit(solution)/shard_map/ti,to->io/dot_general | solution.py:391
  556.0 7.6 %reduce-scatter.7.cloned.1.call-done = bf16[512,2048]{1,0:T(8,128)(2,1)} async-done(((bf16[2048,2048]{1,0:T(8,128)(2,1)}), bf16[512,2048]{1,0:T(8,128)(2,1)}) %reduce-scatter.7.cloned.1.call-update) | async-done | bytes 2097168 | tf_op jit(solution)/shard_map/reduce_scatter | solution.py:388
  589.9 14.7 %collective-permute-done.73 = bf16[192,2048]{1,0:T(8,128)(2,1)} collective-permute-done((bf16[192,2048]{1,0:T(8,128)(2,1)}, bf16[192,2048]{1,0:T(8,128)(2,1)}, u32[]{:S(2)}, u32[]{:S(2)}) %collective-permute-start.73) | collective-permute-done | bytes 786464 | tf_op jit(solution)/shard_map/ppermute | solution.py:288
  611.1 15.9 %reduce-scatter.9.cloned.1.call-done = bf16[512,768]{1,0:T(8,128)(2,1)} async-done(((bf16[2048,768]{1,0:T(8,128)(2,1)}), bf16[512,768]{1,0:T(8,128)(2,1)}) %reduce-scatter.9.cloned.1.call-update) | async-done | bytes 786448 | tf_op jit(solution)/shard_map/reduce_scatter | solution.py:388
  649.1 7.8 %all-to-all-done.2 = bf16[8,64,1,768]{3,1,2,0:T(8,128)(2,1)S(1)} async-done(((bf16[8,64,1,768]{3,1,2,0:T(8,128)(2,1)}), bf16[8,64,1,768]{3,1,2,0:T(8,128)(2,1)S(1)}, u32[]{:S(2)}, u32[]{:S(2)}) %all-to-all-start.2) | async-done | bytes 786464 | tf_op jit(solution)/shard_map/all_to_all | solution.py:380
  (446 shorter events, 347.6 us)
Async XLA Ops:
  7.2 51.6 %all-gather.5.cloned.1.call-start = ((), (), s32[]{:S(2)}) async-start(), calls=%async_computation.8 | async-start | bytes 2621440 | tf_op jit(solution)/shard_map/all_gather | solution.py:385
  24.0 41.3 %collective-permute-start = (bf16[96,2048]{1,0:T(8,128)(2,1)}, bf16[96,2048]{1,0:T(8,128)(2,1)}, u32[]{:S(2)}, u32[]{:S(2)}) collective-permute-start(bf16[96,2048]{1,0:T(8,128)(2,1)} %get-tuple-element.134), channel_id=1, source_target_pairs={{0,16},{4,20},{8,24},{12,28},{16,0},{20,4},{24,8},{28,12},{1,17},{... | collective-permute-start | bytes 1179656 | tf_op jit(solution)/shard_map/ppermute | solution.py:288
  26.0 42.6 %collective-permute-start.1 = (bf16[96,2048]{1,0:T(8,128)(2,1)}, bf16[96,2048]{1,0:T(8,128)(2,1)}, u32[]{:S(2)}, u32[]{:S(2)}) collective-permute-start(bf16[96,2048]{1,0:T(8,128)(2,1)} %get-tuple-element.134), channel_id=1, source_target_pairs={{0,8},{4,12},{8,0},{12,4},{16,24},{20,28},{24,16},{28,20},{1,9},{5... | collective-permute-start | bytes 1179656 | tf_op jit(solution)/shard_map/ppermute | solution.py:288
  27.5 60.4 %collective-permute-start.3 = (bf16[96,2048]{1,0:T(8,128)(2,1)}, bf16[96,2048]{1,0:T(8,128)(2,1)}, u32[]{:S(2)}, u32[]{:S(2)}) collective-permute-start(bf16[96,2048]{1,0:T(8,128)(2,1)} %get-tuple-element.133), channel_id=1, source_target_pairs={{0,8},{4,12},{8,0},{12,4},{16,24},{20,28},{24,16},{28,20},{1,9},{5... | collective-permute-start | bytes 1179656 | tf_op jit(solution)/shard_map/ppermute | solution.py:288
  28.0 62.3 %collective-permute-start.4 = (bf16[96,2048]{1,0:T(8,128)(2,1)}, bf16[96,2048]{1,0:T(8,128)(2,1)}, u32[]{:S(2)}, u32[]{:S(2)}) collective-permute-start(bf16[96,2048]{1,0:T(8,128)(2,1)} %get-tuple-element.133), channel_id=1, source_target_pairs={{0,16},{4,20},{8,24},{12,28},{16,0},{20,4},{24,8},{28,12},{1,17},{... | collective-permute-start | bytes 1179656 | tf_op jit(solution)/shard_map/ppermute | solution.py:288
  28.1 116.9 %collective-permute-start.6 = (bf16[96,2048]{1,0:T(8,128)(2,1)}, bf16[96,2048]{1,0:T(8,128)(2,1)}, u32[]{:S(2)}, u32[]{:S(2)}) collective-permute-start(bf16[96,2048]{1,0:T(8,128)(2,1)} %get-tuple-element.134), channel_id=1, source_target_pairs={{0,4},{4,0},{8,12},{12,8},{16,20},{20,16},{24,28},{28,24},{1,5},{5... | collective-permute-start | bytes 1179656 | tf_op jit(solution)/shard_map/ppermute | solution.py:288
  43.0 42.5 %all-to-all-start.1 = ((bf16[64,8,2048]{2,0,1:T(8,128)(2,1)}), bf16[64,8,2048]{2,0,1:T(8,128)(2,1)}, u32[]{:S(2)}, u32[]{:S(2)}) async-start(bf16[64,8,2048]{2,0,1:T(8,128)(2,1)} %copy.74), calls=%async_computation.1 | async-start | bytes 4194304 | tf_op jit(solution)/shard_map/all_to_all | solution.py:377
  47.4 95.2 %all-gather.7.cloned.1.call-start = ((), (), s32[]{:S(2)}) async-start(), calls=%async_computation.9 | async-start | bytes 5406720 | tf_op jit(solution)/shard_map/all_gather | solution.py:385
  58.9 233.5 %all-gather.9.cloned.1.call-start = ((), (), s32[]{:S(2)}) async-start(), calls=%async_computation.10 | async-start | bytes 10485760 | tf_op jit(solution)/shard_map/all_gather | solution.py:385
  68.6 81.7 %collective-permute-start.10 = (bf16[96,2048]{1,0:T(8,128)(2,1)}, bf16[96,2048]{1,0:T(8,128)(2,1)S(1)}, u32[]{:S(2)}, u32[]{:S(2)}) collective-permute-start(bf16[96,2048]{1,0:T(8,128)(2,1)} %get-tuple-element.133), channel_id=1, source_target_pairs={{0,4},{4,0},{8,12},{12,8},{16,20},{20,16},{24,28},{28,24},{1,5},{5... | collective-permute-start | bytes 1179656 | tf_op jit(solution)/shard_map/ppermute | solution.py:288
  101.7 41.2 %collective-permute-start.5 = (bf16[96,2048]{1,0:T(8,128)(2,1)}, bf16[96,2048]{1,0:T(8,128)(2,1)}, u32[]{:S(2)}, u32[]{:S(2)}) collective-permute-start(bf16[96,2048]{1,0:T(8,128)(2,1)} %collective-permute-done.3), channel_id=1, source_target_pairs={{0,16},{4,20},{8,24},{12,28},{16,0},{20,4},{24,8},{28,12},{1,17},{... | collective-permute-start | bytes 1179656 | tf_op jit(solution)/shard_map/ppermute | solution.py:288
  142.7 195.9 %all-gather.11.cloned.1.call-start = ((), (), s32[]{:S(2)}) async-start(), calls=%async_computation.11 | async-start | bytes 2621440 | tf_op jit(solution)/shard_map/all_gather | solution.py:385
  233.5 26.8 %collective-permute-start.24 = (bf16[96,2048]{1,0:T(8,128)(2,1)S(1)}, bf16[96,2048]{1,0:T(8,128)(2,1)S(1)}, u32[]{:S(2)}, u32[]{:S(2)}) collective-permute-start(bf16[96,2048]{1,0:T(8,128)(2,1)S(1)} %get-tuple-element.127), channel_id=1, source_target_pairs={{0,16},{4,20},{8,24},{12,28},{16,0},{20,4},{24,8},{28,12},{1,17},{... | collective-permute-start | bytes 1179656 | tf_op jit(solution)/shard_map/ppermute | solution.py:288
  233.9 33.1 %collective-permute-start.26 = (bf16[96,2048]{1,0:T(8,128)(2,1)S(1)}, bf16[96,2048]{1,0:T(8,128)(2,1)S(1)}, u32[]{:S(2)}, u32[]{:S(2)}) collective-permute-start(bf16[96,2048]{1,0:T(8,128)(2,1)S(1)} %get-tuple-element.129), channel_id=1, source_target_pairs={{0,4},{4,0},{8,12},{12,8},{16,20},{20,16},{24,28},{28,24},{1,5},{5... | collective-permute-start | bytes 1179656 | tf_op jit(solution)/shard_map/ppermute | solution.py:288
  244.3 26.9 %collective-permute-start.30 = (bf16[96,2048]{1,0:T(8,128)(2,1)S(1)}, bf16[96,2048]{1,0:T(8,128)(2,1)S(1)}, u32[]{:S(2)}, u32[]{:S(2)}) collective-permute-start(bf16[96,2048]{1,0:T(8,128)(2,1)S(1)} %get-tuple-element.127), channel_id=1, source_target_pairs={{0,4},{4,0},{8,12},{12,8},{16,20},{20,16},{24,28},{28,24},{1,5},{5... | collective-permute-start | bytes 1179656 | tf_op jit(solution)/shard_map/ppermute | solution.py:288
  292.4 123.8 %reduce-scatter.5.cloned.1.call-start = ((), (), s32[]{:S(2)}) async-start(), calls=%async_computation.12 | async-start | bytes 5242880 | tf_op jit(solution)/shard_map/reduce_scatter | solution.py:388
  338.6 225.0 %reduce-scatter.7.cloned.1.call-start = ((), (), s32[]{:S(2)}) async-start(), calls=%async_computation.13 | async-start | bytes 10485760 | tf_op jit(solution)/shard_map/reduce_scatter | solution.py:388
  416.3 210.7 %reduce-scatter.9.cloned.1.call-start = ((), (), s32[]{:S(2)}) async-start(), calls=%async_computation.14 | async-start | bytes 3932160 | tf_op jit(solution)/shard_map/reduce_scatter | solution.py:388
  457.2 27.0 %collective-permute-start.58 = (bf16[96,2048]{1,0:T(8,128)(2,1)S(1)}, bf16[96,2048]{1,0:T(8,128)(2,1)S(1)}, u32[]{:S(2)}, u32[]{:S(2)}) collective-permute-start(bf16[96,2048]{1,0:T(8,128)(2,1)S(1)} %get-tuple-element.124), channel_id=1, source_target_pairs={{0,16},{4,20},{8,24},{12,28},{16,0},{20,4},{24,8},{28,12},{1,17},{... | collective-permute-start | bytes 1179656 | tf_op jit(solution)/shard_map/ppermute | solution.py:288
  458.6 31.0 %collective-permute-start.60 = (bf16[96,2048]{1,0:T(8,128)(2,1)S(1)}, bf16[96,2048]{1,0:T(8,128)(2,1)S(1)}, u32[]{:S(2)}, u32[]{:S(2)}) collective-permute-start(bf16[96,2048]{1,0:T(8,128)(2,1)S(1)} %get-tuple-element.126), channel_id=1, source_target_pairs={{0,4},{4,0},{8,12},{12,8},{16,20},{20,16},{24,28},{28,24},{1,5},{5... | collective-permute-start | bytes 1179656 | tf_op jit(solution)/shard_map/ppermute | solution.py:288
  501.3 30.6 %collective-permute-start.68 = (bf16[192,2048]{1,0:T(8,128)(2,1)S(1)}, bf16[192,2048]{1,0:T(8,128)(2,1)}, u32[]{:S(2)}, u32[]{:S(2)}) collective-permute-start(bf16[192,2048]{1,0:T(8,128)(2,1)S(1)} %get-tuple-element.113), channel_id=1, source_target_pairs={{0,8},{4,12},{8,0},{12,4},{16,24},{20,28},{24,16},{28,20},{1,9},{5... | collective-permute-start | bytes 2359304 | tf_op jit(solution)/shard_map/ppermute | solution.py:288
  502.0 30.0 %collective-permute-start.70 = (bf16[192,2048]{1,0:T(8,128)(2,1)S(1)}, bf16[192,2048]{1,0:T(8,128)(2,1)}, u32[]{:S(2)}, u32[]{:S(2)}) collective-permute-start(bf16[192,2048]{1,0:T(8,128)(2,1)S(1)} %get-tuple-element.114), channel_id=1, source_target_pairs={{0,16},{4,20},{8,24},{12,28},{16,0},{20,4},{24,8},{28,12},{1,17},{... | collective-permute-start | bytes 2359304 | tf_op jit(solution)/shard_map/ppermute | solution.py:288
  580.5 55.3 %all-to-all-start.3 = ((bf16[8,64,1,2048]{3,1,2,0:T(8,128)(2,1)}), bf16[8,64,1,2048]{3,1,2,0:T(8,128)(2,1)}, u32[]{:S(2)}, u32[]{:S(2)}) async-start(bf16[8,64,1,2048]{3,1,2,0:T(8,128)(2,1)} %bitcast.150), calls=%async_computation.6 | async-start | bytes 4194304 | tf_op jit(solution)/shard_map/all_to_all | solution.py:380
  584.9 73.3 %reduce-scatter.11.cloned.1.call-start = ((), (), s32[]{:S(2)}) async-start(), calls=%async_computation.15 | async-start | bytes 1310720 | tf_op jit(solution)/shard_map/reduce_scatter | solution.py:388
  (117 other events, 1447.6 us)
Sparse Core Ops, SparseCore 0:
  10.2 48.6 all-gather.4
  61.0 81.6 all-gather.6
  144.2 148.1 all-gather.8
  294.4 44.1 all-gather.10
  340.8 75.4 reduce-scatter.4
  418.6 144.9 reduce-scatter.6
  566.0 60.9 reduce-scatter.8
  629.4 27.1 reduce-scatter.10

commit v5 on v4

--- a/solution.py
+++ b/solution.py
@@ -394,7 +394,8 @@
     near = jnp.broadcast_to(near[:, None], (wrows, seq, LANES)).reshape(wrows, seq * LANES)
     qkv_piece = swap(w_q, w_k, w_v, near)
     pair_piece = swap(after(w_gate, qkv_piece), w_up)
-    down_first = gathered(w_down[:, : width // 2])
+    cut = width * 3 // 8
+    down_first = gathered(w_down[:, :cut])
     tall = seq * wrows
     wide = 4 * group
     piece = jnp.concatenate([qkv_piece[:, : 3 * group], w_o.reshape(tall, group)], -1)
@@ -407,7 +408,7 @@
     gains = first[:, tall:].reshape(fsdp, -1)[:, : 2 * tall].reshape(fsdp, 2, tall).swapaxes(0, 1).reshape(2, width)
     grad_out = gather_tokens(after(own_grad, pair_piece), seq)
     pair_weight = gathered(after(pair_piece, first, grad_out))
-    down_last = gathered(after(w_down[:, width // 2 :], pair_weight))
+    down_last = gathered(after(w_down[:, cut:], pair_weight))
 
     (normed_one,) = norm_call(
         norm_kernel, "norm_one", counts, 0, gains, [after(gather_tokens(own_tokens, seq), pair_piece)], [], [LOW], seq
@@ -429,8 +430,8 @@
     down_part = summed(after(down_whole, down_last))
     cot = after(grad_out, down_whole)
     grad_mixed = jnp.einsum(
-        "td,fd->tf", cot[:, : width // 2], down_first, preferred_element_type=F32
-    ) + jnp.einsum("td,fd->tf", cot[:, width // 2 :], down_last, preferred_element_type=F32)
+        "td,fd->tf", cot[:, :cut], down_first, preferred_element_type=F32
+    ) + jnp.einsum("td,fd->tf", cot[:, cut:], down_last, preferred_element_type=F32)
     down_weight = jnp.concatenate([down_first, down_last], -1)
     grad_gate = (grad_mixed * up * sigmoid * (1.0 + gate * (1.0 - sigmoid))).astype(LOW)
     grad_up = (grad_mixed * gate * sigmoid).astype(LOW)

time: 675 us -> 676 us (level)
    ppermute x77, waiting for transfers between devices: 161 us -> 169 us  [flip(): return lax.ppermute(values, axis, [(i, i ^ mask) for i in range(count)])]
    unnamed x173 -> x179, local copies, waits for them, and re-layouts: 67 us -> 68.8 us
  transfers between devices with their start and end apart: 89 -> 89, of which waited for: 38 -> 37; matrix products, arithmetic and copies ran while one was open for 41% -> 41% of each run, Pallas kernels for 8% -> 8%
where the time goes in v5:
time: 676 us; the launch traced here: 668 us
  waiting for transfers between devices  247 us (37%)
  matrix products  139 us (21%)
  local copies, waits for them, and re-layouts  99.9 us (15%)
  starting transfers between devices  64.2 us (9%)
  Pallas kernels  51.7 us (8%)
  other arithmetic  50.7 us (8%)
  between operations  15.5 us (2%)
    ppermute x77, waiting for transfers between devices, flip(): return lax.ppermute(values, axis, [(i, i ^ mask) for i in range(count)])  169 us
    unnamed x179, local copies, waits for them, and re-layouts  68.8 us
    dot_general x10, matrix products, part(): lax.dot_general(rows, weight, (dims, ((), ())), preferred_element_type=F32)  46.6 us
    ppermute x77, starting transfers between devices, flip(): return lax.ppermute(values, axis, [(i, i ^ mask) for i in range(count)])  46.2 us
    dot_general x4, matrix products, outer(): jnp.einsum('ti,to->io', left, right, preferred_element_type=F32).astype(LOW)  41.9 us
    reduce_scatter x4, waiting for transfers between devices, summed(): return lax.psum_scatter(whole, 'fsdp', scatter_dimension=0, tiled=True)  37.8 us
    all_gather x4, waiting for transfers between devices, gathered(): return lax.all_gather(piece, 'fsdp', axis=0, tiled=True)  29.2 us
    pallas_call x1, Pallas kernels, attend_backward(): pl.pallas_call(functools.partial(attend_back_kernel, block), grid_spec=pl...  23.5 us
  transfers between devices with their start and end apart: 89, of which 37 were waited for; matrix products, arithmetic and copies ran while one was open for 41% of the time, Pallas kernels for 8%

profile of v5, /device:TPU:0, one launch (start us, length us, event | category | flops | bytes accessed | tf_op | source)
XLA Modules:
  0.0 667.8 jit_solution(13635594017136972884)
XLA Ops:
  61.4 22.1 %collective-permute-done.2 = bf16[96,2048]{1,0:T(8,128)(2,1)S(1)} collective-permute-done((bf16[96,2048]{1,0:T(8,128)(2,1)}, bf16[96,2048]{1,0:T(8,128)(2,1)S(1)}, u32[]{:S(2)}, u32[]{:S(2)}) %collective-permute-start.2) | collective-permute-done | bytes 393248 | tf_op jit(solution)/shard_map/ppermute | solution.py:288
  102.6 7.1 %collective-permute-done.37 = bf16[96,2048]{1,0:T(8,128)(2,1)S(1)} collective-permute-done((bf16[96,2048]{1,0:T(8,128)(2,1)S(1)}, bf16[96,2048]{1,0:T(8,128)(2,1)S(1)}, u32[]{:S(2)}, u32[]{:S(2)}) %collective-permute-start.37) | collective-permute-done | bytes 393248 | tf_op jit(solution)/shard_map/ppermute | solution.py:288
  165.2 17.2 %attend_forward.1 = (bf16[1536,256]{1,0:T(8,128)(2,1)S(1)}, bf16[1536,256]{1,0:T(8,128)(2,1)S(1)}, bf16[1536,256]{1,0:T(8,128)(2,1)S(1)}, bf16[1536,256]{1,0:T(8,128)(2,1)S(1)}, f32[2,2,1536]{2,1,0:T(2,128)S(1)}) custom-call(s32[16]{0:T(128)S(1)} %stack.67.order, f32[1536,768]{1,0:T(8,128)} %fusion.40.q.k.v, f32[1536,768]{1,0:T(8,128)} %fusion.40.q.k.v, ...), custom_call_target="tpu_custom_call" | custom-call | tf_op jit(solution)/shard_map/attend_forward/pallas_call | solution.py:116
  190.7 16.6 %collective-permute-done.18 = bf16[192,2048]{1,0:T(8,128)(2,1)S(1)} collective-permute-done((bf16[192,2048]{1,0:T(8,128)(2,1)S(1)}, bf16[192,2048]{1,0:T(8,128)(2,1)S(1)}, u32[]{:S(2)}, u32[]{:S(2)}) %collective-permute-start.18) | collective-permute-done | bytes 786464 | tf_op jit(solution)/shard_map/ppermute | solution.py:288
  210.8 7.5 %collective-permute-done.19.refs_3_ = bf16[96,2048]{1,0:T(8,128)(2,1)S(1)} collective-permute-done((bf16[96,2048]{1,0:T(8,128)(2,1)S(1)}, bf16[96,2048]{1,0:T(8,128)(2,1)S(1)}, u32[]{:S(2)}, u32[]{:S(2)}) %collective-permute-start.19) | collective-permute-done | bytes 393248 | tf_op jit(solution)/shard_map/ppermute | solution.py:288
  227.7 7.4 %collective-permute-done.20 = bf16[96,2048]{1,0:T(8,128)(2,1)} collective-permute-done((bf16[96,2048]{1,0:T(8,128)(2,1)}, bf16[96,2048]{1,0:T(8,128)(2,1)}, u32[]{:S(2)}, u32[]{:S(2)}) %collective-permute-start.20) | collective-permute-done | bytes 393248 | tf_op jit(solution)/shard_map/ppermute | solution.py:288
  266.7 19.0 %all-gather.9.cloned.1.call-done = bf16[2048,2048]{1,0:T(8,128)(2,1)} async-done(((bf16[512,2048]{1,0:T(8,128)(2,1)}), bf16[2048,2048]{1,0:T(8,128)(2,1)}) %all-gather.9.cloned.1.call-update) | async-done | bytes 8388624 | tf_op jit(solution)/shard_map/all_gather | solution.py:385
  285.8 17.8 %fusion.41 = f32[1536,2048]{1,0:T(8,128)S(1)} fusion(bf16[1536,2048]{1,0:T(8,128)(2,1)} %constant_dynamic-update-slice_fusion.16, bf16[2048,2048]{1,0:T(8,128)(2,1)} %all-gather.9.cloned.1.call-done), kind=kOutput, calls=%fused_computation.180 | convolution fusion | flops 12884901888 | bytes 27262976 | tf_op jit(solution)/shard_map/dot_general | solution.py:425
  311.9 11.2 %convolution_convert_fusion.1 = bf16[1024,2048]{1,0:T(8,128)(2,1)} fusion(bf16[1536,1024]{1,0:T(8,128)(2,1)S(1)} %multiply_convert_fusion.2, bf16[1536,2048]{1,0:T(8,128)(2,1)} %constant_dynamic-update-slice_fusion.32), kind=kOutput, calls=%fused_computation.15 | convolution fusion | flops 6444548096 | bytes 13631488 | tf_op jit(solution)/shard_map/ti,to->io/dot_general | solution.py:391
  323.1 7.5 %fusion.6 = f32[1536,1024]{1,0:T(8,128)} fusion(bf16[1024,768]{1,0:T(8,128)(2,1)} %all-gather.5.cloned.1.call-done, bf16[1536,2048]{1,0:T(8,128)(2,1)} %constant_dynamic-update-slice_fusion.32), kind=kOutput, calls=%fused_computation.29 | convolution fusion | flops 2415919104 | bytes 10223616 | tf_op jit(solution)/shard_map/td,fd->tf/dot_general | solution.py:432
  330.6 9.5 %all-gather.11.cloned.1.call-done = bf16[1024,1280]{1,0:T(8,128)(2,1)} async-done(((bf16[256,1280]{1,0:T(8,128)(2,1)}), bf16[1024,1280]{1,0:T(8,128)(2,1)}) %all-gather.11.cloned.1.call-update) | async-done | bytes 2621456 | tf_op jit(solution)/shard_map/all_gather | solution.py:385
  340.3 12.4 %multiply_convert_fusion = (bf16[1536,1024]{1,0:T(8,128)(2,1)S(1)}, bf16[1536,1024]{1,0:T(8,128)(2,1)S(1)}) fusion(f32[1536,2048]{1,0:T(8,128)} %copy-done.19, f32[1536,1024]{1,0:T(8,128)} %fusion.6, bf16[1024,1280]{1,0:T(8,128)(2,1)} %all-gather.11.cloned.1.call-done, bf16[1536,2048]{1,0:T(8,128)(2,1)} %constant_dynamic-update-slice_fusion.32), kind=kOutput, calls=%fused_computation.9 | convolution fusion | flops 4048551936 | bytes 31719424 | tf_op jit(solution)/shard_map/td,fd->tf/dot_general | solution.py:434
  352.7 11.4 %convolution_convert_fusion.2 = bf16[768,2048]{1,0:T(8,128)(2,1)} fusion(bf16[2048,2048]{1,0:T(8,128)(2,1)} %all-gather.9.cloned.1.call-done, bf16[1536,1024]{1,0:T(8,128)(2,1)S(1)} %get-tuple-element.104, bf16[1536,1024]{1,0:T(8,128)(2,1)S(1)} %get-tuple-element.103), kind=kOutput, calls=%fused_computation.16 | convolution fusion | flops 6450315264 | bytes 17825792 | tf_op jit(solution)/shard_map/dot_general | solution.py:335
  370.1 13.3 %fusion.33 = (bf16[768,2048]{1,0:T(8,128)(2,1)}, f32[768,2048]{1,0:T(8,128)}) fusion(bf16[768,2048]{1,0:T(8,128)(2,1)} %collective-permute-done.48, bf16[2048,2048]{1,0:T(8,128)(2,1)} %all-gather.9.cloned.1.call-done, bf16[1536,1024]{1,0:T(8,128)(2,1)} %copy-done.32, bf16[1536,1024]{1,0:T(8,128)(2,1)S(1)} %get-tuple-element.103), kind=kOutput, calls=%fused_computation.172 | convolution fusion | flops 6453460992 | bytes 27262976 | tf_op jit(solution)/shard_map/dot_general | solution.py:335
  383.4 18.0 %convolution_convert_fusion = bf16[2048,2048]{1,0:T(8,128)(2,1)} fusion(bf16[1536,2048]{1,0:T(8,128)(2,1)} %constant_dynamic-update-slice_fusion.16, bf16[1536,2048]{1,0:T(8,128)(2,1)S(1)} %pad_maximum_fusion), kind=kOutput, calls=%fused_computation.5 | convolution fusion | flops 12889096192 | bytes 20971520 | tf_op jit(solution)/shard_map/ti,to->io/dot_general | solution.py:391
  401.5 16.4 %reduce-scatter.5.cloned.1.call-done = bf16[256,2048]{1,0:T(8,128)(2,1)} async-done(((bf16[1024,2048]{1,0:T(8,128)(2,1)}), bf16[256,2048]{1,0:T(8,128)(2,1)}) %reduce-scatter.5.cloned.1.call-update) | async-done | bytes 1048592 | tf_op jit(solution)/shard_map/reduce_scatter | solution.py:388
  422.7 16.4 %collective-permute-done.49 = bf16[192,2048]{1,0:T(8,128)(2,1)S(1)} collective-permute-done((bf16[192,2048]{1,0:T(8,128)(2,1)S(1)}, bf16[192,2048]{1,0:T(8,128)(2,1)S(1)}, u32[]{:S(2)}, u32[]{:S(2)}) %collective-permute-start.49) | collective-permute-done | bytes 786464 | tf_op jit(solution)/shard_map/ppermute | solution.py:288
  445.9 7.0 %collective-permute-done.50.refs_1_ = bf16[96,2048]{1,0:T(8,128)(2,1)S(1)} collective-permute-done((bf16[96,2048]{1,0:T(8,128)(2,1)S(1)}, bf16[96,2048]{1,0:T(8,128)(2,1)S(1)}, u32[]{:S(2)}, u32[]{:S(2)}) %collective-permute-start.50) | collective-permute-done | bytes 393248 | tf_op jit(solution)/shard_map/ppermute | solution.py:288
  474.4 7.7 %collective-permute-done.56 = bf16[96,2048]{1,0:T(8,128)(2,1)S(1)} collective-permute-done((bf16[96,2048]{1,0:T(8,128)(2,1)S(1)}, bf16[96,2048]{1,0:T(8,128)(2,1)S(1)}, u32[]{:S(2)}, u32[]{:S(2)}) %collective-permute-start.56) | collective-permute-done | bytes 393248 | tf_op jit(solution)/shard_map/ppermute | solution.py:288
  512.0 23.5 %attend_backward.1 = (bf16[1536,256]{1,0:T(8,128)(2,1)S(1)}, bf16[1536,256]{1,0:T(8,128)(2,1)S(1)}, bf16[1536,256]{1,0:T(8,128)(2,1)S(1)}) custom-call(s32[16]{0:T(128)S(1)} %copy-done.16, bf16[1536,256]{1,0:T(8,128)(2,1)S(1)} %copy-done.11, bf16[1536,256]{1,0:T(8,128)(2,1)S(1)} %copy-done.13, bf16[1536,256]{1,0:T(8,128)(2,1)} %copy-done.14, ...), custom_call_target="tpu_custom_call" | custom-call | tf_op jit(solution)/shard_map/attend_backward/pallas_call | solution.py:194
  537.2 7.0 %convolution_convert_fusion.5 = bf16[2048,768]{1,0:T(8,128)(2,1)} fusion(bf16[1536,2048]{1,0:T(8,128)(2,1)S(1)} %bitcast.127, bf16[1536,768]{1,0:T(8,128)(2,1)S(1)} %constant_dynamic-update-slice_fusion.66), kind=kOutput, calls=%fused_computation.19 | convolution fusion | flops 4833411072 | bytes 11796480 | tf_op jit(solution)/shard_map/ti,to->io/dot_general | solution.py:391
  591.6 14.7 %collective-permute-done.73 = bf16[192,2048]{1,0:T(8,128)(2,1)} collective-permute-done((bf16[192,2048]{1,0:T(8,128)(2,1)}, bf16[192,2048]{1,0:T(8,128)(2,1)}, u32[]{:S(2)}, u32[]{:S(2)}) %collective-permute-start.73) | collective-permute-done | bytes 786464 | tf_op jit(solution)/shard_map/ppermute | solution.py:288
  612.5 16.2 %reduce-scatter.9.cloned.1.call-done = bf16[512,768]{1,0:T(8,128)(2,1)} async-done(((bf16[2048,768]{1,0:T(8,128)(2,1)}), bf16[512,768]{1,0:T(8,128)(2,1)}) %reduce-scatter.9.cloned.1.call-update) | async-done | bytes 786448 | tf_op jit(solution)/shard_map/reduce_scatter | solution.py:388
  649.2 8.1 %all-to-all-done.2 = bf16[8,64,1,768]{3,1,2,0:T(8,128)(2,1)S(1)} async-done(((bf16[8,64,1,768]{3,1,2,0:T(8,128)(2,1)}), bf16[8,64,1,768]{3,1,2,0:T(8,128)(2,1)S(1)}, u32[]{:S(2)}, u32[]{:S(2)}) %all-to-all-start.2) | async-done | bytes 786464 | tf_op jit(solution)/shard_map/all_to_all | solution.py:380
  (453 shorter events, 337.0 us)
Async XLA Ops:
  7.2 42.8 %all-gather.5.cloned.1.call-start = ((), (), s32[]{:S(2)}) async-start(), calls=%async_computation.8 | async-start | bytes 1966080 | tf_op jit(solution)/shard_map/all_gather | solution.py:385
  23.5 32.7 %collective-permute-start = (bf16[96,2048]{1,0:T(8,128)(2,1)}, bf16[96,2048]{1,0:T(8,128)(2,1)}, u32[]{:S(2)}, u32[]{:S(2)}) collective-permute-start(bf16[96,2048]{1,0:T(8,128)(2,1)} %get-tuple-element.132), channel_id=1, source_target_pairs={{0,16},{4,20},{8,24},{12,28},{16,0},{20,4},{24,8},{28,12},{1,17},{... | collective-permute-start | bytes 1179656 | tf_op jit(solution)/shard_map/ppermute | solution.py:288
  25.6 34.0 %collective-permute-start.1 = (bf16[96,2048]{1,0:T(8,128)(2,1)}, bf16[96,2048]{1,0:T(8,128)(2,1)}, u32[]{:S(2)}, u32[]{:S(2)}) collective-permute-start(bf16[96,2048]{1,0:T(8,128)(2,1)} %get-tuple-element.132), channel_id=1, source_target_pairs={{0,8},{4,12},{8,0},{12,4},{16,24},{20,28},{24,16},{28,20},{1,9},{5... | collective-permute-start | bytes 1179656 | tf_op jit(solution)/shard_map/ppermute | solution.py:288
  27.0 60.5 %collective-permute-start.3 = (bf16[96,2048]{1,0:T(8,128)(2,1)}, bf16[96,2048]{1,0:T(8,128)(2,1)}, u32[]{:S(2)}, u32[]{:S(2)}) collective-permute-start(bf16[96,2048]{1,0:T(8,128)(2,1)} %get-tuple-element.131), channel_id=1, source_target_pairs={{0,8},{4,12},{8,0},{12,4},{16,24},{20,28},{24,16},{28,20},{1,9},{5... | collective-permute-start | bytes 1179656 | tf_op jit(solution)/shard_map/ppermute | solution.py:288
  27.6 62.3 %collective-permute-start.4 = (bf16[96,2048]{1,0:T(8,128)(2,1)}, bf16[96,2048]{1,0:T(8,128)(2,1)}, u32[]{:S(2)}, u32[]{:S(2)}) collective-permute-start(bf16[96,2048]{1,0:T(8,128)(2,1)} %get-tuple-element.131), channel_id=1, source_target_pairs={{0,16},{4,20},{8,24},{12,28},{16,0},{20,4},{24,8},{28,12},{1,17},{... | collective-permute-start | bytes 1179656 | tf_op jit(solution)/shard_map/ppermute | solution.py:288
  27.6 109.7 %collective-permute-start.6 = (bf16[96,2048]{1,0:T(8,128)(2,1)}, bf16[96,2048]{1,0:T(8,128)(2,1)}, u32[]{:S(2)}, u32[]{:S(2)}) collective-permute-start(bf16[96,2048]{1,0:T(8,128)(2,1)} %get-tuple-element.132), channel_id=1, source_target_pairs={{0,4},{4,0},{8,12},{12,8},{16,20},{20,16},{24,28},{28,24},{1,5},{5... | collective-permute-start | bytes 1179656 | tf_op jit(solution)/shard_map/ppermute | solution.py:288
  42.6 42.5 %all-to-all-start.1 = ((bf16[64,8,2048]{2,0,1:T(8,128)(2,1)}), bf16[64,8,2048]{2,0,1:T(8,128)(2,1)}, u32[]{:S(2)}, u32[]{:S(2)}) async-start(bf16[64,8,2048]{2,0,1:T(8,128)(2,1)} %copy.74), calls=%async_computation.1 | async-start | bytes 4194304 | tf_op jit(solution)/shard_map/all_to_all | solution.py:377
  46.9 88.7 %all-gather.7.cloned.1.call-start = ((), (), s32[]{:S(2)}) async-start(), calls=%async_computation.9 | async-start | bytes 5406720 | tf_op jit(solution)/shard_map/all_gather | solution.py:385
  50.0 235.7 %all-gather.9.cloned.1.call-start = ((), (), s32[]{:S(2)}) async-start(), calls=%async_computation.10 | async-start | bytes 10485760 | tf_op jit(solution)/shard_map/all_gather | solution.py:385
  56.2 27.3 %collective-permute-start.2 = (bf16[96,2048]{1,0:T(8,128)(2,1)}, bf16[96,2048]{1,0:T(8,128)(2,1)S(1)}, u32[]{:S(2)}, u32[]{:S(2)}) collective-permute-start(bf16[96,2048]{1,0:T(8,128)(2,1)} %collective-permute-done), channel_id=1, source_target_pairs={{0,8},{4,12},{8,0},{12,4},{16,24},{20,28},{24,16},{28,20},{1,9},{5... | collective-permute-start | bytes 1179656 | tf_op jit(solution)/shard_map/ppermute | solution.py:288
  59.6 82.4 %collective-permute-start.10 = (bf16[96,2048]{1,0:T(8,128)(2,1)}, bf16[96,2048]{1,0:T(8,128)(2,1)S(1)}, u32[]{:S(2)}, u32[]{:S(2)}) collective-permute-start(bf16[96,2048]{1,0:T(8,128)(2,1)} %get-tuple-element.131), channel_id=1, source_target_pairs={{0,4},{4,0},{8,12},{12,8},{16,20},{20,16},{24,28},{28,24},{1,5},{5... | collective-permute-start | bytes 1179656 | tf_op jit(solution)/shard_map/ppermute | solution.py:288
  101.3 34.6 %collective-permute-start.5 = (bf16[96,2048]{1,0:T(8,128)(2,1)}, bf16[96,2048]{1,0:T(8,128)(2,1)S(1)}, u32[]{:S(2)}, u32[]{:S(2)}) collective-permute-start(bf16[96,2048]{1,0:T(8,128)(2,1)} %collective-permute-done.3), channel_id=1, source_target_pairs={{0,16},{4,20},{8,24},{12,28},{16,0},{20,4},{24,8},{28,12},{1,17},{... | collective-permute-start | bytes 1179656 | tf_op jit(solution)/shard_map/ppermute | solution.py:288
  135.7 204.5 %all-gather.11.cloned.1.call-start = ((), (), s32[]{:S(2)}) async-start(), calls=%async_computation.11 | async-start | bytes 3276800 | tf_op jit(solution)/shard_map/all_gather | solution.py:385
  226.4 27.4 %collective-permute-start.24 = (bf16[96,2048]{1,0:T(8,128)(2,1)}, bf16[96,2048]{1,0:T(8,128)(2,1)S(1)}, u32[]{:S(2)}, u32[]{:S(2)}) collective-permute-start(bf16[96,2048]{1,0:T(8,128)(2,1)} %get-tuple-element.125), channel_id=1, source_target_pairs={{0,16},{4,20},{8,24},{12,28},{16,0},{20,4},{24,8},{28,12},{1,17},{... | collective-permute-start | bytes 1179656 | tf_op jit(solution)/shard_map/ppermute | solution.py:288
  227.7 31.8 %collective-permute-start.26 = (bf16[96,2048]{1,0:T(8,128)(2,1)}, bf16[96,2048]{1,0:T(8,128)(2,1)S(1)}, u32[]{:S(2)}, u32[]{:S(2)}) collective-permute-start(bf16[96,2048]{1,0:T(8,128)(2,1)} %get-tuple-element.127), channel_id=1, source_target_pairs={{0,4},{4,0},{8,12},{12,8},{16,20},{20,16},{24,28},{28,24},{1,5},{5... | collective-permute-start | bytes 1179656 | tf_op jit(solution)/shard_map/ppermute | solution.py:288
  285.7 132.2 %reduce-scatter.5.cloned.1.call-start = ((), (), s32[]{:S(2)}) async-start(), calls=%async_computation.12 | async-start | bytes 5242880 | tf_op jit(solution)/shard_map/reduce_scatter | solution.py:388
  340.2 225.0 %reduce-scatter.7.cloned.1.call-start = ((), (), s32[]{:S(2)}) async-start(), calls=%async_computation.13 | async-start | bytes 10485760 | tf_op jit(solution)/shard_map/reduce_scatter | solution.py:388
  417.9 210.7 %reduce-scatter.9.cloned.1.call-start = ((), (), s32[]{:S(2)}) async-start(), calls=%async_computation.14 | async-start | bytes 3932160 | tf_op jit(solution)/shard_map/reduce_scatter | solution.py:388
  458.9 27.0 %collective-permute-start.58 = (bf16[96,2048]{1,0:T(8,128)(2,1)S(1)}, bf16[96,2048]{1,0:T(8,128)(2,1)S(1)}, u32[]{:S(2)}, u32[]{:S(2)}) collective-permute-start(bf16[96,2048]{1,0:T(8,128)(2,1)S(1)} %get-tuple-element.122), channel_id=1, source_target_pairs={{0,16},{4,20},{8,24},{12,28},{16,0},{20,4},{24,8},{28,12},{1,17},{... | collective-permute-start | bytes 1179656 | tf_op jit(solution)/shard_map/ppermute | solution.py:288
  460.4 33.0 %collective-permute-start.60 = (bf16[96,2048]{1,0:T(8,128)(2,1)S(1)}, bf16[96,2048]{1,0:T(8,128)(2,1)S(1)}, u32[]{:S(2)}, u32[]{:S(2)}) collective-permute-start(bf16[96,2048]{1,0:T(8,128)(2,1)S(1)} %get-tuple-element.124), channel_id=1, source_target_pairs={{0,4},{4,0},{8,12},{12,8},{16,20},{20,16},{24,28},{28,24},{1,5},{5... | collective-permute-start | bytes 1179656 | tf_op jit(solution)/shard_map/ppermute | solution.py:288
  505.1 30.7 %collective-permute-start.68 = (bf16[192,2048]{1,0:T(8,128)(2,1)S(1)}, bf16[192,2048]{1,0:T(8,128)(2,1)}, u32[]{:S(2)}, u32[]{:S(2)}) collective-permute-start(bf16[192,2048]{1,0:T(8,128)(2,1)S(1)} %get-tuple-element.113), channel_id=1, source_target_pairs={{0,8},{4,12},{8,0},{12,4},{16,24},{20,28},{24,16},{28,20},{1,9},{5... | collective-permute-start | bytes 2359304 | tf_op jit(solution)/shard_map/ppermute | solution.py:288
  505.7 30.0 %collective-permute-start.70 = (bf16[192,2048]{1,0:T(8,128)(2,1)S(1)}, bf16[192,2048]{1,0:T(8,128)(2,1)}, u32[]{:S(2)}, u32[]{:S(2)}) collective-permute-start(bf16[192,2048]{1,0:T(8,128)(2,1)S(1)} %get-tuple-element.114), channel_id=1, source_target_pairs={{0,16},{4,20},{8,24},{12,28},{16,0},{20,4},{24,8},{28,12},{1,17},{... | collective-permute-start | bytes 2359304 | tf_op jit(solution)/shard_map/ppermute | solution.py:288
  582.2 55.3 %all-to-all-start.3 = ((bf16[8,64,1,2048]{3,1,2,0:T(8,128)(2,1)}), bf16[8,64,1,2048]{3,1,2,0:T(8,128)(2,1)}, u32[]{:S(2)}, u32[]{:S(2)}) async-start(bf16[8,64,1,2048]{3,1,2,0:T(8,128)(2,1)} %bitcast.150), calls=%async_computation.6 | async-start | bytes 4194304 | tf_op jit(solution)/shard_map/all_to_all | solution.py:380
  586.5 72.4 %reduce-scatter.11.cloned.1.call-start = ((), (), s32[]{:S(2)}) async-start(), calls=%async_computation.15 | async-start | bytes 1310720 | tf_op jit(solution)/shard_map/reduce_scatter | solution.py:388
  (120 other events, 1500.0 us)
Sparse Core Ops, SparseCore 0:
  10.2 39.7 all-gather.4
  52.2 82.7 all-gather.6
  136.5 149.1 all-gather.8
  287.1 53.0 all-gather.10
  342.3 75.5 reduce-scatter.4
  420.2 144.9 reduce-scatter.6
  567.6 60.9 reduce-scatter.8
  631.0 27.1 reduce-scatter.10
